TPU v7x, 32 devices: a whole 2x2x4 slice. The times are simulated.
32 devices in a mesh: seq: 16 (over z, y, core), head: 2 (over x).
Axes of the slice: x: 2, y: 2, z: 4, core: 2. Of those that a mesh axis runs over, the one named last changes fastest.
Arguments:
- query: bfloat16 [4096, 3584], P('seq', 'head'), may hold values from -6 to 6
- key: bfloat16 [4096, 512], P('seq', 'head'), may hold values from -6 to 6
- value: bfloat16 [4096, 512], P('seq', 'head'), may hold values from -6 to 6
- output: bfloat16 [4096, 3584], P('seq', 'head'), may hold values from -6 to 6
- output_gradient: bfloat16 [4096, 3584], P('seq', 'head'), may hold values from -6 to 6
- lse: float32 [28, 4096], P('head', 'seq'), may hold values from 3 to 6
- doc_lengths: int32 [4], replicated, may hold values from 1 to 2048, as said below
- w_query: bfloat16 [3584, 3584], P('seq', 'head'), may hold values from -0.09375 to 0.09375
- key_weight: bfloat16 [3584, 512], P('seq', 'head'), may hold values from -0.09375 to 0.09375
- value_weight: bfloat16 [3584, 512], P('seq', 'head'), may hold values from -0.09375 to 0.09375
Outputs:
- grad_input: bfloat16 [4096, 3584], P('seq', 'head')
Inputs may be any that keep to these rules, and one draw needn't show every extreme that they name: `doc_lengths`: the documents lie end to end and fill the 4096 tokens of the pack; the first has 1024 tokens, and one of exactly 2048 tokens begins at token 1024.
All inputs are finite; a program needn't handle non-finite values.
Results may differ from a plain program's by a relative error of at most 0.0056.
Values may be sent and summed in bfloat16 or wider, within the bound.
No kernel may reach another device: no remote copies, remote signals or barrier semaphores. Data moves between devices by JAX's collectives and lax.ppermute only.
A program may use at most 128 MiB of HBM per device.

v0:
```python
import math

import jax
import jax.numpy as jnp
from jax import lax
from jax.sharding import PartitionSpec as P

HEAD_SIZE = 128
WINDOW = 512


def shifted(array, axis, by):
    peers = lax.axis_size(axis)
    pairs = [(i, i + by) for i in range(peers) if 0 <= i + by < peers]
    return lax.ppermute(array, axis, pairs)


def lower_bounds(positions, doc_lengths, window):
    starts = jnp.cumsum(doc_lengths, dtype=jnp.int32) - doc_lengths
    inside = starts[None, :] <= positions[:, None]
    doc_begin = jnp.max(jnp.where(inside, starts[None, :], 0), axis=1)
    return jnp.maximum(doc_begin, positions - window + 1)


def attend(
    query_rows,
    key_row_block,
    value_row_block,
    visible,
    logsumexp_rows,
    output_grad_rows,
    row_delta,
    score_scale,
):
    scores = (
        jnp.einsum("tgjd,kgd->gjtk", query_rows, key_row_block, preferred_element_type=jnp.float32)
        * score_scale
    )
    prob_full = jnp.where(visible[None, None], jnp.exp(scores - logsumexp_rows[..., None]), 0.0)
    prob_low = prob_full.astype(jnp.bfloat16)
    grad_val = jnp.einsum(
        "gjtk,tgjd->kgd", prob_low, output_grad_rows, preferred_element_type=jnp.float32
    )
    grad_prob = jnp.einsum(
        "tgjd,kgd->gjtk", output_grad_rows, value_row_block, preferred_element_type=jnp.float32
    )
    dscore = (prob_full * (grad_prob - row_delta[..., None]) * score_scale).astype(jnp.bfloat16)
    grad_qry = jnp.einsum(
        "gjtk,kgd->tgjd", dscore, key_row_block, preferred_element_type=jnp.float32
    )
    grad_key = jnp.einsum("gjtk,tgjd->kgd", dscore, query_rows, preferred_element_type=jnp.float32)
    return (grad_qry, grad_key, grad_val)


def projector(grad_rows, w_piece):
    return jnp.einsum("tc,rc->tr", grad_rows, w_piece, preferred_element_type=jnp.float32)


def shards(
    query, key, value, output, output_gradient, lse, doc_lengths, w_query, key_weight, value_weight
):
    tok_rows = query.shape[0]
    key_value_width = key.shape[1]
    kv_heads = key_value_width // HEAD_SIZE
    q_heads = query.shape[1] // HEAD_SIZE
    per_group = q_heads // kv_heads
    score_scale = 1.0 / math.sqrt(HEAD_SIZE)
    seq_index = lax.axis_index("seq")
    positions = seq_index * tok_rows + jnp.arange(tok_rows, dtype=jnp.int32)
    lower = lower_bounds(positions, doc_lengths, WINDOW)
    query_rows = query.reshape(tok_rows, kv_heads, per_group, HEAD_SIZE)
    output_rows = output.reshape(tok_rows, kv_heads, per_group, HEAD_SIZE)
    output_grad_rows = output_gradient.reshape(tok_rows, kv_heads, per_group, HEAD_SIZE)
    row_delta = jnp.einsum(
        "tgjd,tgjd->gjt", output_grad_rows, output_rows, preferred_element_type=jnp.float32
    )
    logsumexp_rows = lse.reshape(kv_heads, per_group, tok_rows)
    near_pair = shifted((key, value), "seq", 1)
    far_pair = shifted((key, value), "seq", 2)
    key_all = jnp.concatenate([far_pair[0], near_pair[0], key], 0).reshape(
        3 * tok_rows, kv_heads, HEAD_SIZE
    )
    value_all = jnp.concatenate([far_pair[1], near_pair[1], value], 0).reshape(
        3 * tok_rows, kv_heads, HEAD_SIZE
    )
    key_pos = positions[0] - 2 * tok_rows + jnp.arange(3 * tok_rows, dtype=jnp.int32)
    visible = (key_pos[None, :] >= lower[:, None]) & (key_pos[None, :] <= positions[:, None])
    grad_qry, grad_key, grad_val = attend(
        query_rows,
        key_all,
        value_all,
        visible,
        logsumexp_rows,
        output_grad_rows,
        row_delta,
        score_scale,
    )
    key_parts = grad_key.reshape(3, tok_rows, key_value_width)
    value_parts = grad_val.reshape(3, tok_rows, key_value_width)
    key_far, key_near, key_own = (key_parts[0], key_parts[1], key_parts[2])
    value_far, value_near, value_own = (value_parts[0], value_parts[1], value_parts[2])
    back_near = shifted((key_near, value_near), "seq", -1)
    back_far = shifted((key_far, value_far), "seq", -2)
    key_total = key_own + back_near[0] + back_far[0]
    value_total = value_own + back_near[1] + back_far[1]
    q_grad_low = grad_qry.reshape(tok_rows, q_heads * HEAD_SIZE).astype(jnp.bfloat16)
    k_grad_low = key_total.astype(jnp.bfloat16)
    v_grad_low = value_total.astype(jnp.bfloat16)
    grad_joined = jnp.concatenate([q_grad_low, k_grad_low, v_grad_low], 1)
    w_joined = jnp.concatenate([w_query, key_weight, value_weight], 1)
    partial_sum = projector(grad_joined, lax.all_gather(w_joined, "seq", axis=0, tiled=True))
    summed = lax.psum_scatter(partial_sum, "head", scatter_dimension=1, tiled=True)
    return summed.astype(jnp.bfloat16)


def solution(mesh):
    in_specs = (
        P("seq", "head"),
        P("seq", "head"),
        P("seq", "head"),
        P("seq", "head"),
        P("seq", "head"),
        P("head", "seq"),
        P(),
        P("seq", "head"),
        P("seq", "head"),
        P("seq", "head"),
    )
    out_specs = P("seq", "head")
    return jax.shard_map(shards, mesh=mesh, in_specs=in_specs, out_specs=out_specs, check_vma=False)
```

profile of v0, /device:TPU:0, one launch (start us, length us, event | category | flops | bytes accessed | tf_op | source)
XLA Modules:
  0.0 216.8 jit_solution(18084362860949936077)
XLA Ops:
  6.5 2.4 %pad_maximum_fusion = bf16[224,2304]{1,0:T(8,128)(2,1)} fusion(bf16[224,256]{1,0:T(8,128)(2,1)} %param.19, bf16[224,256]{1,0:T(8,128)(2,1)} %param.18, bf16[224,1792]{1,0:T(8,128)(2,1)} %param.17), kind=kLoop, calls=%fused_computation.21 | loop fusion | flops 3096576 | bytes 2064384 | tf_op jit(solution)/shard_map/concatenate | solution.py:110
  9.0 1.7 copy.35
  10.7 5.5 %collective-permute-start = (bf16[256,256]{0,1:T(8,128)(2,1)}, bf16[256,256]{0,1:T(8,128)(2,1)}, u32[]{:S(2)}, u32[]{:S(2)}) collective-permute-start(bf16[256,256]{0,1:T(8,128)(2,1)} %copy.35), channel_id=1, source_target_pairs={{0,4},{2,6},{4,8},{6,10},{8,12},{10,14},{12,16},{14,18},{16,20},{1... | collective-permute-start | bytes 393224 | tf_op jit(solution)/shard_map/ppermute | solution.py:15
  16.2 2.1 collective-permute-start.1
  18.3 1.0 copy.41
  19.3 3.3 %collective-permute-start.2 = (bf16[256,256]{0,1:T(8,128)(2,1)S(1)}, bf16[256,256]{0,1:T(8,128)(2,1)}, u32[]{:S(2)}, u32[]{:S(2)}) collective-permute-start(bf16[256,256]{0,1:T(8,128)(2,1)S(1)} %copy.41), channel_id=1, source_target_pairs={{0,4},{2,6},{4,8},{6,10},{8,12},{10,14},{12,16},{14,18},{16,20},{1... | collective-permute-start | bytes 393224 | tf_op jit(solution)/shard_map/ppermute | solution.py:15
  22.6 3.9 %collective-permute-start.3 = (bf16[256,256]{0,1:T(8,128)(2,1)S(1)}, bf16[256,256]{0,1:T(8,128)(2,1)}, u32[]{:S(2)}, u32[]{:S(2)}) collective-permute-start(bf16[256,256]{0,1:T(8,128)(2,1)S(1)} %copy.41), channel_id=1, source_target_pairs={{0,2},{2,4},{4,6},{6,8},{8,10},{10,12},{12,14},{14,16},{16,18},{18... | collective-permute-start | bytes 393224 | tf_op jit(solution)/shard_map/ppermute | solution.py:15
  26.5 0.6 slice.27
  27.1 1.5 copy.44
  28.5 0.5 copy.73
  30.0 0.9 compare_and_fusion
  30.9 0.3 fusion.9
  31.2 1.5 copy.38
  32.7 1.1 pad_maximum_fusion.1
  33.8 1.0 pad_maximum_fusion.2
  34.8 1.6 fusion.28
  36.4 4.0 %fusion.2 = bf16[2,7,256,768]{2,3,1,0:T(8,128)(2,1)S(1)} fusion(f32[2,768,256,7]{2,1,3,0:T(8,128)S(1)} %fusion.28, f32[2,7,256]{2,1,0:T(8,128)S(1)} %fusion.9, f32[2,7,256]{2,1,0:T(8,128)S(1)} %sub.31, pred[256,768]{0,1:T(8,128)(4,1)S(1)} %copy-done.1, bf16[768,2,128,1]{0,2,3,1:T(8,128)(2,1)S(1)} %bitcast.96, bf16[256,2,7,128]{0,3,2,1:T(8,128)(2,1)S(1)} %bitcast.90), kind=kOutput, calls=%fused_computation.3 | convolution fusion | flops 723910656 | bytes 18051072 | tf_op jit(solution)/shard_map/tgjd,kgd->gjtk/dot_general | solution.py:44
  40.5 1.9 convolution_bitcast_fusion
  42.3 0.9 fusion.26
  43.2 1.3 collective-permute-start.4
  44.5 1.3 collective-permute-start.5
  45.8 3.9 %fusion.10 = f32[768,2,128]{0,2,1:T(8,128)} fusion(bf16[256,2,7,128]{0,3,2,1:T(8,128)(2,1)S(1)} %bitcast.91, f32[2,768,256,7]{2,1,3,0:T(8,128)S(1)} %fusion.28, f32[2,7,256]{2,1,0:T(8,128)S(1)} %copy-done.4, pred[256,768]{0,1:T(8,128)(4,1)} %compare_and_fusion), kind=kOutput, calls=%fused_computation.13 | convolution fusion | flops 715653120 | bytes 12924928 | tf_op jit(solution)/shard_map/gjtk,tgjd->kgd/dot_general | solution.py:41
  49.7 1.2 fusion.27
  50.9 1.3 collective-permute-start.6
  52.2 1.5 collective-permute-start.7
  53.7 0.9 convolution_convert_fusion
  54.6 2.7 %collective-permute-done.5 = f32[256,256]{0,1:T(8,128)S(1)} collective-permute-done((f32[256,256]{0,1:T(8,128)}, f32[256,256]{0,1:T(8,128)S(1)}, u32[]{:S(2)}, u32[]{:S(2)}) %collective-permute-start.5) | collective-permute-done | bytes 262176 | tf_op jit(solution)/shard_map/ppermute | solution.py:15
  57.3 8.7 %collective-permute-done.7 = f32[256,256]{0,1:T(8,128)S(1)} collective-permute-done((f32[256,256]{0,1:T(8,128)S(1)}, f32[256,256]{0,1:T(8,128)S(1)}, u32[]{:S(2)}, u32[]{:S(2)}) %collective-permute-start.7) | collective-permute-done | bytes 262176 | tf_op jit(solution)/shard_map/ppermute | solution.py:15
  66.0 79.6 %all-gather.2.cloned.1.call-done = bf16[3584,2304]{1,0:T(8,128)(2,1)} async-done(((bf16[224,2304]{1,0:T(8,128)(2,1)}), bf16[3584,2304]{1,0:T(8,128)(2,1)}) %all-gather.2.cloned.1.call-update) | async-done | bytes 16515088 | tf_op jit(solution)/shard_map/all_gather | solution.py:111
  145.7 12.0 %fusion.13 = f32[256,3584]{1,0:T(8,128)} fusion(bf16[3584,2304]{1,0:T(8,128)(2,1)} %all-gather.2.cloned.1.call-done, bf16[256,256]{0,1:T(8,128)(2,1)S(1)} %fusion.20, bf16[256,256]{0,1:T(8,128)(2,1)S(1)} %fusion.22, bf16[256,1792]{0,1:T(8,128)(2,1)S(1)} %bitcast.95), kind=kOutput, calls=%fused_computation.15 | convolution fusion | flops 4231397376 | bytes 21364736 | tf_op jit(solution)/shard_map/tc,rc->tr/dot_general | solution.py:56
  157.7 49.7 %reduce-scatter.2.cloned.1.call-done = f32[256,1792]{1,0:T(8,128)} async-done(((f32[256,3584]{1,0:T(8,128)}), f32[256,1792]{1,0:T(8,128)}) %reduce-scatter.2.cloned.1.call-update) | async-done | bytes 1835024 | tf_op jit(solution)/shard_map/reduce_scatter | solution.py:112
  207.5 2.5 %convert_element_type.31 = bf16[256,1792]{1,0:T(8,128)(2,1)} convert(f32[256,1792]{1,0:T(8,128)} %reduce-scatter.2.cloned.1.call-done) | non-fusion elementwise | flops 458752 | bytes 2752512 | tf_op jit(solution)/shard_map/convert_element_type | solution.py:113
  (31 shorter events, 0.5 us)
Async XLA Ops:
  6.5 22.0 %copy-start = (bf16[256,1792]{1,0:T(8,128)(2,1)S(1)}, bf16[256,1792]{1,0:T(8,128)(2,1)}, u32[]{:S(2)}) copy-start(bf16[256,1792]{1,0:T(8,128)(2,1)} %param.13) | copy-start | bytes 2752516
  6.5 22.5 %copy-start.5 = (s32[4]{0:T(128)S(1)}, s32[4]{0:T(128)}, u32[]{:S(2)}) copy-start(s32[4]{0:T(128)} %param.16) | copy-start | bytes 52
  6.5 26.1 %copy-start.2 = (f32[14,256]{1,0:T(8,128)S(1)}, f32[14,256]{1,0:T(8,128)}, u32[]{:S(2)}) copy-start(f32[14,256]{1,0:T(8,128)} %param.15) | copy-start | bytes 43012
  6.5 139.1 %all-gather.2.cloned.1.call-start = ((), (), s32[]{:S(2)}) async-start(), calls=%async_computation.1 | async-start | bytes 17547264 | tf_op jit(solution)/shard_map/all_gather | solution.py:111
  8.9 198.5 %reduce-scatter.2.cloned.1.call-start = ((), (), s32[]{:S(2)}) async-start(), calls=%async_computation.2 | async-start | bytes 5505024 | tf_op jit(solution)/shard_map/reduce_scatter | solution.py:112
  10.7 22.0 %collective-permute-start = (bf16[256,256]{0,1:T(8,128)(2,1)}, bf16[256,256]{0,1:T(8,128)(2,1)}, u32[]{:S(2)}, u32[]{:S(2)}) collective-permute-start(bf16[256,256]{0,1:T(8,128)(2,1)} %copy.35), channel_id=1, source_target_pairs={{0,4},{2,6},{4,8},{6,10},{8,12},{10,14},{12,16},{14,18},{16,20},{1... | collective-permute-start | bytes 393224 | tf_op jit(solution)/shard_map/ppermute | solution.py:15
  16.2 16.5 %collective-permute-start.1 = (bf16[256,256]{0,1:T(8,128)(2,1)}, bf16[256,256]{0,1:T(8,128)(2,1)}, u32[]{:S(2)}, u32[]{:S(2)}) collective-permute-start(bf16[256,256]{0,1:T(8,128)(2,1)} %copy.35), channel_id=1, source_target_pairs={{0,2},{2,4},{4,6},{6,8},{8,10},{10,12},{12,14},{14,16},{16,18},{18... | collective-permute-start | bytes 393224 | tf_op jit(solution)/shard_map/ppermute | solution.py:15
  19.3 14.5 %collective-permute-start.2 = (bf16[256,256]{0,1:T(8,128)(2,1)S(1)}, bf16[256,256]{0,1:T(8,128)(2,1)}, u32[]{:S(2)}, u32[]{:S(2)}) collective-permute-start(bf16[256,256]{0,1:T(8,128)(2,1)S(1)} %copy.41), channel_id=1, source_target_pairs={{0,4},{2,6},{4,8},{6,10},{8,12},{10,14},{12,16},{14,18},{16,20},{1... | collective-permute-start | bytes 393224 | tf_op jit(solution)/shard_map/ppermute | solution.py:15
  22.6 11.2 %collective-permute-start.3 = (bf16[256,256]{0,1:T(8,128)(2,1)S(1)}, bf16[256,256]{0,1:T(8,128)(2,1)}, u32[]{:S(2)}, u32[]{:S(2)}) collective-permute-start(bf16[256,256]{0,1:T(8,128)(2,1)S(1)} %copy.41), channel_id=1, source_target_pairs={{0,2},{2,4},{4,6},{6,8},{8,10},{10,12},{12,14},{14,16},{16,18},{18... | collective-permute-start | bytes 393224 | tf_op jit(solution)/shard_map/ppermute | solution.py:15
  32.7 3.8 %copy-start.3 = (f32[2,7,256]{2,1,0:T(8,128)}, f32[2,7,256]{2,1,0:T(8,128)S(1)}, u32[]{:S(2)}) copy-start(f32[2,7,256]{2,1,0:T(8,128)S(1)} %sub.31) | copy-start | bytes 43012
  34.8 1.7 copy-start.1
  40.5 5.3 %copy-start.4 = (f32[2,7,256]{2,1,0:T(8,128)S(1)}, f32[2,7,256]{2,1,0:T(8,128)}, u32[]{:S(2)}) copy-start(f32[2,7,256]{2,1,0:T(8,128)} %copy-done.3) | copy-start | bytes 43012
  43.2 11.4 %collective-permute-start.4 = (f32[256,256]{0,1:T(8,128)}, f32[256,256]{0,1:T(8,128)S(1)}, u32[]{:S(2)}, u32[]{:S(2)}) collective-permute-start(f32[256,256]{0,1:T(8,128)} %bitcast.27), channel_id=1, source_target_pairs={{2,0},{4,2},{6,4},{8,6},{10,8},{12,10},{14,12},{16,14},{18,16},{20... | collective-permute-start | bytes 786440 | tf_op jit(solution)/shard_map/ppermute | solution.py:15
  44.5 12.8 %collective-permute-start.5 = (f32[256,256]{0,1:T(8,128)}, f32[256,256]{0,1:T(8,128)S(1)}, u32[]{:S(2)}, u32[]{:S(2)}) collective-permute-start(f32[256,256]{0,1:T(8,128)} %bitcast.28), channel_id=1, source_target_pairs={{4,0},{6,2},{8,4},{10,6},{12,8},{14,10},{16,12},{18,14},{20,16},{2... | collective-permute-start | bytes 786440 | tf_op jit(solution)/shard_map/ppermute | solution.py:15
  50.9 6.4 %collective-permute-start.6 = (f32[256,256]{0,1:T(8,128)S(1)}, f32[256,256]{0,1:T(8,128)S(1)}, u32[]{:S(2)}, u32[]{:S(2)}) collective-permute-start(f32[256,256]{0,1:T(8,128)S(1)} %bitcast.98), channel_id=1, source_target_pairs={{2,0},{4,2},{6,4},{8,6},{10,8},{12,10},{14,12},{16,14},{18,16},{20... | collective-permute-start | bytes 786440 | tf_op jit(solution)/shard_map/ppermute | solution.py:15
  52.2 13.8 %collective-permute-start.7 = (f32[256,256]{0,1:T(8,128)S(1)}, f32[256,256]{0,1:T(8,128)S(1)}, u32[]{:S(2)}, u32[]{:S(2)}) collective-permute-start(f32[256,256]{0,1:T(8,128)S(1)} %bitcast.97), channel_id=1, source_target_pairs={{4,0},{6,2},{8,4},{10,6},{12,8},{14,10},{16,12},{18,14},{20,16},{2... | collective-permute-start | bytes 786440 | tf_op jit(solution)/shard_map/ppermute | solution.py:15
Sparse Core Ops, SparseCore 0:
  9.7 135.9 all-gather.1
  157.8 49.5 reduce-scatter.1
where the time goes:
time: 217 us
  waiting for transfers between devices  141 us (65%)
  matrix products  24.3 us (11%)
  starting transfers between devices  20.2 us (9%)
  between operations  14.3 us (7%)
  local copies, waits for them, and re-layouts  8.76 us (4%)
  other arithmetic  8.48 us (4%)
    all_gather x1, waiting for transfers between devices, shards(): lax.all_gather(w_joined, 'seq', axis=0, tiled=True)  79.6 us
    reduce_scatter x1, waiting for transfers between devices, shards(): lax.psum_scatter(partial_sum, 'head', scatter_dimension=1, tiled=True)  49.7 us
    ppermute x8, starting transfers between devices, shifted(): return lax.ppermute(array, axis, pairs)  20.2 us
    dot_general x1, matrix products, projector(): jnp.einsum('tc,rc->tr', grad_rows, w_piece, preferred_element_type=jnp.fl...  12 us
    ppermute x8, waiting for transfers between devices, shifted(): return lax.ppermute(array, axis, pairs)  11.4 us
    unnamed x17, local copies, waits for them, and re-layouts  6.14 us
  transfers between devices with their start and end apart: 10, of which 4 were waited for; matrix products, arithmetic and copies ran while one was open for 11% of the time, Pallas kernels for 0%

commit v1 on v0

v1 whole, which is shorter than its diff:
```python
import math

import jax
import jax.numpy as jnp
from jax import lax
from jax.experimental import pallas as pl
from jax.experimental.pallas import tpu as pltpu
from jax.sharding import PartitionSpec as P

HEAD_SIZE = 128
WINDOW = 512
INNER = 4
LOG2E = 1.4426950408889634
F32 = jnp.float32
BF16 = jnp.bfloat16


def attention_kernel(
    first_ref, docs_ref, q_ref, do_ref, o_ref, lse_ref,
    k_own_ref, v_own_ref, k_near_ref, v_near_ref, k_far_ref, v_far_ref,
    dq_ref, own_ref, near_ref, far_ref,
    bias_ref, acc_k, acc_v,
):
    tokens = k_own_ref.shape[0]
    per_group = q_ref.shape[1] // HEAD_SIZE
    group = pl.program_id(0)
    groups = own_ref.shape[1] // (2 * HEAD_SIZE)
    scale = 1.0 / math.sqrt(HEAD_SIZE)
    rows = lax.broadcasted_iota(jnp.int32, (tokens, tokens), 0)
    cols = lax.broadcasted_iota(jnp.int32, (tokens, tokens), 1)
    causal = rows <= cols

    @pl.when(group == 0)
    def _():
        first = first_ref[0]
        spot = first + lax.broadcasted_iota(jnp.int32, (8, tokens), 1)
        start = jnp.int32(0)
        doc_begin = jnp.zeros((8, tokens), jnp.int32)
        for d in range(docs_ref.shape[0]):
            doc_begin = jnp.maximum(doc_begin, jnp.where(start <= spot, start, 0))
            start = start + docs_ref[d]
        doc_row = doc_begin[0:1]
        mixed = first + rows - jnp.where(causal, 0, 2 * tokens)
        near = first - tokens + rows
        bias_ref[0] = jnp.where(mixed >= doc_row, 0.0, -1e30)
        bias_ref[1] = jnp.where(near >= doc_row, 0.0, -1e30)

    nt = (((1,), (1,)), ((), ()))
    tn = (((0,), (0,)), ((), ()))

    def dot(a, b, dims=(((1,), (0,)), ((), ()))):
        return lax.dot_general(a, b, dims, preferred_element_type=F32)

    k_own, k_near, k_far = k_own_ref[...], k_near_ref[...], k_far_ref[...]
    v_own, v_near, v_far = v_own_ref[...], v_near_ref[...], v_far_ref[...]
    for j in range(per_group):
        span = slice(j * HEAD_SIZE, (j + 1) * HEAD_SIZE)
        q, do, o = q_ref[:, span], do_ref[:, span], o_ref[:, span]
        lse2 = lse_ref[pl.ds(group * per_group + j, 1), :] * LOG2E
        delta = jnp.sum((do.astype(F32) * o.astype(F32)).T, axis=0, keepdims=True)

        def prob(scores, bias):
            return jnp.exp2(scores * (scale * LOG2E) - lse2 + bias)

        p_mix = prob(jnp.where(causal, dot(k_own, q, nt), dot(k_far, q, nt)), bias_ref[0])
        p_near = prob(dot(k_near, q, nt), bias_ref[1])
        g_mix = jnp.where(causal, dot(v_own, do, nt), dot(v_far, do, nt))
        g_near = dot(v_near, do, nt)
        ds_mix = p_mix * (g_mix - delta) * scale
        ds_near = (p_near * (g_near - delta) * scale).astype(BF16)
        zero = jnp.zeros_like(p_mix)
        ds_own = jnp.where(causal, ds_mix, zero).astype(BF16)
        ds_far = jnp.where(causal, zero, ds_mix).astype(BF16)
        p_own = jnp.where(causal, p_mix, zero).astype(BF16)
        p_far = jnp.where(causal, zero, p_mix).astype(BF16)
        p_near = p_near.astype(BF16)
        dq = dot(ds_own, k_own, tn) + dot(ds_near, k_near, tn) + dot(ds_far, k_far, tn)
        dq_ref[:, span] = dq.astype(BF16)
        for i, (p, ds) in enumerate(((p_own, ds_own), (p_near, ds_near), (p_far, ds_far))):
            dv, dk = dot(p, do), dot(ds, q)
            if j == 0:
                acc_v[i], acc_k[i] = dv, dk
            else:
                acc_v[i] += dv
                acc_k[i] += dk
    k_cols = pl.ds(pl.multiple_of(group * HEAD_SIZE, HEAD_SIZE), HEAD_SIZE)
    v_cols = pl.ds(pl.multiple_of((groups + group) * HEAD_SIZE, HEAD_SIZE), HEAD_SIZE)
    for i, ref in enumerate((own_ref, near_ref, far_ref)):
        ref[:, k_cols] = acc_k[i].astype(ref.dtype)
        ref[:, v_cols] = acc_v[i].astype(ref.dtype)


def attention(first, doc_lengths, query, output_gradient, output, lse, own, near, far):
    tokens, width = query.shape
    kv_width = own.shape[1]
    groups = kv_width // (2 * HEAD_SIZE)
    wide = pl.BlockSpec((tokens, width // groups), lambda g: (0, g))
    smem = pl.BlockSpec(memory_space=pltpu.SMEM)
    k_spec = pl.BlockSpec((tokens, HEAD_SIZE), lambda g: (0, g))
    v_spec = pl.BlockSpec((tokens, HEAD_SIZE), lambda g: (0, groups + g))
    whole = pl.BlockSpec((tokens, kv_width), lambda g: (0, 0))
    return pl.pallas_call(
        attention_kernel,
        grid=(groups,),
        in_specs=[smem, smem, wide, wide, wide, pl.BlockSpec(lse.shape, lambda g: (0, 0))]
        + [k_spec, v_spec] * 3,
        out_specs=[wide, whole, whole, whole],
        out_shape=[
            jax.ShapeDtypeStruct((tokens, width), BF16),
            jax.ShapeDtypeStruct((tokens, kv_width), F32),
            jax.ShapeDtypeStruct((tokens, kv_width), BF16),
            jax.ShapeDtypeStruct((tokens, kv_width), BF16),
        ],
        scratch_shapes=[
            pltpu.VMEM((2, tokens, tokens), F32),
            pltpu.VMEM((3, tokens, HEAD_SIZE), F32),
            pltpu.VMEM((3, tokens, HEAD_SIZE), F32),
        ],
        compiler_params=pltpu.CompilerParams(vmem_limit_bytes=48 * 2**20),
        name="attention",
    )(first, doc_lengths, query, output_gradient, output, lse, own, own, near, near, far, far)


def project_kernel(pick_ref, grad_ref, *refs):
    shards, out_ref, weight, sem = refs[:-3], refs[-3], refs[-2], refs[-1]

    @pl.when(pl.program_id(0) == 0)
    def _():
        for i, shard in enumerate(shards):
            @pl.when(pick_ref[0] == i)
            def _():
                copy = pltpu.make_async_copy(shard, weight, sem)
                copy.start()
                copy.wait()

    out_ref[...] = lax.dot_general(
        grad_ref[...], weight[...], (((1,), (1,)), ((), ())), preferred_element_type=F32
    ).astype(out_ref.dtype)


def project(pick, grads, shards, dtype):
    tokens, depth = grads.shape
    cols = shards[0].shape[0]
    block = tokens // INNER
    return pl.pallas_call(
        project_kernel,
        grid=(INNER,),
        in_specs=[
            pl.BlockSpec(memory_space=pltpu.SMEM),
            pl.BlockSpec((block, depth), lambda t: (t, 0)),
        ]
        + [pl.BlockSpec(memory_space=pl.ANY)] * len(shards),
        out_specs=pl.BlockSpec((block, cols), lambda t: (t, 0)),
        out_shape=jax.ShapeDtypeStruct((tokens, cols), dtype),
        scratch_shapes=[pltpu.VMEM(shards[0].shape, BF16), pltpu.SemaphoreType.DMA],
        compiler_params=pltpu.CompilerParams(vmem_limit_bytes=32 * 2**20),
        name="project",
    )(pick.reshape(1).astype(jnp.int32), grads, *shards)


def shifted(array, by):
    peers = lax.axis_size("seq")
    pairs = [(i, i + by) for i in range(peers) if 0 <= i + by < peers]
    return lax.ppermute(array, "seq", pairs)


def swapped(array, bits):
    peers = lax.axis_size("seq")
    return lax.ppermute(array, "seq", [(i, i ^ bits) for i in range(peers)])


def layered(array, moves):
    pairs = [(a * INNER + i, b * INNER + i) for a, b in moves for i in range(INNER)]
    return lax.ppermute(array, "seq", pairs)


def returned(done, tokens):
    blocks = done.reshape(INNER, tokens, -1)
    return [blocks[0], swapped(blocks[2], 1), swapped(blocks[1], 2), swapped(blocks[3], 3)]


def ordered(blocks, inner):
    cols = []
    for j in range(INNER):
        pick = blocks[j]
        for i in range(1, INNER):
            pick = jnp.where(inner == i, blocks[j ^ i], pick)
        cols.append(pick)
    return jnp.concatenate(cols, 1)


def project_gathered(grads, weight, layers, tokens, head, inner):
    rows = weight.shape[0]
    groups = [[z * INNER + i for z in range(layers)] for i in range(INNER)]
    every = lax.all_gather(weight, "seq", axis=0, tiled=True, axis_index_groups=groups)
    halves = every.reshape(2, layers // 2 * rows, -1)

    def times(piece):
        return lax.dot_general(
            grads, piece, (((1,), (1,)), ((), ())), preferred_element_type=F32
        )

    send = times(jnp.where(head == 0, halves[1], halves[0])).astype(BF16)
    got = lax.ppermute(send, "head", [(0, 1), (1, 0)])
    keep = times(jnp.where(head == 0, halves[0], halves[1]))
    blocks = returned((keep + got.astype(F32)).astype(BF16), tokens)
    blocks = [b.reshape(tokens * (layers // 2), rows) for b in blocks]
    return ordered(blocks, inner).reshape(tokens, -1)


def shards(
    query, key, value, output, output_gradient, lse, doc_lengths, w_query, key_weight, value_weight
):
    tokens = query.shape[0]
    seq = lax.axis_index("seq")
    head = lax.axis_index("head")
    layer, inner = seq // INNER, seq % INNER
    layers = lax.axis_size("seq") // INNER
    half = layer // (layers // 2)

    weight = jnp.concatenate([w_query, key_weight, value_weight], 1)
    pair = jnp.concatenate([key, value], 1)
    near = shifted(pair, 1)
    far = shifted(pair, 2)
    if layers == 4:
        mate = layered(weight, [(0, 1), (1, 0), (2, 3), (3, 2)])
        mid = layered(weight, [(1, 2), (2, 1)])
        edge_third = layered(mid, [(1, 0), (2, 3)])
        mid_fourth = layered(mate, [(1, 2), (2, 1)])
        edge_fourth = layered(mid_fourth, [(1, 0), (2, 3)])

    first = (seq * tokens).astype(jnp.int32).reshape(1)
    dq, own_part, near_part, far_part = attention(
        first, doc_lengths, query, output_gradient, output, lse, pair, near, far
    )
    back_near = shifted(near_part, -1)
    back_far = shifted(far_part, -2)
    pair_grad = (own_part + back_near.astype(F32) + back_far.astype(F32)).astype(BF16)
    grads = jnp.concatenate([dq, pair_grad], 1)
    two = jnp.concatenate([grads, swapped(grads, 2)], 0)
    four = jnp.concatenate([two, swapped(two, 1)], 0)

    if layers != 4:
        return project_gathered(four, weight, layers, tokens, head, inner)

    is_edge = (layer == 0) | (layer == 3)
    same = head == half
    third = jnp.where(is_edge, 1, 2)
    fourth = jnp.where(is_edge, 1, 2)
    set_a = (weight, edge_third, mid)
    set_b = (mate, edge_fourth, mid_fourth)

    def finish(a_set, other):
        send = project(jnp.where(same, other, 0), four, a_set, BF16)
        got = lax.ppermute(send, "head", [(0, 1), (1, 0)])
        keep = project(jnp.where(same, 0, other), four, a_set, F32)
        return returned((keep + got.astype(F32)).astype(BF16), tokens)

    part_a = finish(set_a, third)
    part_b = finish(set_b, fourth)

    part_a, part_b = ordered(part_a, inner), ordered(part_b, inner)
    a_first = jnp.where(same, layer % 2 == 0, half == 0)
    return jnp.where(
        a_first,
        jnp.concatenate([part_a, part_b], 1),
        jnp.concatenate([part_b, part_a], 1),
    )


def solution(mesh):
    in_specs = (
        P("seq", "head"),
        P("seq", "head"),
        P("seq", "head"),
        P("seq", "head"),
        P("seq", "head"),
        P("head", "seq"),
        P(),
        P("seq", "head"),
        P("seq", "head"),
        P("seq", "head"),
    )
    out_specs = P("seq", "head")
    return jax.shard_map(shards, mesh=mesh, in_specs=in_specs, out_specs=out_specs, check_vma=False)
```

time: 217 us -> 181 us (0.83)
  waiting for transfers between devices: 141 us -> 108 us
  matrix products: 24.3 us -> 0 us
  Pallas kernels: 0 us -> 22.8 us
  between operations: 14.3 us -> 0.37 us
  starting transfers between devices: 20.2 us -> 29.5 us
  local copies, waits for them, and re-layouts: 8.76 us -> 12.6 us
    ppermute x8 -> x19, waiting for transfers between devices: 11.4 us -> 108 us  [the longest x5 57.3 us: layered(): return lax.ppermute(array, 'seq', pairs)]
    all_gather x1 -> x0, waiting for transfers between devices: 79.6 us -> none  [shards(): lax.all_gather(w_joined, 'seq', axis=0, tiled=True)]
    reduce_scatter x1 -> x0, waiting for transfers between devices: 49.7 us -> none  [shards(): lax.psum_scatter(partial_sum, 'head', scatter_dimension=1, tiled=True)]
    dot_general x6 -> x0, matrix products: 24.3 us -> none  [the longest x1 12 us: projector(): jnp.einsum('tc,rc->tr', grad_rows, w_piece, preferred_element_type=jnp.fl...]
    pallas_call x0 -> x5, Pallas kernels: none -> 22.8 us  [the longest x4 11.5 us: project(): pl.pallas_call(project_kernel, grid=(INNER,), in_specs=[pl.BlockSpec(memo...]
    ppermute x8 -> x19, starting transfers between devices: 20.2 us -> 29.5 us  [the longest x8 9.85 us: swapped(): return lax.ppermute(array, 'seq', [(i, i ^ bits) for i in range(peers)])]
    unnamed x17 -> x27, local copies, waits for them, and re-layouts: 6.14 us -> 10.4 us
    slice x3 -> x2, local copies, waits for them, and re-layouts: 2.62 us -> 0.06 us  [returned(): blocks[2]]
  transfers between devices with their start and end apart: 10 -> 19, of which waited for: 4 -> 9; matrix products, arithmetic and copies ran while one was open for 11% -> 3% of each run, Pallas kernels for 0% -> 6%
where the time goes in v1:
time: 181 us
  waiting for transfers between devices  108 us (60%)
  starting transfers between devices  29.5 us (16%)
  Pallas kernels  22.8 us (13%)
  local copies, waits for them, and re-layouts  12.6 us (7%)
  other arithmetic  7.78 us (4%)
    ppermute x5, waiting for transfers between devices, layered(): return lax.ppermute(array, 'seq', pairs)  57.3 us
    ppermute x8, waiting for transfers between devices, swapped(): return lax.ppermute(array, 'seq', [(i, i ^ bits) for i in range(peers)])  31.3 us
    ppermute x4, waiting for transfers between devices, shifted(): return lax.ppermute(array, 'seq', pairs)  15 us
    pallas_call x4, Pallas kernels, project(): pl.pallas_call(project_kernel, grid=(INNER,), in_specs=[pl.BlockSpec(memo...  11.5 us
    pallas_call x1, Pallas kernels, attention(): pl.pallas_call(attention_kernel, grid=(groups,), in_specs=[smem, smem, wi...  11.3 us
    unnamed x27, local copies, waits for them, and re-layouts  10.4 us
    ppermute x8, starting transfers between devices, swapped(): return lax.ppermute(array, 'seq', [(i, i ^ bits) for i in range(peers)])  9.85 us
    ppermute x4, starting transfers between devices, shifted(): return lax.ppermute(array, 'seq', pairs)  9.52 us
  transfers between devices with their start and end apart: 19, of which 9 were waited for; matrix products, arithmetic and copies ran while one was open for 3% of the time, Pallas kernels for 6%

profile of v1, /device:TPU:0, one launch (start us, length us, event | category | flops | bytes accessed | tf_op | source)
XLA Modules:
  0.0 180.6 jit_solution(13500245506673341233)
XLA Ops:
  1.8 2.4 %collective-permute-start = (bf16[256,512]{1,0:T(8,128)(2,1)S(1)}, bf16[256,512]{1,0:T(8,128)(2,1)S(1)}, u32[]{:S(2)}, u32[]{:S(2)}) collective-permute-start(bf16[256,512]{1,0:T(8,128)(2,1)S(1)} %constant_dynamic-update-slice_fusion.k_own_ref.v_own_ref), channel_id=1, source_target_pairs={{0,2},{2,4},{4,6},{6,8},{8,10},{10,12},{12,14},{14,16},{16,18},{18... | collective-permute-start | bytes 786440 | tf_op jit(solution)/shard_map/ppermute | solution.py:164
  4.2 4.4 %collective-permute-start.1 = (bf16[256,512]{1,0:T(8,128)(2,1)S(1)}, bf16[256,512]{1,0:T(8,128)(2,1)S(1)}, u32[]{:S(2)}, u32[]{:S(2)}) collective-permute-start(bf16[256,512]{1,0:T(8,128)(2,1)S(1)} %constant_dynamic-update-slice_fusion.k_own_ref.v_own_ref), channel_id=1, source_target_pairs={{0,4},{2,6},{4,8},{6,10},{8,12},{10,14},{12,16},{14,18},{16,20},{1... | collective-permute-start | bytes 786440 | tf_op jit(solution)/shard_map/ppermute | solution.py:164
  8.7 6.7 %collective-permute-done.1.k_far_ref.v_far_ref = bf16[256,512]{1,0:T(8,128)(2,1)S(1)} collective-permute-done((bf16[256,512]{1,0:T(8,128)(2,1)S(1)}, bf16[256,512]{1,0:T(8,128)(2,1)S(1)}, u32[]{:S(2)}, u32[]{:S(2)}) %collective-permute-start.1) | collective-permute-done | bytes 262176 | tf_op jit(solution)/shard_map/ppermute | solution.py:164
  15.3 1.2 copy-done.3
  20.2 11.3 %attention.1 = (bf16[256,1792]{1,0:T(8,128)(2,1)S(1)}, f32[256,512]{1,0:T(8,128)S(1)}, bf16[256,512]{1,0:T(8,128)(2,1)S(1)}, bf16[256,512]{1,0:T(8,128)(2,1)S(1)}) custom-call(s32[1]{0:T(128)} %bitcast.1.first_ref, s32[4]{0:T(128)S(1)} %copy-done.7, bf16[256,1792]{1,0:T(8,128)(2,1)S(1)} %copy-done.3, bf16[256,1792]{1,0:T(8,128)(2,1)S(1)} %copy-done.4, ...), custom_call_target="tpu_custom_call" | custom-call | tf_op jit(solution)/shard_map/attention/pallas_call | solution.py:102
  31.6 1.4 collective-permute-start.3
  33.0 1.3 collective-permute-start.2
  34.3 8.4 %collective-permute-done.3 = bf16[256,512]{1,0:T(8,128)(2,1)S(1)} collective-permute-done((bf16[256,512]{1,0:T(8,128)(2,1)S(1)}, bf16[256,512]{1,0:T(8,128)(2,1)S(1)}, u32[]{:S(2)}, u32[]{:S(2)}) %collective-permute-start.3) | collective-permute-done | bytes 262176 | tf_op jit(solution)/shard_map/ppermute | solution.py:164
  42.9 2.7 %collective-permute-start.4 = (bf16[256,2304]{1,0:T(8,128)(2,1)S(1)}, bf16[256,2304]{1,0:T(8,128)(2,1)S(1)}, u32[]{:S(2)}, u32[]{:S(2)}) collective-permute-start(bf16[256,2304]{1,0:T(8,128)(2,1)S(1)} %pad_maximum_fusion.2), channel_id=1, source_target_pairs={{0,4},{2,6},{4,0},{6,2},{8,12},{10,14},{12,8},{14,10},{16,20},{18,... | collective-permute-start | bytes 3538952 | tf_op jit(solution)/shard_map/ppermute | solution.py:169
  45.6 24.8 %collective-permute-done.4 = bf16[256,2304]{1,0:T(8,128)(2,1)S(1)} collective-permute-done((bf16[256,2304]{1,0:T(8,128)(2,1)S(1)}, bf16[256,2304]{1,0:T(8,128)(2,1)S(1)}, u32[]{:S(2)}, u32[]{:S(2)}) %collective-permute-start.4) | collective-permute-done | bytes 1179680 | tf_op jit(solution)/shard_map/ppermute | solution.py:169
  70.5 1.7 pad_maximum_fusion.1
  72.2 1.8 %collective-permute-start.5 = (bf16[512,2304]{1,0:T(8,128)(2,1)}, bf16[512,2304]{1,0:T(8,128)(2,1)}, u32[]{:S(2)}, u32[]{:S(2)}) collective-permute-start(bf16[512,2304]{1,0:T(8,128)(2,1)} %pad_maximum_fusion.1), channel_id=1, source_target_pairs={{0,2},{2,0},{4,6},{6,4},{8,10},{10,8},{12,14},{14,12},{16,18},{18,... | collective-permute-start | bytes 7077896 | tf_op jit(solution)/shard_map/ppermute | solution.py:169
  74.1 3.0 %collective-permute-start.12 = (bf16[224,2304]{1,0:T(8,128)(2,1)S(1)}, bf16[224,2304]{1,0:T(8,128)(2,1)S(1)}, u32[]{:S(2)}, u32[]{:S(2)}) collective-permute-start(bf16[224,2304]{1,0:T(8,128)(2,1)S(1)} %constant_dynamic-update-slice_fusion.2.refs_0_), channel_id=1, source_target_pairs={{0,8},{2,10},{4,12},{6,14},{8,0},{10,2},{12,4},{14,6},{16,24},{18,... | collective-permute-start | bytes 3096584 | tf_op jit(solution)/shard_map/ppermute | solution.py:174
  77.1 1.7 collective-permute-start.6
  78.7 21.3 %collective-permute-done.12.refs_0_ = bf16[224,2304]{1,0:T(8,128)(2,1)S(1)} collective-permute-done((bf16[224,2304]{1,0:T(8,128)(2,1)S(1)}, bf16[224,2304]{1,0:T(8,128)(2,1)S(1)}, u32[]{:S(2)}, u32[]{:S(2)}) %collective-permute-start.12) | collective-permute-done | bytes 1032224 | tf_op jit(solution)/shard_map/ppermute | solution.py:174
  100.1 1.7 collective-permute-start.13
  101.7 1.3 collective-permute-start.7
  103.0 1.3 collective-permute-start.14
  104.4 4.5 %pad_maximum_fusion.grad_ref = bf16[1024,2304]{1,0:T(8,128)(2,1)S(1)} fusion(bf16[512,2304]{1,0:T(8,128)(2,1)} %collective-permute-done.5, bf16[256,2304]{1,0:T(8,128)(2,1)} %copy-done.8, bf16[256,512]{1,0:T(8,128)(2,1)S(1)} %add_convert_fusion.2, bf16[256,1792]{1,0:T(8,128)(2,1)S(1)} %get-tuple-element.9), kind=kLoop, calls=%fused_computation | loop fusion | flops 18874368 | bytes 9437184 | tf_op jit(solution)/shard_map/concatenate | solution.py:241
  108.9 20.2 %collective-permute-done.7.refs_1_ = bf16[224,2304]{1,0:T(8,128)(2,1)} collective-permute-done((bf16[224,2304]{1,0:T(8,128)(2,1)}, bf16[224,2304]{1,0:T(8,128)(2,1)}, u32[]{:S(2)}, u32[]{:S(2)}) %collective-permute-start.7) | collective-permute-done | bytes 1032224 | tf_op jit(solution)/shard_map/ppermute | solution.py:174
  129.0 3.2 %project.5 = bf16[1024,224]{1,0:T(8,128)(2,1)S(1)} custom-call(s32[1]{0:T(128)} %bitcast.2.pick_ref, bf16[1024,2304]{1,0:T(8,128)(2,1)S(1)} %pad_maximum_fusion.grad_ref, bf16[224,2304]{1,0:T(8,128)(2,1)S(1)} %constant_dynamic-update-slice_fusion.2.refs_0_, bf16[224,2304]{1,0:T(8,128)(2,1)} %collective-permute-done.7.refs_1_, ...), custom_call_target="tpu_custom_call" | custom-call | tf_op jit(solution)/shard_map/project/pallas_call | solution.py:145
  132.3 2.1 %copy-done = bf16[1024,2304]{1,0:T(8,128)(2,1)} copy-done((bf16[1024,2304]{1,0:T(8,128)(2,1)}, bf16[1024,2304]{1,0:T(8,128)(2,1)S(1)}, u32[]{:S(2)}) %copy-start) | copy-done | bytes 4718616
  135.1 15.8 %collective-permute-done.14.refs_1_ = bf16[224,2304]{1,0:T(8,128)(2,1)} collective-permute-done((bf16[224,2304]{1,0:T(8,128)(2,1)}, bf16[224,2304]{1,0:T(8,128)(2,1)}, u32[]{:S(2)}, u32[]{:S(2)}) %collective-permute-start.14) | collective-permute-done | bytes 1032224 | tf_op jit(solution)/shard_map/ppermute | solution.py:174
  150.9 2.3 %copy-done.1 = bf16[1024,2304]{1,0:T(8,128)(2,1)S(1)} copy-done((bf16[1024,2304]{1,0:T(8,128)(2,1)S(1)}, bf16[1024,2304]{1,0:T(8,128)(2,1)}, u32[]{:S(2)}) %copy-start.1) | copy-done | bytes 4718616
  153.3 3.4 %project.7 = bf16[1024,224]{1,0:T(8,128)(2,1)S(1)} custom-call(s32[1]{0:T(128)} %bitcast.2.pick_ref, bf16[1024,2304]{1,0:T(8,128)(2,1)S(1)} %copy-done.1, bf16[224,2304]{1,0:T(8,128)(2,1)S(1)} %collective-permute-done.12.refs_0_, bf16[224,2304]{1,0:T(8,128)(2,1)} %collective-permute-done.14.refs_1_, bf16[224,2304]{1,0:T(8,128)(2,1)} %collective-permute-done.13.refs_2_), custom_call_target="tpu_custom_call" | custom-call | tf_op jit(solution)/shard_map/project/pallas_call | solution.py:145
  157.3 2.4 %project.4 = f32[1024,224]{1,0:T(8,128)S(1)} custom-call(s32[1]{0:T(128)} %bitcast.pick_ref, bf16[1024,2304]{1,0:T(8,128)(2,1)S(1)} %copy-done.2, bf16[224,2304]{1,0:T(8,128)(2,1)S(1)} %constant_dynamic-update-slice_fusion.2.refs_0_, bf16[224,2304]{1,0:T(8,128)(2,1)} %collective-permute-done.7.refs_1_, bf16[224,2304]{1,0:T(8,128)(2,1)} %collective-permute-done.6.refs_2_), custom_call_target="tpu_custom_call" | custom-call | tf_op jit(solution)/shard_map/project/pallas_call | solution.py:145
  159.7 2.4 %project.6 = f32[1024,224]{1,0:T(8,128)S(1)} custom-call(s32[1]{0:T(128)} %bitcast.pick_ref, bf16[1024,2304]{1,0:T(8,128)(2,1)S(1)} %copy-done.2, bf16[224,2304]{1,0:T(8,128)(2,1)S(1)} %collective-permute-done.12.refs_0_, bf16[224,2304]{1,0:T(8,128)(2,1)} %collective-permute-done.14.refs_1_, bf16[224,2304]{1,0:T(8,128)(2,1)} %collective-permute-done.13.refs_2_), custom_call_target="tpu_custom_call" | custom-call | tf_op jit(solution)/shard_map/project/pallas_call | solution.py:145
  162.4 2.2 %collective-permute-start.10 = (bf16[256,224]{1,0:T(8,128)(2,1)S(1)}, bf16[256,224]{1,0:T(8,128)(2,1)S(1)}, u32[]{:S(2)}, u32[]{:S(2)}) collective-permute-start(bf16[256,224]{1,0:T(8,128)(2,1)S(1)} %get-tuple-element.25), channel_id=1, source_target_pairs={{0,4},{2,6},{4,0},{6,2},{8,12},{10,14},{12,8},{14,10},{16,20},{18,... | collective-permute-start | bytes 344072 | tf_op jit(solution)/shard_map/ppermute | solution.py:169
  164.7 3.9 %collective-permute-done.15 = bf16[1024,224]{1,0:T(8,128)(2,1)S(1)} collective-permute-done((bf16[1024,224]{1,0:T(8,128)(2,1)S(1)}, bf16[1024,224]{1,0:T(8,128)(2,1)S(1)}, u32[]{:S(2)}, u32[]{:S(2)}) %collective-permute-start.15) | collective-permute-done | bytes 458784 | tf_op jit(solution)/shard_map/ppermute | solution.py:255
  168.8 2.8 %collective-permute-start.17 = (bf16[256,224]{1,0:T(8,128)(2,1)S(1)}, bf16[256,224]{1,0:T(8,128)(2,1)S(1)}, u32[]{:S(2)}, u32[]{:S(2)}) collective-permute-start(bf16[256,224]{1,0:T(8,128)(2,1)S(1)} %get-tuple-element.22), channel_id=1, source_target_pairs={{0,4},{2,6},{4,0},{6,2},{8,12},{10,14},{12,8},{14,10},{16,20},{18,... | collective-permute-start | bytes 344072 | tf_op jit(solution)/shard_map/ppermute | solution.py:169
  171.8 4.2 %collective-permute-done.17 = bf16[256,224]{1,0:T(8,128)(2,1)S(1)} collective-permute-done((bf16[256,224]{1,0:T(8,128)(2,1)S(1)}, bf16[256,224]{1,0:T(8,128)(2,1)S(1)}, u32[]{:S(2)}, u32[]{:S(2)}) %collective-permute-start.17) | collective-permute-done | bytes 114720 | tf_op jit(solution)/shard_map/ppermute | solution.py:169
  176.0 2.3 %collective-permute-done.16 = bf16[256,224]{1,0:T(8,128)(2,1)S(1)} collective-permute-done((bf16[256,224]{1,0:T(8,128)(2,1)S(1)}, bf16[256,224]{1,0:T(8,128)(2,1)S(1)}, u32[]{:S(2)}, u32[]{:S(2)}) %collective-permute-start.16) | collective-permute-done | bytes 114720 | tf_op jit(solution)/shard_map/ppermute | solution.py:169
  (53 shorter events, 10.1 us)
Async XLA Ops:
  1.8 6.8 %collective-permute-start = (bf16[256,512]{1,0:T(8,128)(2,1)S(1)}, bf16[256,512]{1,0:T(8,128)(2,1)S(1)}, u32[]{:S(2)}, u32[]{:S(2)}) collective-permute-start(bf16[256,512]{1,0:T(8,128)(2,1)S(1)} %constant_dynamic-update-slice_fusion.k_own_ref.v_own_ref), channel_id=1, source_target_pairs={{0,2},{2,4},{4,6},{6,8},{8,10},{10,12},{12,14},{14,16},{16,18},{18... | collective-permute-start | bytes 786440 | tf_op jit(solution)/shard_map/ppermute | solution.py:164
  4.2 11.1 %collective-permute-start.1 = (bf16[256,512]{1,0:T(8,128)(2,1)S(1)}, bf16[256,512]{1,0:T(8,128)(2,1)S(1)}, u32[]{:S(2)}, u32[]{:S(2)}) collective-permute-start(bf16[256,512]{1,0:T(8,128)(2,1)S(1)} %constant_dynamic-update-slice_fusion.k_own_ref.v_own_ref), channel_id=1, source_target_pairs={{0,4},{2,6},{4,8},{6,10},{8,12},{10,14},{12,16},{14,18},{16,20},{1... | collective-permute-start | bytes 786440 | tf_op jit(solution)/shard_map/ppermute | solution.py:164
  15.3 1.2 copy-start.3
  16.5 1.2 copy-start.4
  17.7 1.2 copy-start.5
  18.9 0.7 copy-start.6
  19.6 0.7 copy-start.7
  31.6 42.4 %copy-start.9 = (bf16[224,1792]{1,0:T(8,128)(2,1)S(1)}, bf16[224,1792]{1,0:T(8,128)(2,1)}, u32[]{:S(2)}) copy-start(bf16[224,1792]{1,0:T(8,128)(2,1)} %param.17) | copy-start | bytes 2408452
  31.6 11.1 %collective-permute-start.3 = (bf16[256,512]{1,0:T(8,128)(2,1)S(1)}, bf16[256,512]{1,0:T(8,128)(2,1)S(1)}, u32[]{:S(2)}, u32[]{:S(2)}) collective-permute-start(bf16[256,512]{1,0:T(8,128)(2,1)S(1)} %get-tuple-element.12), channel_id=1, source_target_pairs={{4,0},{6,2},{8,4},{10,6},{12,8},{14,10},{16,12},{18,14},{20,16},{2... | collective-permute-start | bytes 786440 | tf_op jit(solution)/shard_map/ppermute | solution.py:164
  33.0 9.7 %collective-permute-start.2 = (bf16[256,512]{1,0:T(8,128)(2,1)S(1)}, bf16[256,512]{1,0:T(8,128)(2,1)S(1)}, u32[]{:S(2)}, u32[]{:S(2)}) collective-permute-start(bf16[256,512]{1,0:T(8,128)(2,1)S(1)} %get-tuple-element.11), channel_id=1, source_target_pairs={{2,0},{4,2},{6,4},{8,6},{10,8},{12,10},{14,12},{16,14},{18,16},{20... | collective-permute-start | bytes 786440 | tf_op jit(solution)/shard_map/ppermute | solution.py:164
  42.7 31.3 %copy-start.10 = (bf16[224,256]{1,0:T(8,128)(2,1)S(1)}, bf16[224,256]{1,0:T(8,128)(2,1)}, u32[]{:S(2)}) copy-start(bf16[224,256]{1,0:T(8,128)(2,1)} %param.18) | copy-start | bytes 344068
  42.8 31.2 %copy-start.11 = (bf16[224,256]{1,0:T(8,128)(2,1)S(1)}, bf16[224,256]{1,0:T(8,128)(2,1)}, u32[]{:S(2)}) copy-start(bf16[224,256]{1,0:T(8,128)(2,1)} %param.19) | copy-start | bytes 344068
  42.9 27.5 %collective-permute-start.4 = (bf16[256,2304]{1,0:T(8,128)(2,1)S(1)}, bf16[256,2304]{1,0:T(8,128)(2,1)S(1)}, u32[]{:S(2)}, u32[]{:S(2)}) collective-permute-start(bf16[256,2304]{1,0:T(8,128)(2,1)S(1)} %pad_maximum_fusion.2), channel_id=1, source_target_pairs={{0,4},{2,6},{4,0},{6,2},{8,12},{10,14},{12,8},{14,10},{16,20},{18,... | collective-permute-start | bytes 3538952 | tf_op jit(solution)/shard_map/ppermute | solution.py:169
  70.5 32.6 %copy-start.8 = (bf16[256,2304]{1,0:T(8,128)(2,1)}, bf16[256,2304]{1,0:T(8,128)(2,1)S(1)}, u32[]{:S(2)}) copy-start(bf16[256,2304]{1,0:T(8,128)(2,1)S(1)} %collective-permute-done.4) | copy-start | bytes 3538948
  72.2 32.2 %collective-permute-start.5 = (bf16[512,2304]{1,0:T(8,128)(2,1)}, bf16[512,2304]{1,0:T(8,128)(2,1)}, u32[]{:S(2)}, u32[]{:S(2)}) collective-permute-start(bf16[512,2304]{1,0:T(8,128)(2,1)} %pad_maximum_fusion.1), channel_id=1, source_target_pairs={{0,2},{2,0},{4,6},{6,4},{8,10},{10,8},{12,14},{14,12},{16,18},{18,... | collective-permute-start | bytes 7077896 | tf_op jit(solution)/shard_map/ppermute | solution.py:169
  74.1 25.9 %collective-permute-start.12 = (bf16[224,2304]{1,0:T(8,128)(2,1)S(1)}, bf16[224,2304]{1,0:T(8,128)(2,1)S(1)}, u32[]{:S(2)}, u32[]{:S(2)}) collective-permute-start(bf16[224,2304]{1,0:T(8,128)(2,1)S(1)} %constant_dynamic-update-slice_fusion.2.refs_0_), channel_id=1, source_target_pairs={{0,8},{2,10},{4,12},{6,14},{8,0},{10,2},{12,4},{14,6},{16,24},{18,... | collective-permute-start | bytes 3096584 | tf_op jit(solution)/shard_map/ppermute | solution.py:174
  77.1 24.6 %collective-permute-start.6 = (bf16[224,2304]{1,0:T(8,128)(2,1)S(1)}, bf16[224,2304]{1,0:T(8,128)(2,1)}, u32[]{:S(2)}, u32[]{:S(2)}) collective-permute-start(bf16[224,2304]{1,0:T(8,128)(2,1)S(1)} %constant_dynamic-update-slice_fusion.2.refs_0_), channel_id=1, source_target_pairs={{8,16},{10,18},{12,20},{14,22},{16,8},{18,10},{20,12},{22,14},{9,1... | collective-permute-start | bytes 3096584 | tf_op jit(solution)/shard_map/ppermute | solution.py:174
  100.1 3.0 %collective-permute-start.13 = (bf16[224,2304]{1,0:T(8,128)(2,1)S(1)}, bf16[224,2304]{1,0:T(8,128)(2,1)}, u32[]{:S(2)}, u32[]{:S(2)}) collective-permute-start(bf16[224,2304]{1,0:T(8,128)(2,1)S(1)} %collective-permute-done.12.refs_0_), channel_id=1, source_target_pairs={{8,16},{10,18},{12,20},{14,22},{16,8},{18,10},{20,12},{22,14},{9,1... | collective-permute-start | bytes 3096584 | tf_op jit(solution)/shard_map/ppermute | solution.py:174
  101.7 27.3 %collective-permute-start.7 = (bf16[224,2304]{1,0:T(8,128)(2,1)}, bf16[224,2304]{1,0:T(8,128)(2,1)}, u32[]{:S(2)}, u32[]{:S(2)}) collective-permute-start(bf16[224,2304]{1,0:T(8,128)(2,1)} %collective-permute-done.6.refs_2_), channel_id=1, source_target_pairs={{8,0},{10,2},{12,4},{14,6},{16,24},{18,26},{20,28},{22,30},{9,1},{... | collective-permute-start | bytes 3096584 | tf_op jit(solution)/shard_map/ppermute | solution.py:174
  103.0 47.9 %collective-permute-start.14 = (bf16[224,2304]{1,0:T(8,128)(2,1)}, bf16[224,2304]{1,0:T(8,128)(2,1)}, u32[]{:S(2)}, u32[]{:S(2)}) collective-permute-start(bf16[224,2304]{1,0:T(8,128)(2,1)} %collective-permute-done.13.refs_2_), channel_id=1, source_target_pairs={{8,0},{10,2},{12,4},{14,6},{16,24},{18,26},{20,28},{22,30},{9,1},{... | collective-permute-start | bytes 3096584 | tf_op jit(solution)/shard_map/ppermute | solution.py:174
  132.3 2.1 %copy-start = (bf16[1024,2304]{1,0:T(8,128)(2,1)}, bf16[1024,2304]{1,0:T(8,128)(2,1)S(1)}, u32[]{:S(2)}) copy-start(bf16[1024,2304]{1,0:T(8,128)(2,1)S(1)} %pad_maximum_fusion.grad_ref) | copy-start | bytes 14155780
  134.4 27.7 %collective-permute-start.8 = (bf16[1024,224]{1,0:T(8,128)(2,1)S(1)}, bf16[1024,224]{1,0:T(8,128)(2,1)S(1)}, u32[]{:S(2)}, u32[]{:S(2)}) collective-permute-start(bf16[1024,224]{1,0:T(8,128)(2,1)S(1)} %project.5), channel_id=1, source_target_pairs={{0,1},{1,0},{2,3},{3,2},{4,5},{5,4},{6,7},{7,6},{8,9},{9,8},{10,11... | collective-permute-start | bytes 1376264 | tf_op jit(solution)/shard_map/ppermute | solution.py:255
  150.9 2.3 %copy-start.1 = (bf16[1024,2304]{1,0:T(8,128)(2,1)S(1)}, bf16[1024,2304]{1,0:T(8,128)(2,1)}, u32[]{:S(2)}) copy-start(bf16[1024,2304]{1,0:T(8,128)(2,1)} %copy-done) | copy-start | bytes 14155780
  153.3 4.0 %copy-start.2 = (bf16[1024,2304]{1,0:T(8,128)(2,1)S(1)}, bf16[1024,2304]{1,0:T(8,128)(2,1)}, u32[]{:S(2)}) copy-start(bf16[1024,2304]{1,0:T(8,128)(2,1)} %copy-done) | copy-start | bytes 14155780
  156.7 11.9 %collective-permute-start.15 = (bf16[1024,224]{1,0:T(8,128)(2,1)S(1)}, bf16[1024,224]{1,0:T(8,128)(2,1)S(1)}, u32[]{:S(2)}, u32[]{:S(2)}) collective-permute-start(bf16[1024,224]{1,0:T(8,128)(2,1)S(1)} %project.7), channel_id=1, source_target_pairs={{0,1},{1,0},{2,3},{3,2},{4,5},{5,4},{6,7},{7,6},{8,9},{9,8},{10,11... | collective-permute-start | bytes 1376264 | tf_op jit(solution)/shard_map/ppermute | solution.py:255
  162.3 9.4 %collective-permute-start.11 = (bf16[256,224]{1,0:T(8,128)(2,1)S(1)}, bf16[256,224]{1,0:T(8,128)(2,1)S(1)}, u32[]{:S(2)}, u32[]{:S(2)}) collective-permute-start(bf16[256,224]{1,0:T(8,128)(2,1)S(1)} %get-tuple-element.24), channel_id=1, source_target_pairs={{0,2},{2,0},{4,6},{6,4},{8,10},{10,8},{12,14},{14,12},{16,18},{18,... | collective-permute-start | bytes 344072 | tf_op jit(solution)/shard_map/ppermute | solution.py:169
  162.4 9.4 %collective-permute-start.10 = (bf16[256,224]{1,0:T(8,128)(2,1)S(1)}, bf16[256,224]{1,0:T(8,128)(2,1)S(1)}, u32[]{:S(2)}, u32[]{:S(2)}) collective-permute-start(bf16[256,224]{1,0:T(8,128)(2,1)S(1)} %get-tuple-element.25), channel_id=1, source_target_pairs={{0,4},{2,6},{4,0},{6,2},{8,12},{10,14},{12,8},{14,10},{16,20},{18,... | collective-permute-start | bytes 344072 | tf_op jit(solution)/shard_map/ppermute | solution.py:169
  164.6 7.1 %collective-permute-start.9 = (bf16[256,224]{1,0:T(8,128)(2,1)S(1)}, bf16[256,224]{1,0:T(8,128)(2,1)S(1)}, u32[]{:S(2)}, u32[]{:S(2)}) collective-permute-start(bf16[256,224]{1,0:T(8,128)(2,1)S(1)} %get-tuple-element.26), channel_id=1, source_target_pairs={{0,6},{2,4},{4,2},{6,0},{8,14},{10,12},{12,10},{14,8},{16,22},{18,... | collective-permute-start | bytes 344072 | tf_op jit(solution)/shard_map/ppermute | solution.py:169
  168.7 3.0 %collective-permute-start.18 = (bf16[256,224]{1,0:T(8,128)(2,1)S(1)}, bf16[256,224]{1,0:T(8,128)(2,1)S(1)}, u32[]{:S(2)}, u32[]{:S(2)}) collective-permute-start(bf16[256,224]{1,0:T(8,128)(2,1)S(1)} %get-tuple-element.21), channel_id=1, source_target_pairs={{0,2},{2,0},{4,6},{6,4},{8,10},{10,8},{12,14},{14,12},{16,18},{18,... | collective-permute-start | bytes 344072 | tf_op jit(solution)/shard_map/ppermute | solution.py:169
  168.8 7.2 %collective-permute-start.17 = (bf16[256,224]{1,0:T(8,128)(2,1)S(1)}, bf16[256,224]{1,0:T(8,128)(2,1)S(1)}, u32[]{:S(2)}, u32[]{:S(2)}) collective-permute-start(bf16[256,224]{1,0:T(8,128)(2,1)S(1)} %get-tuple-element.22), channel_id=1, source_target_pairs={{0,4},{2,6},{4,0},{6,2},{8,12},{10,14},{12,8},{14,10},{16,20},{18,... | collective-permute-start | bytes 344072 | tf_op jit(solution)/shard_map/ppermute | solution.py:169
  171.7 6.6 %collective-permute-start.16 = (bf16[256,224]{1,0:T(8,128)(2,1)S(1)}, bf16[256,224]{1,0:T(8,128)(2,1)S(1)}, u32[]{:S(2)}, u32[]{:S(2)}) collective-permute-start(bf16[256,224]{1,0:T(8,128)(2,1)S(1)} %get-tuple-element.23), channel_id=1, source_target_pairs={{0,6},{2,4},{4,2},{6,0},{8,14},{10,12},{12,10},{14,8},{16,22},{18,... | collective-permute-start | bytes 344072 | tf_op jit(solution)/shard_map/ppermute | solution.py:169

commit v2 on v1

v2 whole, which is shorter than its diff:
```python
import functools
import math

import jax
import jax.numpy as jnp
from jax import lax
from jax.experimental import pallas as pl
from jax.experimental.pallas import tpu as pltpu
from jax.sharding import PartitionSpec as P

HEAD_SIZE = 128
WINDOW = 512
INNER = 4
LOG2E = 1.4426950408889634
VMEM_LIMIT = 63 * 2**20
F32 = jnp.float32
BF16 = jnp.bfloat16


def attention_kernel(
    group, groups, first_ref, docs_ref, q_ref, do_ref, o_ref, lse_ref,
    k_own_ref, v_own_ref, k_near_ref, v_near_ref, k_far_ref, v_far_ref,
    *refs,
):
    *earlier, dq_ref, own_ref, near_ref, far_ref, acc_k, acc_v = refs
    tokens = k_own_ref.shape[0]
    per_group = q_ref.shape[1] // HEAD_SIZE
    scale = 1.0 / math.sqrt(HEAD_SIZE)
    rows = lax.broadcasted_iota(jnp.int32, (tokens, tokens), 0)
    cols = lax.broadcasted_iota(jnp.int32, (tokens, tokens), 1)
    causal = rows <= cols
    first = first_ref[0]
    spot = first + lax.broadcasted_iota(jnp.int32, (8, tokens), 1)
    start = jnp.int32(0)
    doc_begin = jnp.zeros((8, tokens), jnp.int32)
    for d in range(docs_ref.shape[0]):
        doc_begin = jnp.maximum(doc_begin, jnp.where(start <= spot, start, 0))
        start = start + docs_ref[d]
    doc_row = doc_begin[0:1]
    mixed = first + rows - jnp.where(causal, 0, 2 * tokens)
    bias_mix = jnp.where(mixed >= doc_row, 0.0, -1e30)
    bias_near = jnp.where(first - tokens + rows >= doc_row, 0.0, -1e30)

    nt = (((1,), (1,)), ((), ()))
    tn = (((0,), (0,)), ((), ()))

    def dot(a, b, dims=(((1,), (0,)), ((), ()))):
        return lax.dot_general(a, b, dims, preferred_element_type=F32)

    k_own, k_near, k_far = k_own_ref[...], k_near_ref[...], k_far_ref[...]
    v_own, v_near, v_far = v_own_ref[...], v_near_ref[...], v_far_ref[...]
    for j in range(per_group):
        span = slice(j * HEAD_SIZE, (j + 1) * HEAD_SIZE)
        q, do, o = q_ref[:, span], do_ref[:, span], o_ref[:, span]
        head = group * per_group + j
        lse2 = lse_ref[head : head + 1, :] * LOG2E
        delta = jnp.sum((do.astype(F32) * o.astype(F32)).T, axis=0, keepdims=True)

        def prob(scores, bias):
            return jnp.exp2(scores * (scale * LOG2E) - lse2 + bias)

        p_mix = prob(jnp.where(causal, dot(k_own, q, nt), dot(k_far, q, nt)), bias_mix)
        p_near = prob(dot(k_near, q, nt), bias_near)
        g_mix = jnp.where(causal, dot(v_own, do, nt), dot(v_far, do, nt))
        g_near = dot(v_near, do, nt)
        ds_mix = p_mix * (g_mix - delta) * scale
        ds_near = (p_near * (g_near - delta) * scale).astype(BF16)
        zero = jnp.zeros_like(p_mix)
        ds_own = jnp.where(causal, ds_mix, zero).astype(BF16)
        ds_far = jnp.where(causal, zero, ds_mix).astype(BF16)
        p_own = jnp.where(causal, p_mix, zero).astype(BF16)
        p_far = jnp.where(causal, zero, p_mix).astype(BF16)
        p_near = p_near.astype(BF16)
        dq = dot(ds_own, k_own, tn) + dot(ds_near, k_near, tn) + dot(ds_far, k_far, tn)
        dq_ref[:, span] = dq.astype(BF16)
        for i, (p, ds) in enumerate(((p_own, ds_own), (p_near, ds_near), (p_far, ds_far))):
            dv, dk = dot(p, do), dot(ds, q)
            if j == 0:
                acc_v[i], acc_k[i] = dv, dk
            else:
                acc_v[i] += dv
                acc_k[i] += dk
    for i, ref in enumerate((own_ref, near_ref, far_ref)):
        if group < groups - 1:
            ref[:, :HEAD_SIZE] = acc_k[i].astype(ref.dtype)
            ref[:, HEAD_SIZE:] = acc_v[i].astype(ref.dtype)
            continue
        for g in range(groups):
            k_cols = slice(g * HEAD_SIZE, (g + 1) * HEAD_SIZE)
            v_cols = slice((groups + g) * HEAD_SIZE, (groups + g + 1) * HEAD_SIZE)
            if g == group:
                ref[:, k_cols] = acc_k[i].astype(ref.dtype)
                ref[:, v_cols] = acc_v[i].astype(ref.dtype)
            else:
                ref[:, k_cols] = earlier[3 * g + i][:, :HEAD_SIZE]
                ref[:, v_cols] = earlier[3 * g + i][:, HEAD_SIZE:]


def attention(group, cost, first, doc_lengths, query, output_gradient, output, lse, own, near, far, earlier):
    tokens, width = query.shape
    groups = own.shape[1] // (2 * HEAD_SIZE)
    kv_width = own.shape[1] if group == groups - 1 else 2 * HEAD_SIZE
    part = width // groups
    wide = pl.BlockSpec((tokens, part), lambda i: (0, group))
    smem = pl.BlockSpec(memory_space=pltpu.SMEM)
    k_spec = pl.BlockSpec((tokens, HEAD_SIZE), lambda i: (0, group))
    v_spec = pl.BlockSpec((tokens, HEAD_SIZE), lambda i: (0, groups + group))

    def whole(shape):
        return pl.BlockSpec(shape, lambda i: (0, 0))

    return pl.pallas_call(
        functools.partial(attention_kernel, group, groups),
        grid=(1,),
        in_specs=[smem, smem, wide, wide, wide, whole(lse.shape)]
        + [k_spec, v_spec] * 3
        + [whole(array.shape) for array in earlier],
        out_specs=[whole((tokens, part))] + [whole((tokens, kv_width))] * 3,
        out_shape=[
            jax.ShapeDtypeStruct((tokens, part), BF16),
            jax.ShapeDtypeStruct((tokens, kv_width), F32),
            jax.ShapeDtypeStruct((tokens, kv_width), BF16),
            jax.ShapeDtypeStruct((tokens, kv_width), BF16),
        ],
        scratch_shapes=[
            pltpu.VMEM((3, tokens, HEAD_SIZE), F32),
            pltpu.VMEM((3, tokens, HEAD_SIZE), F32),
        ],
        compiler_params=pltpu.CompilerParams(vmem_limit_bytes=VMEM_LIMIT),
        cost_estimate=pl.CostEstimate(flops=cost, transcendentals=0, bytes_accessed=1),
        name="attention",
    )(
        first, doc_lengths, query, output_gradient, output, lse,
        own, own, near, near, far, far, *earlier,
    )


NT = (((1,), (1,)), ((), ()))


def grad_copies(grads, held, sems):
    parts = len(grads) // INNER
    tokens = grads[0].shape[0]
    copies = []
    for t in range(INNER):
        lane = 0
        copies.append([])
        for i, grad in enumerate(grads[t * parts : (t + 1) * parts]):
            width = grad.shape[1]
            copies[-1].append(pltpu.make_async_copy(
                grad,
                held.at[t * tokens : (t + 1) * tokens, lane : lane + width],
                sems.at[t * parts + i],
            ))
            lane += width
    for t in range(2):
        for copy in copies[t]:
            copy.start()

    def ready(t):
        for copy in copies[t]:
            copy.wait()
        if t + 2 < INNER:
            for copy in copies[t + 2]:
                copy.start()

    return ready


def standing(layers):
    layer = lax.axis_index("seq") // INNER
    at_edge = (layer == 0) | (layer == layers - 1)
    return at_edge, lax.axis_index("head") == layer // (layers // 2)


def fetch_either(choice, first, second, weight, sem):
    @pl.when(choice)
    def _():
        pltpu.make_async_copy(first, weight, sem).start()

    @pl.when(jnp.logical_not(choice))
    def _():
        pltpu.make_async_copy(second, weight, sem).start()


def times(grad, weight):
    return lax.dot_general(grad, weight, NT, preferred_element_type=F32)


def send_kernel(layers, count, *refs):
    grads, (own, edge, mid) = refs[:count], refs[count : count + 3]
    send, gathered, held, weight, sems = refs[-5:]
    tokens, cols = grads[0].shape[0], weight.shape[0]
    at_edge, same = standing(layers)

    @pl.when(same)
    def _():
        fetch_either(at_edge, edge, mid, weight, sems.at[count])

    @pl.when(jnp.logical_not(same))
    def _():
        pltpu.make_async_copy(own, weight, sems.at[count]).start()

    ready = grad_copies(grads, held, sems)
    pltpu.make_async_copy(own, weight, sems.at[count]).wait()
    stores = []
    for t in range(INNER):
        ready(t)
        rows = slice(t * tokens, (t + 1) * tokens)
        stores.append(pltpu.make_async_copy(
            held.at[rows], gathered.at[rows], sems.at[count + 1 + t]
        ))
        stores[-1].start()
        lanes = slice(t * cols, (t + 1) * cols)
        send[:, lanes] = times(held[rows, :], weight[...]).astype(BF16)
    for store in stores:
        store.wait()


def keep_kernel(layers, gathered, own, mate, edge, mid, *refs):
    keep, mate_full, mate_low, held, weights, sems = refs[-6:]
    cols = weights.shape[1]
    tokens = held.shape[0] // INNER
    at_edge, same = standing(layers)
    mate_copy = pltpu.make_async_copy(mate, weights.at[1], sems.at[INNER + 1])
    mate_copy.start()
    copies = []
    for t in range(INNER):
        rows = slice(t * tokens, (t + 1) * tokens)
        copies.append(pltpu.make_async_copy(gathered.at[rows], held.at[rows], sems.at[t]))
        copies[-1].start()

    @pl.when(same)
    def _():
        pltpu.make_async_copy(own, weights.at[0], sems.at[INNER]).start()

    @pl.when(jnp.logical_not(same))
    def _():
        fetch_either(at_edge, edge, mid, weights.at[0], sems.at[INNER])

    mate_copy.wait()
    for t in range(INNER):
        copies[t].wait()
        product = times(held[t * tokens : (t + 1) * tokens, :], weights[1])
        mate_full[t] = product
        mate_low[:, t * cols : (t + 1) * cols] = product.astype(BF16)
    pltpu.make_async_copy(own, weights.at[0], sems.at[INNER]).wait()
    for t in range(INNER):
        keep[t] = times(held[t * tokens : (t + 1) * tokens, :], weights[0])


def last_kernel(layers, held, piece, passed, *refs):
    full, low_first, low_second, weight, sem = refs[-5:]
    at_edge, _ = standing(layers)
    fetch_either(at_edge, piece, passed, weight, sem)
    pltpu.make_async_copy(piece, weight, sem).wait()
    tokens, cols = held.shape[0] // INNER, weight.shape[0]
    for t in range(INNER):
        product = times(held[t * tokens : (t + 1) * tokens, :], weight[...])
        full[t] = product
        low = low_first if t % 2 else low_second
        low[:, t // 2 * cols : (t // 2 + 1) * cols] = product.astype(BF16)


def project(kernel, layers, operands, in_vmem, outs, scratch, limit, name):
    vmem = pl.BlockSpec(memory_space=pltpu.VMEM)
    hbm = pl.BlockSpec(memory_space=pltpu.HBM)
    return pl.pallas_call(
        functools.partial(kernel, layers),
        in_specs=[vmem] * in_vmem + [hbm] * (len(operands) - in_vmem),
        out_specs=[vmem if in_place else hbm for in_place, _, _ in outs],
        out_shape=[jax.ShapeDtypeStruct(shape, kind) for _, shape, kind in outs],
        scratch_shapes=scratch,
        compiler_params=pltpu.CompilerParams(vmem_limit_bytes=limit),
        cost_estimate=pl.CostEstimate(flops=1, transcendentals=0, bytes_accessed=1),
        name=name,
    )(*operands)


def project_send(layers, grads, own, edge, mid):
    tokens = grads[0].shape[0]
    cols, depth = own.shape
    return project(
        lambda layers, *refs: send_kernel(layers, len(grads), *refs),
        layers,
        [*grads, own, edge, mid],
        0,
        [(True, (tokens, INNER * cols), BF16), (False, (INNER * tokens, depth), BF16)],
        [
            pltpu.VMEM((INNER * tokens, depth), BF16),
            pltpu.VMEM((cols, depth), BF16),
            pltpu.SemaphoreType.DMA((len(grads) + 1 + INNER,)),
        ],
        VMEM_LIMIT,
        "project_send",
    )


def project_keep(layers, gathered, own, mate, edge, mid, after):
    tokens, depth = gathered.shape[0] // INNER, gathered.shape[1]
    cols = own.shape[0]
    full = (True, (INNER, tokens, cols), F32)
    return project(
        keep_kernel,
        layers,
        [gathered, own, mate, edge, mid, *after],
        0,
        [full, full, (True, (tokens, INNER * cols), BF16)],
        [
            pltpu.VMEM((INNER * tokens, depth), BF16),
            pltpu.VMEM((2, cols, depth), BF16),
            pltpu.SemaphoreType.DMA((INNER + 2,)),
        ],
        VMEM_LIMIT,
        "project_keep",
    )


def project_last(layers, gathered, piece, passed, after):
    tokens, cols = gathered.shape[0] // INNER, piece.shape[0]
    low = (True, (tokens, INNER // 2 * cols), BF16)
    return project(
        last_kernel,
        layers,
        [gathered, piece, passed, *after],
        1,
        [(True, (INNER, tokens, cols), F32), low, low],
        [pltpu.VMEM(piece.shape, BF16), pltpu.SemaphoreType.DMA],
        10 * 2**20,
        "project_last",
    )


def place_kernel(flags, *refs):
    blocks, out = refs[:-1], refs[-1]
    sets = [blocks[k * INNER : (k + 1) * INNER] for k in range(len(blocks) // INNER)]
    width = sets[0][0].shape[1]
    for inner in range(INNER):
        for a_first in range(2):
            @pl.when((flags[0] == inner) & (flags[1] == a_first))
            def _():
                for j in range(INNER):
                    lanes = [(1 - a_first) * INNER * width + j * width]
                    lanes.append(a_first * INNER * width + j * width)
                    for cols in [each[0].shape[1] for each in sets[1:-1]]:
                        lanes.append(lanes[-1] + cols)
                    for lane, each in zip(lanes, sets):
                        block = each[j ^ inner]
                        out[:, lane : lane + block.shape[1]] = block[...]


def place(flags, sets):
    tokens, width = sets[0][0].shape
    blocks = [block for each in sets for block in each]
    vmem = pl.BlockSpec(memory_space=pltpu.VMEM)
    return pl.pallas_call(
        place_kernel,
        in_specs=[pl.BlockSpec(memory_space=pltpu.SMEM)] + [vmem] * len(blocks),
        out_specs=vmem,
        out_shape=jax.ShapeDtypeStruct((tokens, 2 * INNER * width), BF16),
        cost_estimate=pl.CostEstimate(flops=1, transcendentals=0, bytes_accessed=1),
        compiler_params=pltpu.CompilerParams(vmem_limit_bytes=16 * 2**20),
        name="place",
    )(flags, *blocks)


def pack_kernel(*refs):
    sources, out, sems = refs[:-2], refs[-2], refs[-1]
    copies, lane = [], 0
    for source in sources:
        width = source.shape[1]
        copies.append(pltpu.make_async_copy(
            source, out.at[:, lane : lane + width], sems.at[len(copies)]
        ))
        copies[-1].start()
        lane += width
    for copy in copies:
        copy.wait()


def pack(*sources):
    rows = sources[0].shape[0]
    depth = sum(source.shape[1] for source in sources)
    return pl.pallas_call(
        pack_kernel,
        in_specs=[pl.BlockSpec(memory_space=pltpu.HBM)] * len(sources),
        out_specs=pl.BlockSpec(memory_space=pltpu.VMEM),
        out_shape=jax.ShapeDtypeStruct((rows, depth), BF16),
        scratch_shapes=[pltpu.SemaphoreType.DMA((len(sources),))],
        compiler_params=pltpu.CompilerParams(vmem_limit_bytes=VMEM_LIMIT),
        cost_estimate=pl.CostEstimate(flops=1, transcendentals=0, bytes_accessed=1),
        name="pack",
    )(*sources)


def gate_kernel(*refs):
    pass


def gate(array, deps, flops=1):
    hbm = pl.BlockSpec(memory_space=pltpu.HBM)
    return pl.pallas_call(
        gate_kernel,
        in_specs=[hbm] * (1 + len(deps)),
        out_specs=hbm,
        out_shape=jax.ShapeDtypeStruct(array.shape, array.dtype),
        input_output_aliases={0: 0},
        compiler_params=pltpu.CompilerParams(vmem_limit_bytes=VMEM_LIMIT),
        cost_estimate=pl.CostEstimate(flops=flops, transcendentals=0, bytes_accessed=1),
        name="gate",
    )(array, *deps)


def join_kernel(dq, own, near, far, *refs):
    out = refs[-1]
    width = dq.shape[1]
    out[:, :width] = dq[...]
    out[:, width:] = (own[...] + near[...].astype(F32) + far[...].astype(F32)).astype(BF16)


def join(dq, own, near, far, deps):
    tokens, width = dq.shape
    vmem = pl.BlockSpec(memory_space=pltpu.VMEM)
    hbm = pl.BlockSpec(memory_space=pltpu.HBM)
    return pl.pallas_call(
        join_kernel,
        in_specs=[vmem] * 4 + [hbm] * len(deps),
        out_specs=vmem,
        out_shape=jax.ShapeDtypeStruct((tokens, width + own.shape[1]), BF16),
        compiler_params=pltpu.CompilerParams(vmem_limit_bytes=VMEM_LIMIT),
        cost_estimate=pl.CostEstimate(flops=2 * 10**9, transcendentals=0, bytes_accessed=1),
        name="join",
    )(dq, own, near, far, *deps)


def shifted(array, by):
    peers = lax.axis_size("seq")
    pairs = [(i, i + by) for i in range(peers) if 0 <= i + by < peers]
    return lax.ppermute(array, "seq", pairs)


def swapped(array, bits):
    peers = lax.axis_size("seq")
    return lax.ppermute(array, "seq", [(i, i ^ bits) for i in range(peers)])


def layered(array, moves):
    pairs = [(a * INNER + i, b * INNER + i) for a, b in moves for i in range(INNER)]
    return lax.ppermute(array, "seq", pairs)


def crossed(array, layers, inward):
    pairs = []
    for i in range(layers * INNER):
        half = i // INNER // (layers // 2)
        pairs.append((2 * i + 1 - half, 2 * i + half) if inward else (2 * i + half, 2 * i + 1 - half))
    return lax.ppermute(array, ("seq", "head"), pairs)


def returned(blocks):
    return [blocks[0], swapped(blocks[2], 1), swapped(blocks[1], 2), swapped(blocks[3], 3)]


def ordered(blocks, inner):
    cols = []
    for j in range(INNER):
        pick = blocks[j]
        for i in range(1, INNER):
            pick = jnp.where(inner == i, blocks[j ^ i], pick)
        cols.append(pick)
    return jnp.concatenate(cols, 1)


def project_gathered(grads, weight, layers, tokens, head, inner):
    rows = weight.shape[0]
    groups = [[z * INNER + i for z in range(layers)] for i in range(INNER)]
    every = lax.all_gather(weight, "seq", axis=0, tiled=True, axis_index_groups=groups)
    halves = every.reshape(2, layers // 2 * rows, -1)

    def times(piece):
        return lax.dot_general(
            grads, piece, (((1,), (1,)), ((), ())), preferred_element_type=F32
        )

    send = times(jnp.where(head == 0, halves[1], halves[0])).astype(BF16)
    got = lax.ppermute(send, "head", [(0, 1), (1, 0)])
    keep = times(jnp.where(head == 0, halves[0], halves[1]))
    blocks = returned((keep + got.astype(F32)).astype(BF16).reshape(INNER, tokens, -1))
    blocks = [b.reshape(tokens * (layers // 2), rows) for b in blocks]
    return ordered(blocks, inner).reshape(tokens, -1)


def tied(*arrays):
    return lax.optimization_barrier(arrays)


def shards(
    query, key, value, output, output_gradient, lse, doc_lengths, w_query, key_weight, value_weight
):
    tokens = query.shape[0]
    seq = lax.axis_index("seq")
    head = lax.axis_index("head")
    layer, inner = seq // INNER, seq % INNER
    layers = lax.axis_size("seq") // INNER
    half = layer // (layers // 2)
    line = layers == 4

    pair = pack(key, value)
    near = shifted(pair, 1)
    far = shifted(pair, 2)
    rows = w_query.shape[0]
    if line:
        weight = pack(w_query, key_weight, value_weight)
        mate = layered(weight, [(0, 1), (1, 0), (2, 3), (3, 2)])
        mid = layered(weight, [(1, 2), (2, 1)])
        third = layered(mid, [(1, 0), (2, 3)])
        fourth = layered(mate, [(1, 2), (2, 1)])
    else:
        weight = jnp.concatenate([w_query, key_weight, value_weight], 1)
    first = (seq * tokens).astype(jnp.int32).reshape(1)
    groups = key.shape[1] // HEAD_SIZE
    dq, earlier = [], []
    for g in range(groups):
        cost = (4 if g else 24) * 10**9
        dq_part, *parts = attention(
            g, cost, first, doc_lengths, query, output_gradient, output, lse,
            pair, near, far, earlier,
        )
        dq.append(dq_part)
        earlier += parts
    own_part, near_part, far_part = parts
    back_near = shifted(near_part, -1)
    back_far = shifted(far_part, -2)
    dq_y = [swapped(part, 2) for part in dq[:-1]]
    joined = join(dq[-1], own_part, back_near, back_far, [mate, mid, *dq_y] if line else [])
    joined_y = swapped(joined, 2)
    grads = [*dq[:-1], joined, *dq_y, joined_y]
    grads = grads + [swapped(g, 1) for g in grads]

    if not line:
        parts = len(grads) // INNER
        four = jnp.concatenate(
            [jnp.concatenate(grads[t * parts : (t + 1) * parts], 1) for t in range(INNER)], 0
        )
        return project_gathered(four, weight, layers, tokens, head, inner)

    weight = gate(weight, [third, fourth, joined_y])
    last = layered(weight, [(0, 3), (3, 0)])
    same = head == half
    send, held = project_send(layers, grads, weight, third, mid)
    got = lax.ppermute(send, "head", [(0, 1), (1, 0)])
    keep, mate_full, mate_low = project_keep(layers, held, weight, mate, third, mid, [send])
    got_mate = crossed(mate_low, layers, True)
    last_full, low_first, low_second = project_last(layers, held, last, fourth, [got])
    got_first = crossed(low_first, layers, False)
    got_second = crossed(low_second, layers, False)

    def lanes(array, k):
        return array[:, k * rows : (k + 1) * rows].astype(F32)

    sets = [returned([(keep[r] + lanes(got, r)).astype(BF16) for r in range(INNER)])]
    totals = []
    for r in range(INNER):
        got_last = lanes(got_first if r % 2 else got_second, r // 2)
        total = jnp.where(same, mate_full[r] + lanes(got_mate, r), last_full[r] + got_last)
        totals.append(total.astype(BF16))
    sets.append(returned(totals))
    a_first = jnp.where(same, layer % 2 == 0, half == 0)
    return place(jnp.stack([inner, a_first.astype(jnp.int32)]), sets)


def solution(mesh):
    in_specs = (
        P("seq", "head"),
        P("seq", "head"),
        P("seq", "head"),
        P("seq", "head"),
        P("seq", "head"),
        P("head", "seq"),
        P(),
        P("seq", "head"),
        P("seq", "head"),
        P("seq", "head"),
    )
    out_specs = P("seq", "head")
    return jax.shard_map(shards, mesh=mesh, in_specs=in_specs, out_specs=out_specs, check_vma=False)
```

time: 181 us -> 127 us (0.70)
  waiting for transfers between devices: 108 us -> 43.3 us
  Pallas kernels: 22.8 us -> 39.4 us
  starting transfers between devices: 29.5 us -> 38.9 us
  local copies, waits for them, and re-layouts: 12.6 us -> 4 us
  other arithmetic: 7.78 us -> 0.71 us
    ppermute x5, waiting for transfers between devices: 57.3 us -> 5.32 us  [layered(): return lax.ppermute(array, 'seq', pairs)]
    pallas_call x5 -> x10, Pallas kernels: 22.8 us -> 39.4 us  [the longest x3 16.4 us: project(): pl.pallas_call(functools.partial(kernel, layers), in_specs=[vmem] * in_vm...]
    ppermute x8 -> x12, waiting for transfers between devices: 31.3 us -> 22.2 us  [swapped(): return lax.ppermute(array, 'seq', [(i, i ^ bits) for i in range(peers)])]
    ppermute x4, waiting for transfers between devices: 15 us -> 6.92 us  [shifted(): return lax.ppermute(array, 'seq', pairs)]
    unnamed x27 -> x18, local copies, waits for them, and re-layouts: 10.4 us -> 4 us
    ppermute x2 -> x4, starting transfers between devices: 1.25 us -> 7.56 us  [the longest x3 6 us: crossed(): return lax.ppermute(array, ('seq', 'head'), pairs)]
    concatenate x3 -> x0, other arithmetic: 6.25 us -> none  [the longest x1 4.47 us: shards(): four = jnp.concatenate([two, swapped(two, 1)], 0)]
    ppermute x2 -> x4, waiting for transfers between devices: 3.9 us -> 8.81 us  [the longest x3 6.29 us: crossed(): return lax.ppermute(array, ('seq', 'head'), pairs)]
  transfers between devices with their start and end apart: 19 -> 25, of which waited for: 9 -> 12; matrix products, arithmetic and copies ran while one was open for 3% -> 1% of each run, Pallas kernels for 6% -> 28%
where the time goes in v2:
time: 127 us
  waiting for transfers between devices  43.3 us (34%)
  Pallas kernels  39.4 us (31%)
  starting transfers between devices  38.9 us (31%)
  local copies, waits for them, and re-layouts  4 us (3%)
    ppermute x12, waiting for transfers between devices, swapped(): return lax.ppermute(array, 'seq', [(i, i ^ bits) for i in range(peers)])  22.2 us
    pallas_call x3, Pallas kernels, project(): pl.pallas_call(functools.partial(kernel, layers), in_specs=[vmem] * in_vm...  16.4 us
    pallas_call x2, Pallas kernels, attention(): pl.pallas_call(functools.partial(attention_kernel, group, groups), grid=(...  15.1 us
    ppermute x5, starting transfers between devices, layered(): return lax.ppermute(array, 'seq', pairs)  12.6 us
    ppermute x12, starting transfers between devices, swapped(): return lax.ppermute(array, 'seq', [(i, i ^ bits) for i in range(peers)])  9.78 us
    ppermute x4, starting transfers between devices, shifted(): return lax.ppermute(array, 'seq', pairs)  8.93 us
    ppermute x4, waiting for transfers between devices, shifted(): return lax.ppermute(array, 'seq', pairs)  6.92 us
    ppermute x3, waiting for transfers between devices, crossed(): return lax.ppermute(array, ('seq', 'head'), pairs)  6.29 us
  transfers between devices with their start and end apart: 25, of which 12 were waited for; matrix products, arithmetic and copies ran while one was open for 1% of the time, Pallas kernels for 28%

profile of v2, /device:TPU:0, one launch (start us, length us, event | category | flops | bytes accessed | tf_op | source)
XLA Modules:
  0.0 126.6 jit_solution(1771383594879069056)
XLA Ops:
  0.0 1.7 %pack.2.k_own_ref.v_own_ref = bf16[256,512]{1,0:T(8,128)(2,1)} custom-call(bf16[256,256]{1,0:T(8,128)(2,1)} %refs_0_.2, bf16[256,256]{1,0:T(8,128)(2,1)} %refs_1_.2), custom_call_target="tpu_custom_call" | custom-call | flops 1 | bytes 1 | tf_op jit(solution)/shard_map/pack/pallas_call | solution.py:384
  1.7 4.9 %collective-permute-start.1 = (bf16[256,512]{1,0:T(8,128)(2,1)}, bf16[256,512]{1,0:T(8,128)(2,1)S(1)}, u32[]{:S(2)}, u32[]{:S(2)}) collective-permute-start(bf16[256,512]{1,0:T(8,128)(2,1)} %pack.2.k_own_ref.v_own_ref), channel_id=1, source_target_pairs={{0,4},{2,6},{4,8},{6,10},{8,12},{10,14},{12,16},{14,18},{16,20},{1... | collective-permute-start | bytes 786440 | tf_op jit(solution)/shard_map/ppermute | solution.py:439
  6.6 1.5 %collective-permute-start = (bf16[256,512]{1,0:T(8,128)(2,1)}, bf16[256,512]{1,0:T(8,128)(2,1)S(1)}, u32[]{:S(2)}, u32[]{:S(2)}) collective-permute-start(bf16[256,512]{1,0:T(8,128)(2,1)} %pack.2.k_own_ref.v_own_ref), channel_id=1, source_target_pairs={{0,2},{2,4},{4,6},{6,8},{8,10},{10,12},{12,14},{14,16},{16,18},{18... | collective-permute-start | bytes 786440 | tf_op jit(solution)/shard_map/ppermute | solution.py:439
  8.1 2.2 %pack.3.refs_0_ = bf16[224,2304]{1,0:T(8,128)(2,1)} custom-call(bf16[224,1792]{1,0:T(8,128)(2,1)} %refs_0_.3, bf16[224,256]{1,0:T(8,128)(2,1)} %refs_1_.3, bf16[224,256]{1,0:T(8,128)(2,1)} %refs_2_.1), custom_call_target="tpu_custom_call" | custom-call | flops 1 | bytes 1 | tf_op jit(solution)/shard_map/pack/pallas_call | solution.py:384
  10.3 1.7 %collective-permute-start.5 = (bf16[224,2304]{1,0:T(8,128)(2,1)}, bf16[224,2304]{1,0:T(8,128)(2,1)}, u32[]{:S(2)}, u32[]{:S(2)}) collective-permute-start(bf16[224,2304]{1,0:T(8,128)(2,1)} %pack.3.refs_0_), channel_id=1, source_target_pairs={{8,16},{10,18},{12,20},{14,22},{16,8},{18,10},{20,12},{22,14},{9,1... | collective-permute-start | bytes 3096584 | tf_op jit(solution)/shard_map/ppermute | solution.py:449
  11.9 3.9 %collective-permute-start.4 = (bf16[224,2304]{1,0:T(8,128)(2,1)}, bf16[224,2304]{1,0:T(8,128)(2,1)}, u32[]{:S(2)}, u32[]{:S(2)}) collective-permute-start(bf16[224,2304]{1,0:T(8,128)(2,1)} %pack.3.refs_0_), channel_id=1, source_target_pairs={{0,8},{2,10},{4,12},{6,14},{8,0},{10,2},{12,4},{14,6},{16,24},{18,... | collective-permute-start | bytes 3096584 | tf_op jit(solution)/shard_map/ppermute | solution.py:449
  16.6 7.4 %attention.2 = (bf16[256,896]{1,0:T(8,128)(2,1)}, f32[256,256]{1,0:T(8,128)}, bf16[256,256]{1,0:T(8,128)(2,1)}, bf16[256,256]{1,0:T(8,128)(2,1)}) custom-call(s32[1]{0:T(128)} %bitcast.2.first_ref, s32[4]{0:T(128)} %docs_ref.3, bf16[256,1792]{1,0:T(8,128)(2,1)} %q_ref.3, bf16[256,1792]{1,0:T(8,128)(2,1)} %do_ref.3, bf16[256,1792]{1,0:T(8,128)(2,1)} %o_ref.3, ...), custom_call_target="tpu_custom_call" | custom-call | flops 24000000000 | bytes 1 | tf_op jit(solution)/shard_map/attention/pallas_call | solution.py:112
  24.0 1.7 %collective-permute-start.6 = (bf16[256,896]{1,0:T(8,128)(2,1)}, bf16[256,896]{1,0:T(8,128)(2,1)S(1)}, u32[]{:S(2)}, u32[]{:S(2)}) collective-permute-start(bf16[256,896]{1,0:T(8,128)(2,1)} %get-tuple-element.21.refs_0_), channel_id=1, source_target_pairs={{0,4},{2,6},{4,0},{6,2},{8,12},{10,14},{12,8},{14,10},{16,20},{18,... | collective-permute-start | bytes 1376264 | tf_op jit(solution)/shard_map/ppermute | solution.py:444
  25.7 7.8 %attention.3 = (bf16[256,896]{1,0:T(8,128)(2,1)}, f32[256,512]{1,0:T(8,128)}, bf16[256,512]{1,0:T(8,128)(2,1)}, bf16[256,512]{1,0:T(8,128)(2,1)}) custom-call(s32[1]{0:T(128)} %bitcast.2.first_ref, s32[4]{0:T(128)} %docs_ref.3, bf16[256,1792]{1,0:T(8,128)(2,1)} %q_ref.3, bf16[256,1792]{1,0:T(8,128)(2,1)} %do_ref.3, bf16[256,1792]{1,0:T(8,128)(2,1)} %o_ref.3, ...), custom_call_target="tpu_custom_call" | custom-call | flops 4000000000 | bytes 1 | tf_op jit(solution)/shard_map/attention/pallas_call | solution.py:112
  37.3 1.9 %collective-permute-done.4.refs_0_.mate = bf16[224,2304]{1,0:T(8,128)(2,1)} collective-permute-done((bf16[224,2304]{1,0:T(8,128)(2,1)}, bf16[224,2304]{1,0:T(8,128)(2,1)}, u32[]{:S(2)}, u32[]{:S(2)}) %collective-permute-start.4) | collective-permute-done | bytes 1032224 | tf_op jit(solution)/shard_map/ppermute | solution.py:449
  39.2 1.6 %collective-permute-start.13 = (bf16[224,2304]{1,0:T(8,128)(2,1)}, bf16[224,2304]{1,0:T(8,128)(2,1)}, u32[]{:S(2)}, u32[]{:S(2)}) collective-permute-start(bf16[224,2304]{1,0:T(8,128)(2,1)} %collective-permute-done.4.refs_0_.mate), channel_id=1, source_target_pairs={{8,16},{10,18},{12,20},{14,22},{16,8},{18,10},{20,12},{22,14},{9,1... | collective-permute-start | bytes 3096584 | tf_op jit(solution)/shard_map/ppermute | solution.py:449
  40.8 6.9 %collective-permute-done.3.far = bf16[256,512]{1,0:T(8,128)(2,1)S(1)} collective-permute-done((bf16[256,512]{1,0:T(8,128)(2,1)}, bf16[256,512]{1,0:T(8,128)(2,1)S(1)}, u32[]{:S(2)}, u32[]{:S(2)}) %collective-permute-start.3) | collective-permute-done | bytes 262176 | tf_op jit(solution)/shard_map/ppermute | solution.py:439
  48.6 2.3 %join.1.refs_1_ = bf16[256,1408]{1,0:T(8,128)(2,1)} custom-call(bf16[256,896]{1,0:T(8,128)(2,1)} %get-tuple-element.25.dq, f32[256,512]{1,0:T(8,128)} %get-tuple-element.26.own, bf16[256,512]{1,0:T(8,128)(2,1)} %copy-done.7, bf16[256,512]{1,0:T(8,128)(2,1)} %copy-done.8, bf16[224,2304]{1,0:T(8,128)(2,1)} %collective-permute-done.4.refs_0_.mate, ...), custom_call_target="tpu_custom_call" | custom-call | flops 2000000000 | bytes 1 | tf_op jit(solution)/shard_map/join/pallas_call | solution.py:425
  50.9 3.7 %collective-permute-start.7 = (bf16[256,1408]{1,0:T(8,128)(2,1)}, bf16[256,1408]{1,0:T(8,128)(2,1)S(1)}, u32[]{:S(2)}, u32[]{:S(2)}) collective-permute-start(bf16[256,1408]{1,0:T(8,128)(2,1)} %join.1.refs_1_), channel_id=1, source_target_pairs={{0,4},{2,6},{4,0},{6,2},{8,12},{10,14},{12,8},{14,10},{16,20},{18,... | collective-permute-start | bytes 2162696 | tf_op jit(solution)/shard_map/ppermute | solution.py:444
  54.6 13.3 %collective-permute-done.7.refs_3_ = bf16[256,1408]{1,0:T(8,128)(2,1)S(1)} collective-permute-done((bf16[256,1408]{1,0:T(8,128)(2,1)}, bf16[256,1408]{1,0:T(8,128)(2,1)S(1)}, u32[]{:S(2)}, u32[]{:S(2)}) %collective-permute-start.7) | collective-permute-done | bytes 720928 | tf_op jit(solution)/shard_map/ppermute | solution.py:444
  67.9 2.5 %collective-permute-done.12.refs_1_.refs_9_.edge = bf16[224,2304]{1,0:T(8,128)(2,1)} collective-permute-done((bf16[224,2304]{1,0:T(8,128)(2,1)}, bf16[224,2304]{1,0:T(8,128)(2,1)}, u32[]{:S(2)}, u32[]{:S(2)}) %collective-permute-start.12) | collective-permute-done | bytes 1032224 | tf_op jit(solution)/shard_map/ppermute | solution.py:449
  70.4 4.2 %collective-permute-start.19 = (bf16[224,2304]{1,0:T(8,128)(2,1)}, bf16[224,2304]{1,0:T(8,128)(2,1)}, u32[]{:S(2)}, u32[]{:S(2)}) collective-permute-start(bf16[224,2304]{1,0:T(8,128)(2,1)} %gate.1.refs_8_.own), channel_id=1, source_target_pairs={{0,24},{2,26},{4,28},{6,30},{24,0},{26,2},{28,4},{30,6},{1,25},{3,... | collective-permute-start | bytes 3096584 | tf_op jit(solution)/shard_map/ppermute | solution.py:449
  75.1 1.6 %collective-permute-done.8.refs_4_ = bf16[256,896]{1,0:T(8,128)(2,1)} collective-permute-done((bf16[256,896]{1,0:T(8,128)(2,1)}, bf16[256,896]{1,0:T(8,128)(2,1)}, u32[]{:S(2)}, u32[]{:S(2)}) %collective-permute-start.8) | collective-permute-done | bytes 458784 | tf_op jit(solution)/shard_map/ppermute | solution.py:444
  77.4 6.1 %project_send.1 = (bf16[256,896]{1,0:T(8,128)(2,1)}, bf16[1024,2304]{1,0:T(8,128)(2,1)}) custom-call(bf16[256,896]{1,0:T(8,128)(2,1)} %get-tuple-element.21.refs_0_, bf16[256,1408]{1,0:T(8,128)(2,1)} %join.1.refs_1_, bf16[256,896]{1,0:T(8,128)(2,1)} %copy-done.4, bf16[256,1408]{1,0:T(8,128)(2,1)} %copy-done.1, ...), custom_call_target="tpu_custom_call" | custom-call | flops 1 | bytes 1 | tf_op jit(solution)/shard_map/project_send/pallas_call | solution.py:268
  83.5 1.6 %collective-permute-start.14 = (bf16[256,896]{1,0:T(8,128)(2,1)}, bf16[256,896]{1,0:T(8,128)(2,1)S(1)}, u32[]{:S(2)}, u32[]{:S(2)}) collective-permute-start(bf16[256,896]{1,0:T(8,128)(2,1)} %get-tuple-element.30.refs_0_), channel_id=1, source_target_pairs={{0,1},{1,0},{2,3},{3,2},{4,5},{5,4},{6,7},{7,6},{8,9},{9,8},{10,11... | collective-permute-start | bytes 1376264 | tf_op jit(solution)/shard_map/ppermute | solution.py:551
  85.1 7.4 %project_keep.1 = (f32[4,256,224]{2,1,0:T(8,128)}, f32[4,256,224]{2,1,0:T(8,128)}, bf16[256,896]{1,0:T(8,128)(2,1)}) custom-call(bf16[1024,2304]{1,0:T(8,128)(2,1)} %get-tuple-element.29.gathered.held, bf16[224,2304]{1,0:T(8,128)(2,1)} %gate.1.refs_8_.own, bf16[224,2304]{1,0:T(8,128)(2,1)} %collective-permute-done.4.refs_0_.mate, ...), custom_call_target="tpu_custom_call" | custom-call | flops 1 | bytes 1 | tf_op jit(solution)/shard_map/project_keep/pallas_call | solution.py:268
  93.8 2.5 %collective-permute-done.14.refs_0_ = bf16[256,896]{1,0:T(8,128)(2,1)S(1)} collective-permute-done((bf16[256,896]{1,0:T(8,128)(2,1)}, bf16[256,896]{1,0:T(8,128)(2,1)S(1)}, u32[]{:S(2)}, u32[]{:S(2)}) %collective-permute-start.14) | collective-permute-done | bytes 458784 | tf_op jit(solution)/shard_map/ppermute | solution.py:551
  97.3 2.3 %copy-done = bf16[1024,2304]{1,0:T(8,128)(2,1)S(1)} copy-done((bf16[1024,2304]{1,0:T(8,128)(2,1)S(1)}, bf16[1024,2304]{1,0:T(8,128)(2,1)}, u32[]{:S(2)}) %copy-start) | copy-done | bytes 4718616
  99.7 2.9 %project_last.1 = (f32[4,256,224]{2,1,0:T(8,128)S(1)}, bf16[256,448]{1,0:T(8,128)(2,1)S(1)}, bf16[256,448]{1,0:T(8,128)(2,1)S(1)}) custom-call(bf16[1024,2304]{1,0:T(8,128)(2,1)S(1)} %copy-done, bf16[224,2304]{1,0:T(8,128)(2,1)} %collective-permute-done.19.piece, bf16[224,2304]{1,0:T(8,128)(2,1)} %collective-permute-done.13.refs_2_.passed, ...), custom_call_target="tpu_custom_call" | custom-call | flops 1 | bytes 1 | tf_op jit(solution)/shard_map/project_last/pallas_call | solution.py:268
  102.5 3.4 %collective-permute-start.20 = (bf16[256,448]{1,0:T(8,128)(2,1)S(1)}, bf16[256,448]{1,0:T(8,128)(2,1)S(1)}, u32[]{:S(2)}, u32[]{:S(2)}) collective-permute-start(bf16[256,448]{1,0:T(8,128)(2,1)S(1)} %get-tuple-element.35), channel_id=1, source_target_pairs={{0,1},{2,3},{4,5},{6,7},{8,9},{10,11},{12,13},{14,15},{17,16},{19,... | collective-permute-start | bytes 688136 | tf_op jit(solution)/shard_map/ppermute | solution.py:457
  106.0 1.3 %collective-permute-start.22 = (bf16[256,448]{1,0:T(8,128)(2,1)S(1)}, bf16[256,448]{1,0:T(8,128)(2,1)S(1)}, u32[]{:S(2)}, u32[]{:S(2)}) collective-permute-start(bf16[256,448]{1,0:T(8,128)(2,1)S(1)} %get-tuple-element.36), channel_id=1, source_target_pairs={{0,1},{2,3},{4,5},{6,7},{8,9},{10,11},{12,13},{14,15},{17,16},{19,... | collective-permute-start | bytes 688136 | tf_op jit(solution)/shard_map/ppermute | solution.py:457
  109.4 3.3 %collective-permute-done.20 = bf16[256,448]{1,0:T(8,128)(2,1)S(1)} collective-permute-done((bf16[256,448]{1,0:T(8,128)(2,1)S(1)}, bf16[256,448]{1,0:T(8,128)(2,1)S(1)}, u32[]{:S(2)}, u32[]{:S(2)}) %collective-permute-start.20) | collective-permute-done | bytes 229408 | tf_op jit(solution)/shard_map/ppermute | solution.py:457
  112.7 3.0 %collective-permute-done.22 = bf16[256,448]{1,0:T(8,128)(2,1)S(1)} collective-permute-done((bf16[256,448]{1,0:T(8,128)(2,1)S(1)}, bf16[256,448]{1,0:T(8,128)(2,1)S(1)}, u32[]{:S(2)}, u32[]{:S(2)}) %collective-permute-start.22) | collective-permute-done | bytes 229408 | tf_op jit(solution)/shard_map/ppermute | solution.py:457
  116.2 1.6 %collective-permute-start.23 = (bf16[256,224]{1,0:T(8,128)(2,1)S(1)}, bf16[256,224]{1,0:T(8,128)(2,1)S(1)}, u32[]{:S(2)}, u32[]{:S(2)}) collective-permute-start(bf16[256,224]{1,0:T(8,128)(2,1)S(1)} %get-tuple-element.38), channel_id=1, source_target_pairs={{0,4},{2,6},{4,0},{6,2},{8,12},{10,14},{12,8},{14,10},{16,20},{18,... | collective-permute-start | bytes 344072 | tf_op jit(solution)/shard_map/ppermute | solution.py:444
  118.2 3.8 %collective-permute-done.24.refs_7_ = bf16[256,224]{1,0:T(8,128)(2,1)S(1)} collective-permute-done((bf16[256,224]{1,0:T(8,128)(2,1)S(1)}, bf16[256,224]{1,0:T(8,128)(2,1)S(1)}, u32[]{:S(2)}, u32[]{:S(2)}) %collective-permute-start.24) | collective-permute-done | bytes 114720 | tf_op jit(solution)/shard_map/ppermute | solution.py:444
  122.0 2.9 %collective-permute-done.23.refs_6_ = bf16[256,224]{1,0:T(8,128)(2,1)S(1)} collective-permute-done((bf16[256,224]{1,0:T(8,128)(2,1)S(1)}, bf16[256,224]{1,0:T(8,128)(2,1)S(1)}, u32[]{:S(2)}, u32[]{:S(2)}) %collective-permute-start.23) | collective-permute-done | bytes 114720 | tf_op jit(solution)/shard_map/ppermute | solution.py:444
  124.8 1.8 %place.1 = bf16[256,1792]{1,0:T(8,128)(2,1)} custom-call(s32[2]{0:T(128)S(1)} %pad_add_fusion.flags, bf16[256,224]{1,0:T(8,128)(2,1)S(1)} %get-tuple-element.46.refs_0_, bf16[256,224]{1,0:T(8,128)(2,1)S(1)} %collective-permute-done.15.refs_1_, bf16[256,224]{1,0:T(8,128)(2,1)S(1)} %collective-permute-done.16.refs_2_, ...), custom_call_target="tpu_custom_call" | custom-call | flops 1 | bytes 1 | tf_op jit(solution)/shard_map/place/pallas_call | solution.py:356
  (49 shorter events, 12.1 us)
Async XLA Ops:
  1.7 14.1 %collective-permute-start.1 = (bf16[256,512]{1,0:T(8,128)(2,1)}, bf16[256,512]{1,0:T(8,128)(2,1)S(1)}, u32[]{:S(2)}, u32[]{:S(2)}) collective-permute-start(bf16[256,512]{1,0:T(8,128)(2,1)} %pack.2.k_own_ref.v_own_ref), channel_id=1, source_target_pairs={{0,4},{2,6},{4,8},{6,10},{8,12},{10,14},{12,16},{14,18},{16,20},{1... | collective-permute-start | bytes 786440 | tf_op jit(solution)/shard_map/ppermute | solution.py:439
  6.6 9.2 %collective-permute-start = (bf16[256,512]{1,0:T(8,128)(2,1)}, bf16[256,512]{1,0:T(8,128)(2,1)S(1)}, u32[]{:S(2)}, u32[]{:S(2)}) collective-permute-start(bf16[256,512]{1,0:T(8,128)(2,1)} %pack.2.k_own_ref.v_own_ref), channel_id=1, source_target_pairs={{0,2},{2,4},{4,6},{6,8},{8,10},{10,12},{12,14},{14,16},{16,18},{18... | collective-permute-start | bytes 786440 | tf_op jit(solution)/shard_map/ppermute | solution.py:439
  10.3 25.8 %collective-permute-start.5 = (bf16[224,2304]{1,0:T(8,128)(2,1)}, bf16[224,2304]{1,0:T(8,128)(2,1)}, u32[]{:S(2)}, u32[]{:S(2)}) collective-permute-start(bf16[224,2304]{1,0:T(8,128)(2,1)} %pack.3.refs_0_), channel_id=1, source_target_pairs={{8,16},{10,18},{12,20},{14,22},{16,8},{18,10},{20,12},{22,14},{9,1... | collective-permute-start | bytes 3096584 | tf_op jit(solution)/shard_map/ppermute | solution.py:449
  11.9 27.3 %collective-permute-start.4 = (bf16[224,2304]{1,0:T(8,128)(2,1)}, bf16[224,2304]{1,0:T(8,128)(2,1)}, u32[]{:S(2)}, u32[]{:S(2)}) collective-permute-start(bf16[224,2304]{1,0:T(8,128)(2,1)} %pack.3.refs_0_), channel_id=1, source_target_pairs={{0,8},{2,10},{4,12},{6,14},{8,0},{10,2},{12,4},{14,6},{16,24},{18,... | collective-permute-start | bytes 3096584 | tf_op jit(solution)/shard_map/ppermute | solution.py:449
  15.8 0.8 copy-start.6
  24.0 23.7 %collective-permute-start.6 = (bf16[256,896]{1,0:T(8,128)(2,1)}, bf16[256,896]{1,0:T(8,128)(2,1)S(1)}, u32[]{:S(2)}, u32[]{:S(2)}) collective-permute-start(bf16[256,896]{1,0:T(8,128)(2,1)} %get-tuple-element.21.refs_0_), channel_id=1, source_target_pairs={{0,4},{2,6},{4,0},{6,2},{8,12},{10,14},{12,8},{14,10},{16,20},{18,... | collective-permute-start | bytes 1376264 | tf_op jit(solution)/shard_map/ppermute | solution.py:444
  33.4 7.4 %collective-permute-start.2 = (bf16[256,512]{1,0:T(8,128)(2,1)}, bf16[256,512]{1,0:T(8,128)(2,1)S(1)}, u32[]{:S(2)}, u32[]{:S(2)}) collective-permute-start(bf16[256,512]{1,0:T(8,128)(2,1)} %get-tuple-element.27), channel_id=1, source_target_pairs={{2,0},{4,2},{6,4},{8,6},{10,8},{12,10},{14,12},{16,14},{18,16},{20... | collective-permute-start | bytes 786440 | tf_op jit(solution)/shard_map/ppermute | solution.py:439
  34.7 13.0 %collective-permute-start.3 = (bf16[256,512]{1,0:T(8,128)(2,1)}, bf16[256,512]{1,0:T(8,128)(2,1)S(1)}, u32[]{:S(2)}, u32[]{:S(2)}) collective-permute-start(bf16[256,512]{1,0:T(8,128)(2,1)} %get-tuple-element.28), channel_id=1, source_target_pairs={{4,0},{6,2},{8,4},{10,6},{12,8},{14,10},{16,12},{18,14},{20,16},{2... | collective-permute-start | bytes 786440 | tf_op jit(solution)/shard_map/ppermute | solution.py:439
  36.0 34.3 %collective-permute-start.12 = (bf16[224,2304]{1,0:T(8,128)(2,1)}, bf16[224,2304]{1,0:T(8,128)(2,1)}, u32[]{:S(2)}, u32[]{:S(2)}) collective-permute-start(bf16[224,2304]{1,0:T(8,128)(2,1)} %collective-permute-done.5.refs_1_.refs_10_.mid), channel_id=1, source_target_pairs={{8,0},{10,2},{12,4},{14,6},{16,24},{18,26},{20,28},{22,30},{9,1},{... | collective-permute-start | bytes 3096584 | tf_op jit(solution)/shard_map/ppermute | solution.py:449
  39.2 31.2 %collective-permute-start.13 = (bf16[224,2304]{1,0:T(8,128)(2,1)}, bf16[224,2304]{1,0:T(8,128)(2,1)}, u32[]{:S(2)}, u32[]{:S(2)}) collective-permute-start(bf16[224,2304]{1,0:T(8,128)(2,1)} %collective-permute-done.4.refs_0_.mate), channel_id=1, source_target_pairs={{8,16},{10,18},{12,20},{14,22},{16,8},{18,10},{20,12},{22,14},{9,1... | collective-permute-start | bytes 3096584 | tf_op jit(solution)/shard_map/ppermute | solution.py:449
  40.8 6.9 %copy-start.7 = (bf16[256,512]{1,0:T(8,128)(2,1)}, bf16[256,512]{1,0:T(8,128)(2,1)S(1)}, u32[]{:S(2)}) copy-start(bf16[256,512]{1,0:T(8,128)(2,1)S(1)} %collective-permute-done.2.near) | copy-start | bytes 786436
  47.8 0.9 copy-start.4
  50.9 17.0 %collective-permute-start.7 = (bf16[256,1408]{1,0:T(8,128)(2,1)}, bf16[256,1408]{1,0:T(8,128)(2,1)S(1)}, u32[]{:S(2)}, u32[]{:S(2)}) collective-permute-start(bf16[256,1408]{1,0:T(8,128)(2,1)} %join.1.refs_1_), channel_id=1, source_target_pairs={{0,4},{2,6},{4,0},{6,2},{8,12},{10,14},{12,8},{14,10},{16,20},{18,... | collective-permute-start | bytes 2162696 | tf_op jit(solution)/shard_map/ppermute | solution.py:444
  54.6 22.8 %collective-permute-start.9 = (bf16[256,1408]{1,0:T(8,128)(2,1)}, bf16[256,1408]{1,0:T(8,128)(2,1)}, u32[]{:S(2)}, u32[]{:S(2)}) collective-permute-start(bf16[256,1408]{1,0:T(8,128)(2,1)} %join.1.refs_1_), channel_id=1, source_target_pairs={{0,2},{2,0},{4,6},{6,4},{8,10},{10,8},{12,14},{14,12},{16,18},{18,... | collective-permute-start | bytes 2162696 | tf_op jit(solution)/shard_map/ppermute | solution.py:444
  67.9 2.5 %copy-start.1 = (bf16[256,1408]{1,0:T(8,128)(2,1)}, bf16[256,1408]{1,0:T(8,128)(2,1)S(1)}, u32[]{:S(2)}) copy-start(bf16[256,1408]{1,0:T(8,128)(2,1)S(1)} %collective-permute-done.7.refs_3_) | copy-start | bytes 2162692
  67.9 9.5 %collective-permute-start.11 = (bf16[256,1408]{1,0:T(8,128)(2,1)S(1)}, bf16[256,1408]{1,0:T(8,128)(2,1)}, u32[]{:S(2)}, u32[]{:S(2)}) collective-permute-start(bf16[256,1408]{1,0:T(8,128)(2,1)S(1)} %collective-permute-done.7.refs_3_), channel_id=1, source_target_pairs={{0,2},{2,0},{4,6},{6,4},{8,10},{10,8},{12,14},{14,12},{16,18},{18,... | collective-permute-start | bytes 2162696 | tf_op jit(solution)/shard_map/ppermute | solution.py:444
  70.4 27.0 %collective-permute-start.19 = (bf16[224,2304]{1,0:T(8,128)(2,1)}, bf16[224,2304]{1,0:T(8,128)(2,1)}, u32[]{:S(2)}, u32[]{:S(2)}) collective-permute-start(bf16[224,2304]{1,0:T(8,128)(2,1)} %gate.1.refs_8_.own), channel_id=1, source_target_pairs={{0,24},{2,26},{4,28},{6,30},{24,0},{26,2},{28,4},{30,6},{1,25},{3,... | collective-permute-start | bytes 3096584 | tf_op jit(solution)/shard_map/ppermute | solution.py:449
  74.5 2.2 %collective-permute-start.8 = (bf16[256,896]{1,0:T(8,128)(2,1)}, bf16[256,896]{1,0:T(8,128)(2,1)}, u32[]{:S(2)}, u32[]{:S(2)}) collective-permute-start(bf16[256,896]{1,0:T(8,128)(2,1)} %get-tuple-element.21.refs_0_), channel_id=1, source_target_pairs={{0,2},{2,0},{4,6},{6,4},{8,10},{10,8},{12,14},{14,12},{16,18},{18,... | collective-permute-start | bytes 1376264 | tf_op jit(solution)/shard_map/ppermute | solution.py:444
  74.6 2.8 %collective-permute-start.10 = (bf16[256,896]{1,0:T(8,128)(2,1)}, bf16[256,896]{1,0:T(8,128)(2,1)}, u32[]{:S(2)}, u32[]{:S(2)}) collective-permute-start(bf16[256,896]{1,0:T(8,128)(2,1)} %copy-done.4), channel_id=1, source_target_pairs={{0,2},{2,0},{4,6},{6,4},{8,10},{10,8},{12,14},{14,12},{16,18},{18,... | collective-permute-start | bytes 1376264 | tf_op jit(solution)/shard_map/ppermute | solution.py:444
  83.5 12.8 %collective-permute-start.14 = (bf16[256,896]{1,0:T(8,128)(2,1)}, bf16[256,896]{1,0:T(8,128)(2,1)S(1)}, u32[]{:S(2)}, u32[]{:S(2)}) collective-permute-start(bf16[256,896]{1,0:T(8,128)(2,1)} %get-tuple-element.30.refs_0_), channel_id=1, source_target_pairs={{0,1},{1,0},{2,3},{3,2},{4,5},{5,4},{6,7},{7,6},{8,9},{9,8},{10,11... | collective-permute-start | bytes 1376264 | tf_op jit(solution)/shard_map/ppermute | solution.py:551
  92.5 16.4 %collective-permute-start.18 = (bf16[256,896]{1,0:T(8,128)(2,1)}, bf16[256,896]{1,0:T(8,128)(2,1)S(1)}, u32[]{:S(2)}, u32[]{:S(2)}) collective-permute-start(bf16[256,896]{1,0:T(8,128)(2,1)} %get-tuple-element.33), channel_id=1, source_target_pairs={{1,0},{3,2},{5,4},{7,6},{9,8},{11,10},{13,12},{15,14},{16,17},{18,... | collective-permute-start | bytes 1376264 | tf_op jit(solution)/shard_map/ppermute | solution.py:457
  97.3 2.3 %copy-start = (bf16[1024,2304]{1,0:T(8,128)(2,1)S(1)}, bf16[1024,2304]{1,0:T(8,128)(2,1)}, u32[]{:S(2)}) copy-start(bf16[1024,2304]{1,0:T(8,128)(2,1)} %get-tuple-element.29.gathered.held) | copy-start | bytes 14155780
  99.7 7.6 %copy-start.2 = (f32[4,256,224]{2,1,0:T(8,128)S(1)}, f32[4,256,224]{2,1,0:T(8,128)}, u32[]{:S(2)}) copy-start(f32[4,256,224]{2,1,0:T(8,128)} %get-tuple-element.31) | copy-start | bytes 2752516
  99.7 16.0 %copy-start.3 = (f32[4,256,224]{2,1,0:T(8,128)S(1)}, f32[4,256,224]{2,1,0:T(8,128)}, u32[]{:S(2)}) copy-start(f32[4,256,224]{2,1,0:T(8,128)} %get-tuple-element.32) | copy-start | bytes 2752516
  102.5 10.1 %collective-permute-start.20 = (bf16[256,448]{1,0:T(8,128)(2,1)S(1)}, bf16[256,448]{1,0:T(8,128)(2,1)S(1)}, u32[]{:S(2)}, u32[]{:S(2)}) collective-permute-start(bf16[256,448]{1,0:T(8,128)(2,1)S(1)} %get-tuple-element.35), channel_id=1, source_target_pairs={{0,1},{2,3},{4,5},{6,7},{8,9},{10,11},{12,13},{14,15},{17,16},{19,... | collective-permute-start | bytes 688136 | tf_op jit(solution)/shard_map/ppermute | solution.py:457
  106.0 9.8 %collective-permute-start.22 = (bf16[256,448]{1,0:T(8,128)(2,1)S(1)}, bf16[256,448]{1,0:T(8,128)(2,1)S(1)}, u32[]{:S(2)}, u32[]{:S(2)}) collective-permute-start(bf16[256,448]{1,0:T(8,128)(2,1)S(1)} %get-tuple-element.36), channel_id=1, source_target_pairs={{0,1},{2,3},{4,5},{6,7},{8,9},{10,11},{12,13},{14,15},{17,16},{19,... | collective-permute-start | bytes 688136 | tf_op jit(solution)/shard_map/ppermute | solution.py:457
  107.5 10.3 %collective-permute-start.17 = (bf16[256,224]{1,0:T(8,128)(2,1)S(1)}, bf16[256,224]{1,0:T(8,128)(2,1)S(1)}, u32[]{:S(2)}, u32[]{:S(2)}) collective-permute-start(bf16[256,224]{1,0:T(8,128)(2,1)S(1)} %get-tuple-element.43), channel_id=1, source_target_pairs={{0,6},{2,4},{4,2},{6,0},{8,14},{10,12},{12,10},{14,8},{16,22},{18,... | collective-permute-start | bytes 344072 | tf_op jit(solution)/shard_map/ppermute | solution.py:444
  107.6 10.6 %collective-permute-start.16 = (bf16[256,224]{1,0:T(8,128)(2,1)S(1)}, bf16[256,224]{1,0:T(8,128)(2,1)S(1)}, u32[]{:S(2)}, u32[]{:S(2)}) collective-permute-start(bf16[256,224]{1,0:T(8,128)(2,1)S(1)} %get-tuple-element.44), channel_id=1, source_target_pairs={{0,4},{2,6},{4,0},{6,2},{8,12},{10,14},{12,8},{14,10},{16,20},{18,... | collective-permute-start | bytes 344072 | tf_op jit(solution)/shard_map/ppermute | solution.py:444
  108.8 9.3 %collective-permute-start.15 = (bf16[256,224]{1,0:T(8,128)(2,1)S(1)}, bf16[256,224]{1,0:T(8,128)(2,1)S(1)}, u32[]{:S(2)}, u32[]{:S(2)}) collective-permute-start(bf16[256,224]{1,0:T(8,128)(2,1)S(1)} %get-tuple-element.45), channel_id=1, source_target_pairs={{0,2},{2,0},{4,6},{6,4},{8,10},{10,8},{12,14},{14,12},{16,18},{18,... | collective-permute-start | bytes 344072 | tf_op jit(solution)/shard_map/ppermute | solution.py:444
  116.1 5.8 %collective-permute-start.24 = (bf16[256,224]{1,0:T(8,128)(2,1)S(1)}, bf16[256,224]{1,0:T(8,128)(2,1)S(1)}, u32[]{:S(2)}, u32[]{:S(2)}) collective-permute-start(bf16[256,224]{1,0:T(8,128)(2,1)S(1)} %get-tuple-element.37), channel_id=1, source_target_pairs={{0,6},{2,4},{4,2},{6,0},{8,14},{10,12},{12,10},{14,8},{16,22},{18,... | collective-permute-start | bytes 344072 | tf_op jit(solution)/shard_map/ppermute | solution.py:444
  116.2 8.6 %collective-permute-start.23 = (bf16[256,224]{1,0:T(8,128)(2,1)S(1)}, bf16[256,224]{1,0:T(8,128)(2,1)S(1)}, u32[]{:S(2)}, u32[]{:S(2)}) collective-permute-start(bf16[256,224]{1,0:T(8,128)(2,1)S(1)} %get-tuple-element.38), channel_id=1, source_target_pairs={{0,4},{2,6},{4,0},{6,2},{8,12},{10,14},{12,8},{14,10},{16,20},{18,... | collective-permute-start | bytes 344072 | tf_op jit(solution)/shard_map/ppermute | solution.py:444
  117.8 7.0 %collective-permute-start.21 = (bf16[256,224]{1,0:T(8,128)(2,1)S(1)}, bf16[256,224]{1,0:T(8,128)(2,1)S(1)}, u32[]{:S(2)}, u32[]{:S(2)}) collective-permute-start(bf16[256,224]{1,0:T(8,128)(2,1)S(1)} %get-tuple-element.42), channel_id=1, source_target_pairs={{0,2},{2,0},{4,6},{6,4},{8,10},{10,8},{12,14},{14,12},{16,18},{18,... | collective-permute-start | bytes 344072 | tf_op jit(solution)/shard_map/ppermute | solution.py:444
  (2 other events, 1.4 us)

commit v3 on v2

--- a/solution.py
+++ b/solution.py
@@ -13,6 +13,7 @@
 INNER = 4
 LOG2E = 1.4426950408889634
 VMEM_LIMIT = 63 * 2**20
+JOIN_LIMIT = 63 * 2**20
 F32 = jnp.float32
 BF16 = jnp.bfloat16
 
@@ -22,13 +23,14 @@
     k_own_ref, v_own_ref, k_near_ref, v_near_ref, k_far_ref, v_far_ref,
     *refs,
 ):
-    *earlier, dq_ref, own_ref, near_ref, far_ref, acc_k, acc_v = refs
+    *earlier, dq_ref, own_ref, near_ref, far_ref, probs, dscores, do_rows, q_rows = refs
     tokens = k_own_ref.shape[0]
     per_group = q_ref.shape[1] // HEAD_SIZE
     scale = 1.0 / math.sqrt(HEAD_SIZE)
     rows = lax.broadcasted_iota(jnp.int32, (tokens, tokens), 0)
     cols = lax.broadcasted_iota(jnp.int32, (tokens, tokens), 1)
     causal = rows <= cols
+    keep_own = jnp.where(causal, 1.0, 0.0).astype(BF16)
     first = first_ref[0]
     spot = first + lax.broadcasted_iota(jnp.int32, (8, tokens), 1)
     start = jnp.int32(0)
@@ -47,50 +49,65 @@
     def dot(a, b, dims=(((1,), (0,)), ((), ()))):
         return lax.dot_general(a, b, dims, preferred_element_type=F32)
 
-    k_own, k_near, k_far = k_own_ref[...], k_near_ref[...], k_far_ref[...]
-    v_own, v_near, v_far = v_own_ref[...], v_near_ref[...], v_far_ref[...]
+    keys = jnp.concatenate([k_own_ref[...], k_near_ref[...], k_far_ref[...]], 0)
+    values = jnp.concatenate([v_own_ref[...], v_near_ref[...], v_far_ref[...]], 0)
+    keys_t = keys.T
+    own, near, far = slice(0, tokens), slice(tokens, 2 * tokens), slice(2 * tokens, 3 * tokens)
+    def finish(j):
+        span = slice(j * HEAD_SIZE, (j + 1) * HEAD_SIZE)
+        turn = slice(j * tokens, (j + 1) * tokens)
+        dq_ref[:, span] = dot(keys_t, dscores[:, turn]).T.astype(BF16)
+        if j % 2:
+            two = slice((j - 1) * tokens, (j + 1) * tokens)
+        elif j == per_group - 1:
+            two = turn
+        else:
+            return
+        sums.append((dot(probs[:, two], do_rows[two, :]), dot(dscores[:, two], q_rows[two, :])))
+
+    sums = []
     for j in range(per_group):
         span = slice(j * HEAD_SIZE, (j + 1) * HEAD_SIZE)
+        turn = slice(j * tokens, (j + 1) * tokens)
         q, do, o = q_ref[:, span], do_ref[:, span], o_ref[:, span]
+        q_rows[turn, :] = q
+        do_rows[turn, :] = do
         head = group * per_group + j
         lse2 = lse_ref[head : head + 1, :] * LOG2E
         delta = jnp.sum((do.astype(F32) * o.astype(F32)).T, axis=0, keepdims=True)
-
-        def prob(scores, bias):
-            return jnp.exp2(scores * (scale * LOG2E) - lse2 + bias)
-
-        p_mix = prob(jnp.where(causal, dot(k_own, q, nt), dot(k_far, q, nt)), bias_mix)
-        p_near = prob(dot(k_near, q, nt), bias_near)
-        g_mix = jnp.where(causal, dot(v_own, do, nt), dot(v_far, do, nt))
-        g_near = dot(v_near, do, nt)
-        ds_mix = p_mix * (g_mix - delta) * scale
-        ds_near = (p_near * (g_near - delta) * scale).astype(BF16)
-        zero = jnp.zeros_like(p_mix)
-        ds_own = jnp.where(causal, ds_mix, zero).astype(BF16)
-        ds_far = jnp.where(causal, zero, ds_mix).astype(BF16)
-        p_own = jnp.where(causal, p_mix, zero).astype(BF16)
-        p_far = jnp.where(causal, zero, p_mix).astype(BF16)
-        p_near = p_near.astype(BF16)
-        dq = dot(ds_own, k_own, tn) + dot(ds_near, k_near, tn) + dot(ds_far, k_far, tn)
-        dq_ref[:, span] = dq.astype(BF16)
-        for i, (p, ds) in enumerate(((p_own, ds_own), (p_near, ds_near), (p_far, ds_far))):
-            dv, dk = dot(p, do), dot(ds, q)
-            if j == 0:
-                acc_v[i], acc_k[i] = dv, dk
-            else:
-                acc_v[i] += dv
-                acc_k[i] += dk
+        scores, grads = dot(keys, q, nt), dot(values, do, nt)
+
+        if j:
+            finish(j - 1)
+
+        def both(score, grad, bias):
+            prob = jnp.exp2(score * (scale * LOG2E) - lse2 + bias)
+            return prob.astype(BF16), (prob * (grad - delta) * scale).astype(BF16)
+
+        p_mix, ds_mix = both(
+            jnp.where(causal, scores[own], scores[far]),
+            jnp.where(causal, grads[own], grads[far]),
+            bias_mix,
+        )
+        p_near, ds_near = both(scores[near], grads[near], bias_near)
+        p_own, ds_own = p_mix * keep_own, ds_mix * keep_own
+        probs[own, turn], probs[near, turn], probs[far, turn] = p_own, p_near, p_mix - p_own
+        dscores[own, turn], dscores[near, turn], dscores[far, turn] = ds_own, ds_near, ds_mix - ds_own
+    finish(per_group - 1)
+    acc_v = functools.reduce(lambda a, b: a + b, [each[0] for each in sums])
+    acc_k = functools.reduce(lambda a, b: a + b, [each[1] for each in sums])
     for i, ref in enumerate((own_ref, near_ref, far_ref)):
+        part = slice(i * tokens, (i + 1) * tokens)
         if group < groups - 1:
-            ref[:, :HEAD_SIZE] = acc_k[i].astype(ref.dtype)
-            ref[:, HEAD_SIZE:] = acc_v[i].astype(ref.dtype)
+            ref[:, :HEAD_SIZE] = acc_k[part].astype(ref.dtype)
+            ref[:, HEAD_SIZE:] = acc_v[part].astype(ref.dtype)
             continue
         for g in range(groups):
             k_cols = slice(g * HEAD_SIZE, (g + 1) * HEAD_SIZE)
             v_cols = slice((groups + g) * HEAD_SIZE, (groups + g + 1) * HEAD_SIZE)
             if g == group:
-                ref[:, k_cols] = acc_k[i].astype(ref.dtype)
-                ref[:, v_cols] = acc_v[i].astype(ref.dtype)
+                ref[:, k_cols] = acc_k[part].astype(ref.dtype)
+                ref[:, v_cols] = acc_v[part].astype(ref.dtype)
             else:
                 ref[:, k_cols] = earlier[3 * g + i][:, :HEAD_SIZE]
                 ref[:, v_cols] = earlier[3 * g + i][:, HEAD_SIZE:]
@@ -102,6 +119,7 @@
     kv_width = own.shape[1] if group == groups - 1 else 2 * HEAD_SIZE
     part = width // groups
     wide = pl.BlockSpec((tokens, part), lambda i: (0, group))
+    per_group = part // HEAD_SIZE
     smem = pl.BlockSpec(memory_space=pltpu.SMEM)
     k_spec = pl.BlockSpec((tokens, HEAD_SIZE), lambda i: (0, group))
     v_spec = pl.BlockSpec((tokens, HEAD_SIZE), lambda i: (0, groups + group))
@@ -123,8 +141,10 @@
             jax.ShapeDtypeStruct((tokens, kv_width), BF16),
         ],
         scratch_shapes=[
-            pltpu.VMEM((3, tokens, HEAD_SIZE), F32),
-            pltpu.VMEM((3, tokens, HEAD_SIZE), F32),
+            pltpu.VMEM((3 * tokens, per_group * tokens), BF16),
+            pltpu.VMEM((3 * tokens, per_group * tokens), BF16),
+            pltpu.VMEM((per_group * tokens, HEAD_SIZE), BF16),
+            pltpu.VMEM((per_group * tokens, HEAD_SIZE), BF16),
         ],
         compiler_params=pltpu.CompilerParams(vmem_limit_bytes=VMEM_LIMIT),
         cost_estimate=pl.CostEstimate(flops=cost, transcendentals=0, bytes_accessed=1),
@@ -217,49 +237,44 @@
         store.wait()
 
 
-def keep_kernel(layers, gathered, own, mate, edge, mid, *refs):
-    keep, mate_full, mate_low, held, weights, sems = refs[-6:]
+def keep_kernel(layers, held, own, mate, edge, mid, *refs):
+    keep, mate_full, mate_low, weights, sems = refs[-5:]
     cols = weights.shape[1]
     tokens = held.shape[0] // INNER
     at_edge, same = standing(layers)
-    mate_copy = pltpu.make_async_copy(mate, weights.at[1], sems.at[INNER + 1])
+    mate_copy = pltpu.make_async_copy(mate, weights.at[1], sems.at[1])
     mate_copy.start()
-    copies = []
-    for t in range(INNER):
-        rows = slice(t * tokens, (t + 1) * tokens)
-        copies.append(pltpu.make_async_copy(gathered.at[rows], held.at[rows], sems.at[t]))
-        copies[-1].start()
 
     @pl.when(same)
     def _():
-        pltpu.make_async_copy(own, weights.at[0], sems.at[INNER]).start()
+        pltpu.make_async_copy(own, weights.at[0], sems.at[0]).start()
 
     @pl.when(jnp.logical_not(same))
     def _():
-        fetch_either(at_edge, edge, mid, weights.at[0], sems.at[INNER])
+        fetch_either(at_edge, edge, mid, weights.at[0], sems.at[0])
 
     mate_copy.wait()
     for t in range(INNER):
-        copies[t].wait()
         product = times(held[t * tokens : (t + 1) * tokens, :], weights[1])
         mate_full[t] = product
         mate_low[:, t * cols : (t + 1) * cols] = product.astype(BF16)
-    pltpu.make_async_copy(own, weights.at[0], sems.at[INNER]).wait()
+    pltpu.make_async_copy(own, weights.at[0], sems.at[0]).wait()
     for t in range(INNER):
         keep[t] = times(held[t * tokens : (t + 1) * tokens, :], weights[0])
 
 
-def last_kernel(layers, held, piece, passed, *refs):
-    full, low_first, low_second, weight, sem = refs[-5:]
+def last_kernel(parts, layers, held, piece, passed, *refs):
+    outs, weight, sem = refs[-2 - 2 * len(parts) : -2], refs[-2], refs[-1]
     at_edge, _ = standing(layers)
     fetch_either(at_edge, piece, passed, weight, sem)
     pltpu.make_async_copy(piece, weight, sem).wait()
     tokens, cols = held.shape[0] // INNER, weight.shape[0]
-    for t in range(INNER):
-        product = times(held[t * tokens : (t + 1) * tokens, :], weight[...])
-        full[t] = product
-        low = low_first if t % 2 else low_second
-        low[:, t // 2 * cols : (t // 2 + 1) * cols] = product.astype(BF16)
+    for i, picks in enumerate(parts):
+        full, low = outs[2 * i : 2 * i + 2]
+        for k, t in enumerate(picks):
+            product = times(held[t * tokens : (t + 1) * tokens, :], weight[...])
+            full[k] = product
+            low[:, k * cols : (k + 1) * cols] = product.astype(BF16)
 
 
 def project(kernel, layers, operands, in_vmem, outs, scratch, limit, name):
@@ -304,88 +319,124 @@
         keep_kernel,
         layers,
         [gathered, own, mate, edge, mid, *after],
-        0,
+        1,
         [full, full, (True, (tokens, INNER * cols), BF16)],
-        [
-            pltpu.VMEM((INNER * tokens, depth), BF16),
-            pltpu.VMEM((2, cols, depth), BF16),
-            pltpu.SemaphoreType.DMA((INNER + 2,)),
-        ],
-        VMEM_LIMIT,
+        [pltpu.VMEM((2, cols, depth), BF16), pltpu.SemaphoreType.DMA((2,))],
+        59 * 2**20,
         "project_keep",
     )
 
 
-def project_last(layers, gathered, piece, passed, after):
+def project_last(parts, layers, gathered, piece, passed, after):
     tokens, cols = gathered.shape[0] // INNER, piece.shape[0]
-    low = (True, (tokens, INNER // 2 * cols), BF16)
+    outs = []
+    for picks in parts:
+        outs.append((True, (len(picks), tokens, cols), F32))
+        outs.append((True, (tokens, len(picks) * cols), BF16))
     return project(
-        last_kernel,
+        functools.partial(last_kernel, parts),
         layers,
         [gathered, piece, passed, *after],
         1,
-        [(True, (INNER, tokens, cols), F32), low, low],
+        outs,
         [pltpu.VMEM(piece.shape, BF16), pltpu.SemaphoreType.DMA],
         10 * 2**20,
         "project_last",
     )
 
 
-def place_kernel(flags, *refs):
-    blocks, out = refs[:-1], refs[-1]
-    sets = [blocks[k * INNER : (k + 1) * INNER] for k in range(len(blocks) // INNER)]
-    width = sets[0][0].shape[1]
-    for inner in range(INNER):
-        for a_first in range(2):
-            @pl.when((flags[0] == inner) & (flags[1] == a_first))
-            def _():
-                for j in range(INNER):
-                    lanes = [(1 - a_first) * INNER * width + j * width]
-                    lanes.append(a_first * INNER * width + j * width)
-                    for cols in [each[0].shape[1] for each in sets[1:-1]]:
-                        lanes.append(lanes[-1] + cols)
-                    for lane, each in zip(lanes, sets):
-                        block = each[j ^ inner]
-                        out[:, lane : lane + block.shape[1]] = block[...]
-
-
-def place(flags, sets):
-    tokens, width = sets[0][0].shape
-    blocks = [block for each in sets for block in each]
+def combine_kernel(layers, picks, last_full, mate_full, got_mate, got_last, *refs):
+    outs = refs[-len(picks) :]
+    _, same = standing(layers)
+    cols = last_full.shape[2]
+    for k, r in enumerate(picks):
+        @pl.when(same)
+        def _():
+            got = got_mate[:, r * cols : (r + 1) * cols].astype(F32)
+            outs[k][...] = (mate_full[r] + got).astype(BF16)
+
+        @pl.when(jnp.logical_not(same))
+        def _():
+            got = got_last[:, k * cols : (k + 1) * cols].astype(F32)
+            outs[k][...] = (last_full[k] + got).astype(BF16)
+
+
+def combine(layers, picks, last_full, mate_full, got_mate, got_last, after):
+    _, tokens, cols = last_full.shape
     vmem = pl.BlockSpec(memory_space=pltpu.VMEM)
     return pl.pallas_call(
-        place_kernel,
-        in_specs=[pl.BlockSpec(memory_space=pltpu.SMEM)] + [vmem] * len(blocks),
+        functools.partial(combine_kernel, layers, picks),
+        in_specs=[vmem] * 4 + [pl.BlockSpec(memory_space=pltpu.HBM)] * len(after),
+        out_specs=[vmem] * len(picks),
+        out_shape=[jax.ShapeDtypeStruct((tokens, cols), BF16)] * len(picks),
+        compiler_params=pltpu.CompilerParams(vmem_limit_bytes=12 * 2**20),
+        cost_estimate=pl.CostEstimate(flops=1, transcendentals=0, bytes_accessed=1),
+        name="combine",
+    )(last_full, mate_full, got_mate, got_last, *after)
+
+
+def place_kernel(layers, tasks, *refs):
+    out = refs[-1]
+    width = refs[0].shape[1]
+    if len(refs) > len(tasks) + 1:
+        out[...] = refs[-2][...]
+    seq = lax.axis_index("seq")
+    layer, inner = seq // INNER, seq % INNER
+    _, same = standing(layers)
+    lower = layer // (layers // 2) == 0
+    first_low = jnp.where(same, layer % 2 == 0, lower)
+    for i in range(INNER):
+        for low in (True, False):
+            @pl.when((inner == i) & (first_low == low))
+            def _():
+                for block, (which, r) in zip(refs, tasks):
+                    lane = ((which == 0) != low) * INNER * width + (r ^ i) * width
+                    out[:, lane : lane + width] = block[...]
+
+
+def place(layers, tasks, blocks, earlier, cost):
+    tokens, width = blocks[0].shape
+    vmem = pl.BlockSpec(memory_space=pltpu.VMEM)
+    return pl.pallas_call(
+        functools.partial(place_kernel, layers, tasks),
+        in_specs=[vmem] * (len(blocks) + len(earlier)),
         out_specs=vmem,
         out_shape=jax.ShapeDtypeStruct((tokens, 2 * INNER * width), BF16),
-        cost_estimate=pl.CostEstimate(flops=1, transcendentals=0, bytes_accessed=1),
+        cost_estimate=pl.CostEstimate(flops=cost, transcendentals=0, bytes_accessed=1),
         compiler_params=pltpu.CompilerParams(vmem_limit_bytes=16 * 2**20),
         name="place",
-    )(flags, *blocks)
-
-
-def pack_kernel(*refs):
-    sources, out, sems = refs[:-2], refs[-2], refs[-1]
-    copies, lane = [], 0
-    for source in sources:
-        width = source.shape[1]
-        copies.append(pltpu.make_async_copy(
-            source, out.at[:, lane : lane + width], sems.at[len(copies)]
-        ))
-        copies[-1].start()
-        lane += width
+    )(*blocks, *earlier)
+
+
+def pack_kernel(splits, *refs):
+    outs, sems = refs[-1 - len(splits) : -1], refs[-1]
+    copies = []
+    for out, (lo, hi) in zip(outs, splits):
+        lane = 0
+        for source in refs[lo:hi]:
+            width = source.shape[1]
+            copies.append(pltpu.make_async_copy(
+                source, out.at[:, lane : lane + width], sems.at[len(copies)]
+            ))
+            copies[-1].start()
+            lane += width
     for copy in copies:
         copy.wait()
 
 
-def pack(*sources):
-    rows = sources[0].shape[0]
-    depth = sum(source.shape[1] for source in sources)
+def pack(*groups):
+    sources, splits = [], []
+    for group in groups:
+        splits.append((len(sources), len(sources) + len(group)))
+        sources += group
     return pl.pallas_call(
-        pack_kernel,
+        functools.partial(pack_kernel, splits),
         in_specs=[pl.BlockSpec(memory_space=pltpu.HBM)] * len(sources),
-        out_specs=pl.BlockSpec(memory_space=pltpu.VMEM),
-        out_shape=jax.ShapeDtypeStruct((rows, depth), BF16),
+        out_specs=[pl.BlockSpec(memory_space=pltpu.VMEM)] * len(groups),
+        out_shape=[
+            jax.ShapeDtypeStruct((g[0].shape[0], sum(each.shape[1] for each in g)), BF16)
+            for g in groups
+        ],
         scratch_shapes=[pltpu.SemaphoreType.DMA((len(sources),))],
         compiler_params=pltpu.CompilerParams(vmem_limit_bytes=VMEM_LIMIT),
         cost_estimate=pl.CostEstimate(flops=1, transcendentals=0, bytes_accessed=1),
@@ -427,7 +478,7 @@
         in_specs=[vmem] * 4 + [hbm] * len(deps),
         out_specs=vmem,
         out_shape=jax.ShapeDtypeStruct((tokens, width + own.shape[1]), BF16),
-        compiler_params=pltpu.CompilerParams(vmem_limit_bytes=VMEM_LIMIT),
+        compiler_params=pltpu.CompilerParams(vmem_limit_bytes=JOIN_LIMIT),
         cost_estimate=pl.CostEstimate(flops=2 * 10**9, transcendentals=0, bytes_accessed=1),
         name="join",
     )(dq, own, near, far, *deps)
@@ -500,42 +551,44 @@
     tokens = query.shape[0]
     seq = lax.axis_index("seq")
     head = lax.axis_index("head")
-    layer, inner = seq // INNER, seq % INNER
+    inner = seq % INNER
     layers = lax.axis_size("seq") // INNER
-    half = layer // (layers // 2)
     line = layers == 4
 
-    pair = pack(key, value)
+    rows = w_query.shape[0]
+    if line:
+        pair, weight = pack((key, value), (w_query, key_weight, value_weight))
+    else:
+        pair = jnp.concatenate([key, value], 1)
+        weight = jnp.concatenate([w_query, key_weight, value_weight], 1)
+    pair_width = pair.shape[1]
     near = shifted(pair, 1)
     far = shifted(pair, 2)
-    rows = w_query.shape[0]
     if line:
-        weight = pack(w_query, key_weight, value_weight)
         mate = layered(weight, [(0, 1), (1, 0), (2, 3), (3, 2)])
         mid = layered(weight, [(1, 2), (2, 1)])
         third = layered(mid, [(1, 0), (2, 3)])
         fourth = layered(mate, [(1, 2), (2, 1)])
-    else:
-        weight = jnp.concatenate([w_query, key_weight, value_weight], 1)
     first = (seq * tokens).astype(jnp.int32).reshape(1)
     groups = key.shape[1] // HEAD_SIZE
     dq, earlier = [], []
     for g in range(groups):
-        cost = (4 if g else 24) * 10**9
         dq_part, *parts = attention(
-            g, cost, first, doc_lengths, query, output_gradient, output, lse,
+            g, (4 if g else 24) * 10**9, first, doc_lengths, query, output_gradient, output, lse,
             pair, near, far, earlier,
         )
         dq.append(dq_part)
         earlier += parts
     own_part, near_part, far_part = parts
+    dq_y = [swapped(part, 2) for part in dq[:-1]]
     back_near = shifted(near_part, -1)
     back_far = shifted(far_part, -2)
-    dq_y = [swapped(part, 2) for part in dq[:-1]]
-    joined = join(dq[-1], own_part, back_near, back_far, [mate, mid, *dq_y] if line else [])
+    deps = [mate, mid, *dq_y] if line else []
+    joined = join(dq[-1], own_part, back_near, back_far, deps)
     joined_y = swapped(joined, 2)
     grads = [*dq[:-1], joined, *dq_y, joined_y]
-    grads = grads + [swapped(g, 1) for g in grads]
+    others = [swapped(g, 1) for g in grads]
+    grads = grads + others
 
     if not line:
         parts = len(grads) // INNER
@@ -544,29 +597,34 @@
         )
         return project_gathered(four, weight, layers, tokens, head, inner)
 
-    weight = gate(weight, [third, fourth, joined_y])
+    early = [o for o, g in zip(others, grads) if g is not joined and g is not joined_y]
+    weight = gate(weight, [third, fourth, joined_y, *early])
     last = layered(weight, [(0, 3), (3, 0)])
-    same = head == half
     send, held = project_send(layers, grads, weight, third, mid)
     got = lax.ppermute(send, "head", [(0, 1), (1, 0)])
     keep, mate_full, mate_low = project_keep(layers, held, weight, mate, third, mid, [send])
     got_mate = crossed(mate_low, layers, True)
-    last_full, low_first, low_second = project_last(layers, held, last, fourth, [got])
-    got_first = crossed(low_first, layers, False)
-    got_second = crossed(low_second, layers, False)
+    parts = ((1, 3), (0, 2))
+    outs = project_last(parts, layers, held, last, fourth, [got])
+    halves = [
+        (picks, outs[2 * i], crossed(outs[2 * i + 1], layers, False))
+        for i, picks in enumerate(parts)
+    ]
 
     def lanes(array, k):
         return array[:, k * rows : (k + 1) * rows].astype(F32)
 
     sets = [returned([(keep[r] + lanes(got, r)).astype(BF16) for r in range(INNER)])]
-    totals = []
-    for r in range(INNER):
-        got_last = lanes(got_first if r % 2 else got_second, r // 2)
-        total = jnp.where(same, mate_full[r] + lanes(got_mate, r), last_full[r] + got_last)
-        totals.append(total.astype(BF16))
-    sets.append(returned(totals))
-    a_first = jnp.where(same, layer % 2 == 0, half == 0)
-    return place(jnp.stack([inner, a_first.astype(jnp.int32)]), sets)
+    blocks, after = [None] * INNER, sets[0][1:]
+    for picks, full, got_last in halves:
+        after = combine(layers, picks, full, mate_full, got_mate, got_last, after)
+        for r, block in zip(picks, after):
+            blocks[r] = block
+    sets.append(returned(blocks))
+    tasks = [*((0, r) for r in range(INNER)), (1, 2), (1, 3), (1, 0), (1, 1)]
+    blocks = [sets[which][r] for which, r in tasks]
+    partly = place(layers, tasks[:-2], blocks[:-2], [], 4 * 10**9)
+    return place(layers, tasks[-2:], blocks[-2:], [partly], 1)
 
 
 def solution(mesh):

time: 127 us -> 120 us (0.945)
  starting transfers between devices: 38.9 us -> 44.6 us
  waiting for transfers between devices: 43.3 us -> 38 us
  Pallas kernels: 39.4 us -> 35 us
  local copies, waits for them, and re-layouts: 4 us -> 1.67 us
    ppermute x3, waiting for transfers between devices: 6.29 us -> 0.01 us  [crossed(): return lax.ppermute(array, ('seq', 'head'), pairs)]
    ppermute x12, starting transfers between devices: 9.78 us -> 15.1 us  [swapped(): return lax.ppermute(array, 'seq', [(i, i ^ bits) for i in range(peers)])]
    ppermute x5, waiting for transfers between devices: 5.32 us -> 10.6 us  [layered(): return lax.ppermute(array, 'seq', pairs)]
    pallas_call x2, Pallas kernels: 15.1 us -> 12.1 us  [attention(): pl.pallas_call(functools.partial(attention_kernel, group, groups), grid=(...]
    ppermute x4, waiting for transfers between devices: 6.92 us -> 4.53 us  [shifted(): return lax.ppermute(array, 'seq', pairs)]
    unnamed x18 -> x22, local copies, waits for them, and re-layouts: 4 us -> 1.67 us
    pallas_call x3 -> x5, Pallas kernels: 5.66 us -> 4.22 us  [the longest x1 2.43 us: pack(): pl.pallas_call(functools.partial(pack_kernel, splits), in_specs=[pl.Block...]
  transfers between devices with their start and end apart: 25 -> 25, of which waited for: 12 -> 11; matrix products, arithmetic and copies ran while one was open for 1% -> 0% of each run, Pallas kernels for 28% -> 26%
where the time goes in v3:
time: 120 us
  starting transfers between devices  44.6 us (37%)
  waiting for transfers between devices  38 us (32%)
  Pallas kernels  35 us (29%)
  local copies, waits for them, and re-layouts  1.67 us (1%)
    ppermute x12, waiting for transfers between devices, swapped(): return lax.ppermute(array, 'seq', [(i, i ^ bits) for i in range(peers)])  21.5 us
    pallas_call x3, Pallas kernels, project(): pl.pallas_call(functools.partial(kernel, layers), in_specs=[vmem] * in_vm...  16.4 us
    ppermute x12, starting transfers between devices, swapped(): return lax.ppermute(array, 'seq', [(i, i ^ bits) for i in range(peers)])  15.1 us
    ppermute x5, starting transfers between devices, layered(): return lax.ppermute(array, 'seq', pairs)  12.6 us
    pallas_call x2, Pallas kernels, attention(): pl.pallas_call(functools.partial(attention_kernel, group, groups), grid=(...  12.1 us
    ppermute x5, waiting for transfers between devices, layered(): return lax.ppermute(array, 'seq', pairs)  10.6 us
    ppermute x4, starting transfers between devices, shifted(): return lax.ppermute(array, 'seq', pairs)  8.93 us
    ppermute x3, starting transfers between devices, crossed(): return lax.ppermute(array, ('seq', 'head'), pairs)  6.32 us
  transfers between devices with their start and end apart: 25, of which 11 were waited for; matrix products, arithmetic and copies ran while one was open for 0% of the time, Pallas kernels for 26%

profile of v3, /device:TPU:0, one launch (start us, length us, event | category | flops | bytes accessed | tf_op | source)
XLA Modules:
  0.0 119.6 jit_solution(7496798941961279731)
XLA Ops:
  0.0 2.4 %pack.1 = (bf16[256,512]{1,0:T(8,128)(2,1)}, bf16[224,2304]{1,0:T(8,128)(2,1)}) custom-call(bf16[256,256]{1,0:T(8,128)(2,1)} %refs_0_.1, bf16[256,256]{1,0:T(8,128)(2,1)} %refs_1_.1, bf16[224,1792]{1,0:T(8,128)(2,1)} %refs_2_.1, bf16[224,256]{1,0:T(8,128)(2,1)} %refs_3_.1, bf16[224,256]{1,0:T(8,128)(2,1)} %refs_4_.1), custom_call_target="tpu_custom_call" | custom-call | flops 1 | bytes 1 | tf_op jit(solution)/shard_map/pack/pallas_call | solution.py:432
  2.4 4.9 %collective-permute-start.1 = (bf16[256,512]{1,0:T(8,128)(2,1)}, bf16[256,512]{1,0:T(8,128)(2,1)S(1)}, u32[]{:S(2)}, u32[]{:S(2)}) collective-permute-start(bf16[256,512]{1,0:T(8,128)(2,1)} %get-tuple-element.28.k_own_ref.v_own_ref), channel_id=1, source_target_pairs={{0,4},{2,6},{4,8},{6,10},{8,12},{10,14},{12,16},{14,18},{16,20},{1... | collective-permute-start | bytes 786440 | tf_op jit(solution)/shard_map/ppermute | solution.py:490
  7.3 1.5 %collective-permute-start = (bf16[256,512]{1,0:T(8,128)(2,1)}, bf16[256,512]{1,0:T(8,128)(2,1)S(1)}, u32[]{:S(2)}, u32[]{:S(2)}) collective-permute-start(bf16[256,512]{1,0:T(8,128)(2,1)} %get-tuple-element.28.k_own_ref.v_own_ref), channel_id=1, source_target_pairs={{0,2},{2,4},{4,6},{6,8},{8,10},{10,12},{12,14},{14,16},{16,18},{18... | collective-permute-start | bytes 786440 | tf_op jit(solution)/shard_map/ppermute | solution.py:490
  8.8 1.7 %collective-permute-start.5 = (bf16[224,2304]{1,0:T(8,128)(2,1)}, bf16[224,2304]{1,0:T(8,128)(2,1)}, u32[]{:S(2)}, u32[]{:S(2)}) collective-permute-start(bf16[224,2304]{1,0:T(8,128)(2,1)} %get-tuple-element.37.refs_0_), channel_id=1, source_target_pairs={{8,16},{10,18},{12,20},{14,22},{16,8},{18,10},{20,12},{22,14},{9,1... | collective-permute-start | bytes 3096584 | tf_op jit(solution)/shard_map/ppermute | solution.py:500
  10.5 3.9 %collective-permute-start.4 = (bf16[224,2304]{1,0:T(8,128)(2,1)}, bf16[224,2304]{1,0:T(8,128)(2,1)}, u32[]{:S(2)}, u32[]{:S(2)}) collective-permute-start(bf16[224,2304]{1,0:T(8,128)(2,1)} %get-tuple-element.37.refs_0_), channel_id=1, source_target_pairs={{0,8},{2,10},{4,12},{6,14},{8,0},{10,2},{12,4},{14,6},{16,24},{18,... | collective-permute-start | bytes 3096584 | tf_op jit(solution)/shard_map/ppermute | solution.py:500
  15.2 5.8 %attention.2 = (bf16[256,896]{1,0:T(8,128)(2,1)}, f32[256,256]{1,0:T(8,128)}, bf16[256,256]{1,0:T(8,128)(2,1)}, bf16[256,256]{1,0:T(8,128)(2,1)}) custom-call(s32[1]{0:T(128)} %bitcast.first_ref, s32[4]{0:T(128)} %docs_ref.3, bf16[256,1792]{1,0:T(8,128)(2,1)} %q_ref.3, bf16[256,1792]{1,0:T(8,128)(2,1)} %do_ref.3, bf16[256,1792]{1,0:T(8,128)(2,1)} %o_ref.3, ...), custom_call_target="tpu_custom_call" | custom-call | flops 24000000000 | bytes 1 | tf_op jit(solution)/shard_map/attention/pallas_call | solution.py:130
  20.9 3.9 %collective-permute-start.6 = (bf16[256,896]{1,0:T(8,128)(2,1)}, bf16[256,896]{1,0:T(8,128)(2,1)S(1)}, u32[]{:S(2)}, u32[]{:S(2)}) collective-permute-start(bf16[256,896]{1,0:T(8,128)(2,1)} %get-tuple-element.29.refs_0_), channel_id=1, source_target_pairs={{0,4},{2,6},{4,0},{6,2},{8,12},{10,14},{12,8},{14,10},{16,20},{18,... | collective-permute-start | bytes 1376264 | tf_op jit(solution)/shard_map/ppermute | solution.py:495
  24.8 6.3 %attention.3 = (bf16[256,896]{1,0:T(8,128)(2,1)}, f32[256,512]{1,0:T(8,128)}, bf16[256,512]{1,0:T(8,128)(2,1)}, bf16[256,512]{1,0:T(8,128)(2,1)}) custom-call(s32[1]{0:T(128)} %bitcast.first_ref, s32[4]{0:T(128)} %docs_ref.3, bf16[256,1792]{1,0:T(8,128)(2,1)} %q_ref.3, bf16[256,1792]{1,0:T(8,128)(2,1)} %do_ref.3, bf16[256,1792]{1,0:T(8,128)(2,1)} %o_ref.3, ...), custom_call_target="tpu_custom_call" | custom-call | flops 4000000000 | bytes 1 | tf_op jit(solution)/shard_map/attention/pallas_call | solution.py:130
  32.4 1.3 %collective-permute-start.3 = (bf16[256,512]{1,0:T(8,128)(2,1)}, bf16[256,512]{1,0:T(8,128)(2,1)S(1)}, u32[]{:S(2)}, u32[]{:S(2)}) collective-permute-start(bf16[256,512]{1,0:T(8,128)(2,1)} %get-tuple-element.36), channel_id=1, source_target_pairs={{4,0},{6,2},{8,4},{10,6},{12,8},{14,10},{16,12},{18,14},{20,16},{2... | collective-permute-start | bytes 786440 | tf_op jit(solution)/shard_map/ppermute | solution.py:490
  35.0 2.7 %collective-permute-done.4.refs_0_.mate = bf16[224,2304]{1,0:T(8,128)(2,1)} collective-permute-done((bf16[224,2304]{1,0:T(8,128)(2,1)}, bf16[224,2304]{1,0:T(8,128)(2,1)}, u32[]{:S(2)}, u32[]{:S(2)}) %collective-permute-start.4) | collective-permute-done | bytes 1032224 | tf_op jit(solution)/shard_map/ppermute | solution.py:500
  37.8 1.7 %collective-permute-start.13 = (bf16[224,2304]{1,0:T(8,128)(2,1)}, bf16[224,2304]{1,0:T(8,128)(2,1)}, u32[]{:S(2)}, u32[]{:S(2)}) collective-permute-start(bf16[224,2304]{1,0:T(8,128)(2,1)} %collective-permute-done.4.refs_0_.mate), channel_id=1, source_target_pairs={{8,16},{10,18},{12,20},{14,22},{16,8},{18,10},{20,12},{22,14},{9,1... | collective-permute-start | bytes 3096584 | tf_op jit(solution)/shard_map/ppermute | solution.py:500
  39.4 4.5 %collective-permute-done.3.far = bf16[256,512]{1,0:T(8,128)(2,1)S(1)} collective-permute-done((bf16[256,512]{1,0:T(8,128)(2,1)}, bf16[256,512]{1,0:T(8,128)(2,1)S(1)}, u32[]{:S(2)}, u32[]{:S(2)}) %collective-permute-start.3) | collective-permute-done | bytes 262176 | tf_op jit(solution)/shard_map/ppermute | solution.py:490
  44.8 2.3 %join.1.refs_1_ = bf16[256,1408]{1,0:T(8,128)(2,1)} custom-call(bf16[256,896]{1,0:T(8,128)(2,1)} %get-tuple-element.33.dq, f32[256,512]{1,0:T(8,128)} %get-tuple-element.34.own, bf16[256,512]{1,0:T(8,128)(2,1)} %copy-done.7, bf16[256,512]{1,0:T(8,128)(2,1)} %copy-done.8, bf16[224,2304]{1,0:T(8,128)(2,1)} %collective-permute-done.4.refs_0_.mate, ...), custom_call_target="tpu_custom_call" | custom-call | flops 2000000000 | bytes 1 | tf_op jit(solution)/shard_map/join/pallas_call | solution.py:476
  47.1 6.4 %collective-permute-start.7 = (bf16[256,1408]{1,0:T(8,128)(2,1)}, bf16[256,1408]{1,0:T(8,128)(2,1)S(1)}, u32[]{:S(2)}, u32[]{:S(2)}) collective-permute-start(bf16[256,1408]{1,0:T(8,128)(2,1)} %join.1.refs_1_), channel_id=1, source_target_pairs={{0,4},{2,6},{4,0},{6,2},{8,12},{10,14},{12,8},{14,10},{16,20},{18,... | collective-permute-start | bytes 2162696 | tf_op jit(solution)/shard_map/ppermute | solution.py:495
  54.0 1.8 %collective-permute-done.8.refs_4_ = bf16[256,896]{1,0:T(8,128)(2,1)S(1)} collective-permute-done((bf16[256,896]{1,0:T(8,128)(2,1)}, bf16[256,896]{1,0:T(8,128)(2,1)S(1)}, u32[]{:S(2)}, u32[]{:S(2)}) %collective-permute-start.8) | collective-permute-done | bytes 458784 | tf_op jit(solution)/shard_map/ppermute | solution.py:495
  56.0 9.8 %collective-permute-done.7.refs_3_ = bf16[256,1408]{1,0:T(8,128)(2,1)S(1)} collective-permute-done((bf16[256,1408]{1,0:T(8,128)(2,1)}, bf16[256,1408]{1,0:T(8,128)(2,1)S(1)}, u32[]{:S(2)}, u32[]{:S(2)}) %collective-permute-start.7) | collective-permute-done | bytes 720928 | tf_op jit(solution)/shard_map/ppermute | solution.py:495
  65.8 3.2 %collective-permute-done.12.refs_1_.refs_9_.edge = bf16[224,2304]{1,0:T(8,128)(2,1)} collective-permute-done((bf16[224,2304]{1,0:T(8,128)(2,1)}, bf16[224,2304]{1,0:T(8,128)(2,1)}, u32[]{:S(2)}, u32[]{:S(2)}) %collective-permute-start.12) | collective-permute-done | bytes 1032224 | tf_op jit(solution)/shard_map/ppermute | solution.py:500
  68.9 4.1 %collective-permute-start.14 = (bf16[224,2304]{1,0:T(8,128)(2,1)}, bf16[224,2304]{1,0:T(8,128)(2,1)}, u32[]{:S(2)}, u32[]{:S(2)}) collective-permute-start(bf16[224,2304]{1,0:T(8,128)(2,1)} %gate.1.refs_8_.own), channel_id=1, source_target_pairs={{0,24},{2,26},{4,28},{6,30},{24,0},{26,2},{28,4},{30,6},{1,25},{3,... | collective-permute-start | bytes 3096584 | tf_op jit(solution)/shard_map/ppermute | solution.py:500
  73.1 6.1 %project_send.1 = (bf16[256,896]{1,0:T(8,128)(2,1)}, bf16[1024,2304]{1,0:T(8,128)(2,1)}) custom-call(bf16[256,896]{1,0:T(8,128)(2,1)} %get-tuple-element.29.refs_0_, bf16[256,1408]{1,0:T(8,128)(2,1)} %join.1.refs_1_, bf16[256,896]{1,0:T(8,128)(2,1)} %copy-done.4, bf16[256,1408]{1,0:T(8,128)(2,1)} %copy-done.1, bf16[256,896]{1,0:T(8,128)(2,1)} %copy-done.2, ...), custom_call_target="tpu_custom_call" | custom-call | flops 1 | bytes 1 | tf_op jit(solution)/shard_map/project_send/pallas_call | solution.py:283
  79.2 1.6 %collective-permute-start.15 = (bf16[256,896]{1,0:T(8,128)(2,1)}, bf16[256,896]{1,0:T(8,128)(2,1)S(1)}, u32[]{:S(2)}, u32[]{:S(2)}) collective-permute-start(bf16[256,896]{1,0:T(8,128)(2,1)} %get-tuple-element.39.refs_0_), channel_id=1, source_target_pairs={{0,1},{1,0},{2,3},{3,2},{4,5},{5,4},{6,7},{7,6},{8,9},{9,8},{10,11... | collective-permute-start | bytes 1376264 | tf_op jit(solution)/shard_map/ppermute | solution.py:604
  80.8 7.5 %project_keep.1 = (f32[4,256,224]{2,1,0:T(8,128)}, f32[4,256,224]{2,1,0:T(8,128)}, bf16[256,896]{1,0:T(8,128)(2,1)}) custom-call(bf16[1024,2304]{1,0:T(8,128)(2,1)} %get-tuple-element.38.held, bf16[224,2304]{1,0:T(8,128)(2,1)} %gate.1.refs_8_.own, bf16[224,2304]{1,0:T(8,128)(2,1)} %collective-permute-done.4.refs_0_.mate, ...), custom_call_target="tpu_custom_call" | custom-call | flops 1 | bytes 1 | tf_op jit(solution)/shard_map/project_keep/pallas_call | solution.py:283
  88.4 1.6 %collective-permute-start.16 = (bf16[256,896]{1,0:T(8,128)(2,1)}, bf16[256,896]{1,0:T(8,128)(2,1)S(1)}, u32[]{:S(2)}, u32[]{:S(2)}) collective-permute-start(bf16[256,896]{1,0:T(8,128)(2,1)} %get-tuple-element.42), channel_id=1, source_target_pairs={{1,0},{3,2},{5,4},{7,6},{9,8},{11,10},{13,12},{15,14},{16,17},{18,... | collective-permute-start | bytes 1376264 | tf_op jit(solution)/shard_map/ppermute | solution.py:508
  90.0 1.3 %collective-permute-done.15.refs_0_ = bf16[256,896]{1,0:T(8,128)(2,1)S(1)} collective-permute-done((bf16[256,896]{1,0:T(8,128)(2,1)}, bf16[256,896]{1,0:T(8,128)(2,1)S(1)}, u32[]{:S(2)}, u32[]{:S(2)}) %collective-permute-start.15) | collective-permute-done | bytes 458784 | tf_op jit(solution)/shard_map/ppermute | solution.py:604
  91.3 4.7 %collective-permute-done.14.piece = bf16[224,2304]{1,0:T(8,128)(2,1)} collective-permute-done((bf16[224,2304]{1,0:T(8,128)(2,1)}, bf16[224,2304]{1,0:T(8,128)(2,1)}, u32[]{:S(2)}, u32[]{:S(2)}) %collective-permute-start.14) | collective-permute-done | bytes 1032224 | tf_op jit(solution)/shard_map/ppermute | solution.py:500
  96.0 2.7 %project_last.1 = (f32[2,256,224]{2,1,0:T(8,128)S(1)}, bf16[256,448]{1,0:T(8,128)(2,1)S(1)}, f32[2,256,224]{2,1,0:T(8,128)S(1)}, bf16[256,448]{1,0:T(8,128)(2,1)S(1)}) custom-call(bf16[1024,2304]{1,0:T(8,128)(2,1)S(1)} %bitcast.18, bf16[224,2304]{1,0:T(8,128)(2,1)} %collective-permute-done.14.piece, ...), custom_call_target="tpu_custom_call" | custom-call | flops 1 | bytes 1 | tf_op jit(solution)/shard_map/project_last/pallas_call | solution.py:283
  98.7 3.4 %collective-permute-start.18 = (bf16[256,448]{1,0:T(8,128)(2,1)S(1)}, bf16[256,448]{1,0:T(8,128)(2,1)S(1)}, u32[]{:S(2)}, u32[]{:S(2)}) collective-permute-start(bf16[256,448]{1,0:T(8,128)(2,1)S(1)} %get-tuple-element.45), channel_id=1, source_target_pairs={{0,1},{2,3},{4,5},{6,7},{8,9},{10,11},{12,13},{14,15},{17,16},{19,... | collective-permute-start | bytes 688136 | tf_op jit(solution)/shard_map/ppermute | solution.py:508
  104.3 1.3 %collective-permute-start.17 = (bf16[256,448]{1,0:T(8,128)(2,1)S(1)}, bf16[256,448]{1,0:T(8,128)(2,1)S(1)}, u32[]{:S(2)}, u32[]{:S(2)}) collective-permute-start(bf16[256,448]{1,0:T(8,128)(2,1)S(1)} %get-tuple-element.43), channel_id=1, source_target_pairs={{0,1},{2,3},{4,5},{6,7},{8,9},{10,11},{12,13},{14,15},{17,16},{19,... | collective-permute-start | bytes 688136 | tf_op jit(solution)/shard_map/ppermute | solution.py:508
  105.6 2.6 %collective-permute-done.21.refs_2_.refs_3_ = bf16[256,224]{1,0:T(8,128)(2,1)S(1)} collective-permute-done((bf16[256,224]{1,0:T(8,128)(2,1)S(1)}, bf16[256,224]{1,0:T(8,128)(2,1)S(1)}, u32[]{:S(2)}, u32[]{:S(2)}) %collective-permute-start.21) | collective-permute-done | bytes 114720 | tf_op jit(solution)/shard_map/ppermute | solution.py:495
  108.1 1.6 %collective-permute-done.20.refs_1_.refs_2_ = bf16[256,224]{1,0:T(8,128)(2,1)S(1)} collective-permute-done((bf16[256,224]{1,0:T(8,128)(2,1)S(1)}, bf16[256,224]{1,0:T(8,128)(2,1)S(1)}, u32[]{:S(2)}, u32[]{:S(2)}) %collective-permute-start.20) | collective-permute-done | bytes 114720 | tf_op jit(solution)/shard_map/ppermute | solution.py:495
  110.0 1.8 %collective-permute-start.23 = (bf16[256,224]{1,0:T(8,128)(2,1)S(1)}, bf16[256,224]{1,0:T(8,128)(2,1)S(1)}, u32[]{:S(2)}, u32[]{:S(2)}) collective-permute-start(bf16[256,224]{1,0:T(8,128)(2,1)S(1)} %get-tuple-element.47.refs_0_), channel_id=1, source_target_pairs={{0,4},{2,6},{4,0},{6,2},{8,12},{10,14},{12,8},{14,10},{16,20},{18,... | collective-permute-start | bytes 344072 | tf_op jit(solution)/shard_map/ppermute | solution.py:495
  112.4 3.9 %collective-permute-done.23.refs_4_ = bf16[256,224]{1,0:T(8,128)(2,1)S(1)} collective-permute-done((bf16[256,224]{1,0:T(8,128)(2,1)S(1)}, bf16[256,224]{1,0:T(8,128)(2,1)S(1)}, u32[]{:S(2)}, u32[]{:S(2)}) %collective-permute-start.23) | collective-permute-done | bytes 114720 | tf_op jit(solution)/shard_map/ppermute | solution.py:495
  116.3 1.9 %collective-permute-done.24.refs_5_ = bf16[256,224]{1,0:T(8,128)(2,1)S(1)} collective-permute-done((bf16[256,224]{1,0:T(8,128)(2,1)S(1)}, bf16[256,224]{1,0:T(8,128)(2,1)S(1)}, u32[]{:S(2)}, u32[]{:S(2)}) %collective-permute-start.24) | collective-permute-done | bytes 114720 | tf_op jit(solution)/shard_map/ppermute | solution.py:495
  (54 shorter events, 9.3 us)
Async XLA Ops:
  2.4 11.9 %collective-permute-start.1 = (bf16[256,512]{1,0:T(8,128)(2,1)}, bf16[256,512]{1,0:T(8,128)(2,1)S(1)}, u32[]{:S(2)}, u32[]{:S(2)}) collective-permute-start(bf16[256,512]{1,0:T(8,128)(2,1)} %get-tuple-element.28.k_own_ref.v_own_ref), channel_id=1, source_target_pairs={{0,4},{2,6},{4,8},{6,10},{8,12},{10,14},{12,16},{14,18},{16,20},{1... | collective-permute-start | bytes 786440 | tf_op jit(solution)/shard_map/ppermute | solution.py:490
  7.3 7.1 %collective-permute-start = (bf16[256,512]{1,0:T(8,128)(2,1)}, bf16[256,512]{1,0:T(8,128)(2,1)S(1)}, u32[]{:S(2)}, u32[]{:S(2)}) collective-permute-start(bf16[256,512]{1,0:T(8,128)(2,1)} %get-tuple-element.28.k_own_ref.v_own_ref), channel_id=1, source_target_pairs={{0,2},{2,4},{4,6},{6,8},{8,10},{10,12},{12,14},{14,16},{16,18},{18... | collective-permute-start | bytes 786440 | tf_op jit(solution)/shard_map/ppermute | solution.py:490
  8.8 24.9 %collective-permute-start.5 = (bf16[224,2304]{1,0:T(8,128)(2,1)}, bf16[224,2304]{1,0:T(8,128)(2,1)}, u32[]{:S(2)}, u32[]{:S(2)}) collective-permute-start(bf16[224,2304]{1,0:T(8,128)(2,1)} %get-tuple-element.37.refs_0_), channel_id=1, source_target_pairs={{8,16},{10,18},{12,20},{14,22},{16,8},{18,10},{20,12},{22,14},{9,1... | collective-permute-start | bytes 3096584 | tf_op jit(solution)/shard_map/ppermute | solution.py:500
  10.5 27.3 %collective-permute-start.4 = (bf16[224,2304]{1,0:T(8,128)(2,1)}, bf16[224,2304]{1,0:T(8,128)(2,1)}, u32[]{:S(2)}, u32[]{:S(2)}) collective-permute-start(bf16[224,2304]{1,0:T(8,128)(2,1)} %get-tuple-element.37.refs_0_), channel_id=1, source_target_pairs={{0,8},{2,10},{4,12},{6,14},{8,0},{10,2},{12,4},{14,6},{16,24},{18,... | collective-permute-start | bytes 3096584 | tf_op jit(solution)/shard_map/ppermute | solution.py:500
  20.9 23.0 %collective-permute-start.6 = (bf16[256,896]{1,0:T(8,128)(2,1)}, bf16[256,896]{1,0:T(8,128)(2,1)S(1)}, u32[]{:S(2)}, u32[]{:S(2)}) collective-permute-start(bf16[256,896]{1,0:T(8,128)(2,1)} %get-tuple-element.29.refs_0_), channel_id=1, source_target_pairs={{0,4},{2,6},{4,0},{6,2},{8,12},{10,14},{12,8},{14,10},{16,20},{18,... | collective-permute-start | bytes 1376264 | tf_op jit(solution)/shard_map/ppermute | solution.py:495
  31.1 8.3 %collective-permute-start.2 = (bf16[256,512]{1,0:T(8,128)(2,1)}, bf16[256,512]{1,0:T(8,128)(2,1)S(1)}, u32[]{:S(2)}, u32[]{:S(2)}) collective-permute-start(bf16[256,512]{1,0:T(8,128)(2,1)} %get-tuple-element.35), channel_id=1, source_target_pairs={{2,0},{4,2},{6,4},{8,6},{10,8},{12,10},{14,12},{16,14},{18,16},{20... | collective-permute-start | bytes 786440 | tf_op jit(solution)/shard_map/ppermute | solution.py:490
  32.4 11.5 %collective-permute-start.3 = (bf16[256,512]{1,0:T(8,128)(2,1)}, bf16[256,512]{1,0:T(8,128)(2,1)S(1)}, u32[]{:S(2)}, u32[]{:S(2)}) collective-permute-start(bf16[256,512]{1,0:T(8,128)(2,1)} %get-tuple-element.36), channel_id=1, source_target_pairs={{4,0},{6,2},{8,4},{10,6},{12,8},{14,10},{16,12},{18,14},{20,16},{2... | collective-permute-start | bytes 786440 | tf_op jit(solution)/shard_map/ppermute | solution.py:490
  33.7 35.2 %collective-permute-start.12 = (bf16[224,2304]{1,0:T(8,128)(2,1)}, bf16[224,2304]{1,0:T(8,128)(2,1)}, u32[]{:S(2)}, u32[]{:S(2)}) collective-permute-start(bf16[224,2304]{1,0:T(8,128)(2,1)} %collective-permute-done.5.refs_1_.refs_10_.mid), channel_id=1, source_target_pairs={{8,0},{10,2},{12,4},{14,6},{16,24},{18,26},{20,28},{22,30},{9,1},{... | collective-permute-start | bytes 3096584 | tf_op jit(solution)/shard_map/ppermute | solution.py:500
  37.8 31.2 %collective-permute-start.13 = (bf16[224,2304]{1,0:T(8,128)(2,1)}, bf16[224,2304]{1,0:T(8,128)(2,1)}, u32[]{:S(2)}, u32[]{:S(2)}) collective-permute-start(bf16[224,2304]{1,0:T(8,128)(2,1)} %collective-permute-done.4.refs_0_.mate), channel_id=1, source_target_pairs={{8,16},{10,18},{12,20},{14,22},{16,8},{18,10},{20,12},{22,14},{9,1... | collective-permute-start | bytes 3096584 | tf_op jit(solution)/shard_map/ppermute | solution.py:500
  39.4 4.5 %copy-start.7 = (bf16[256,512]{1,0:T(8,128)(2,1)}, bf16[256,512]{1,0:T(8,128)(2,1)S(1)}, u32[]{:S(2)}) copy-start(bf16[256,512]{1,0:T(8,128)(2,1)S(1)} %collective-permute-done.2.near) | copy-start | bytes 786436
  47.1 18.6 %collective-permute-start.7 = (bf16[256,1408]{1,0:T(8,128)(2,1)}, bf16[256,1408]{1,0:T(8,128)(2,1)S(1)}, u32[]{:S(2)}, u32[]{:S(2)}) collective-permute-start(bf16[256,1408]{1,0:T(8,128)(2,1)} %join.1.refs_1_), channel_id=1, source_target_pairs={{0,4},{2,6},{4,0},{6,2},{8,12},{10,14},{12,8},{14,10},{16,20},{18,... | collective-permute-start | bytes 2162696 | tf_op jit(solution)/shard_map/ppermute | solution.py:495
  53.5 2.3 %collective-permute-start.8 = (bf16[256,896]{1,0:T(8,128)(2,1)}, bf16[256,896]{1,0:T(8,128)(2,1)S(1)}, u32[]{:S(2)}, u32[]{:S(2)}) collective-permute-start(bf16[256,896]{1,0:T(8,128)(2,1)} %get-tuple-element.29.refs_0_), channel_id=1, source_target_pairs={{0,2},{2,0},{4,6},{6,4},{8,10},{10,8},{12,14},{14,12},{16,18},{18,... | collective-permute-start | bytes 1376264 | tf_op jit(solution)/shard_map/ppermute | solution.py:495
  53.5 12.2 %collective-permute-start.10 = (bf16[256,896]{1,0:T(8,128)(2,1)}, bf16[256,896]{1,0:T(8,128)(2,1)}, u32[]{:S(2)}, u32[]{:S(2)}) collective-permute-start(bf16[256,896]{1,0:T(8,128)(2,1)} %copy-done.4), channel_id=1, source_target_pairs={{0,2},{2,0},{4,6},{6,4},{8,10},{10,8},{12,14},{14,12},{16,18},{18,... | collective-permute-start | bytes 1376264 | tf_op jit(solution)/shard_map/ppermute | solution.py:495
  55.8 9.9 %copy-start.2 = (bf16[256,896]{1,0:T(8,128)(2,1)}, bf16[256,896]{1,0:T(8,128)(2,1)S(1)}, u32[]{:S(2)}) copy-start(bf16[256,896]{1,0:T(8,128)(2,1)S(1)} %collective-permute-done.8.refs_4_) | copy-start | bytes 1376260
  55.8 17.2 %collective-permute-start.9 = (bf16[256,1408]{1,0:T(8,128)(2,1)}, bf16[256,1408]{1,0:T(8,128)(2,1)}, u32[]{:S(2)}, u32[]{:S(2)}) collective-permute-start(bf16[256,1408]{1,0:T(8,128)(2,1)} %join.1.refs_1_), channel_id=1, source_target_pairs={{0,2},{2,0},{4,6},{6,4},{8,10},{10,8},{12,14},{14,12},{16,18},{18,... | collective-permute-start | bytes 2162696 | tf_op jit(solution)/shard_map/ppermute | solution.py:495
  65.7 3.2 %copy-start.1 = (bf16[256,1408]{1,0:T(8,128)(2,1)}, bf16[256,1408]{1,0:T(8,128)(2,1)S(1)}, u32[]{:S(2)}) copy-start(bf16[256,1408]{1,0:T(8,128)(2,1)S(1)} %collective-permute-done.7.refs_3_) | copy-start | bytes 2162692
  65.7 7.3 %collective-permute-start.11 = (bf16[256,1408]{1,0:T(8,128)(2,1)S(1)}, bf16[256,1408]{1,0:T(8,128)(2,1)}, u32[]{:S(2)}, u32[]{:S(2)}) collective-permute-start(bf16[256,1408]{1,0:T(8,128)(2,1)S(1)} %collective-permute-done.7.refs_3_), channel_id=1, source_target_pairs={{0,2},{2,0},{4,6},{6,4},{8,10},{10,8},{12,14},{14,12},{16,18},{18,... | collective-permute-start | bytes 2162696 | tf_op jit(solution)/shard_map/ppermute | solution.py:495
  68.9 27.1 %collective-permute-start.14 = (bf16[224,2304]{1,0:T(8,128)(2,1)}, bf16[224,2304]{1,0:T(8,128)(2,1)}, u32[]{:S(2)}, u32[]{:S(2)}) collective-permute-start(bf16[224,2304]{1,0:T(8,128)(2,1)} %gate.1.refs_8_.own), channel_id=1, source_target_pairs={{0,24},{2,26},{4,28},{6,30},{24,0},{26,2},{28,4},{30,6},{1,25},{3,... | collective-permute-start | bytes 3096584 | tf_op jit(solution)/shard_map/ppermute | solution.py:500
  79.2 16.8 %slice-start = ((s8[4718592]{0:T(1024)(128)(4,1)}), s8[4194304]{0:T(1024)(128)(4,1)S(1)}, s32[]{:S(2)}) async-start(s8[4718592]{0:T(1024)(128)(4,1)} %bitcast.17), calls=%async_computation | async-start | bytes 8388608
  79.2 12.1 %collective-permute-start.15 = (bf16[256,896]{1,0:T(8,128)(2,1)}, bf16[256,896]{1,0:T(8,128)(2,1)S(1)}, u32[]{:S(2)}, u32[]{:S(2)}) collective-permute-start(bf16[256,896]{1,0:T(8,128)(2,1)} %get-tuple-element.39.refs_0_), channel_id=1, source_target_pairs={{0,1},{1,0},{2,3},{3,2},{4,5},{5,4},{6,7},{7,6},{8,9},{9,8},{10,11... | collective-permute-start | bytes 1376264 | tf_op jit(solution)/shard_map/ppermute | solution.py:604
  80.8 15.2 %slice-start.1 = ((s8[4718592]{0:T(1024)(128)(4,1)}), s8[524288]{0:T(1024)(128)(4,1)S(1)}, s32[]{:S(2)}) async-start(s8[4718592]{0:T(1024)(128)(4,1)} %bitcast.17), calls=%async_computation.1 | async-start | bytes 1048576
  88.3 13.8 %copy-start.3 = (f32[4,256,224]{2,1,0:T(8,128)S(1)}, f32[4,256,224]{2,1,0:T(8,128)}, u32[]{:S(2)}) copy-start(f32[4,256,224]{2,1,0:T(8,128)} %get-tuple-element.46) | copy-start | bytes 2752516
  88.3 21.3 %copy-start = (f32[4,256,224]{2,1,0:T(8,128)S(1)}, f32[4,256,224]{2,1,0:T(8,128)}, u32[]{:S(2)}) copy-start(f32[4,256,224]{2,1,0:T(8,128)} %get-tuple-element.41.mate_full) | copy-start | bytes 2752516
  88.4 15.9 %collective-permute-start.16 = (bf16[256,896]{1,0:T(8,128)(2,1)}, bf16[256,896]{1,0:T(8,128)(2,1)S(1)}, u32[]{:S(2)}, u32[]{:S(2)}) collective-permute-start(bf16[256,896]{1,0:T(8,128)(2,1)} %get-tuple-element.42), channel_id=1, source_target_pairs={{1,0},{3,2},{5,4},{7,6},{9,8},{11,10},{13,12},{15,14},{16,17},{18,... | collective-permute-start | bytes 1376264 | tf_op jit(solution)/shard_map/ppermute | solution.py:508
  98.7 11.0 %collective-permute-start.18 = (bf16[256,448]{1,0:T(8,128)(2,1)S(1)}, bf16[256,448]{1,0:T(8,128)(2,1)S(1)}, u32[]{:S(2)}, u32[]{:S(2)}) collective-permute-start(bf16[256,448]{1,0:T(8,128)(2,1)S(1)} %get-tuple-element.45), channel_id=1, source_target_pairs={{0,1},{2,3},{4,5},{6,7},{8,9},{10,11},{12,13},{14,15},{17,16},{19,... | collective-permute-start | bytes 688136 | tf_op jit(solution)/shard_map/ppermute | solution.py:508
  102.3 5.8 %collective-permute-start.21 = (bf16[256,224]{1,0:T(8,128)(2,1)S(1)}, bf16[256,224]{1,0:T(8,128)(2,1)S(1)}, u32[]{:S(2)}, u32[]{:S(2)}) collective-permute-start(bf16[256,224]{1,0:T(8,128)(2,1)S(1)} %get-tuple-element.52), channel_id=1, source_target_pairs={{0,6},{2,4},{4,2},{6,0},{8,14},{10,12},{12,10},{14,8},{16,22},{18,... | collective-permute-start | bytes 344072 | tf_op jit(solution)/shard_map/ppermute | solution.py:495
  102.4 7.3 %collective-permute-start.20 = (bf16[256,224]{1,0:T(8,128)(2,1)S(1)}, bf16[256,224]{1,0:T(8,128)(2,1)S(1)}, u32[]{:S(2)}, u32[]{:S(2)}) collective-permute-start(bf16[256,224]{1,0:T(8,128)(2,1)S(1)} %get-tuple-element.53), channel_id=1, source_target_pairs={{0,4},{2,6},{4,0},{6,2},{8,12},{10,14},{12,8},{14,10},{16,20},{18,... | collective-permute-start | bytes 344072 | tf_op jit(solution)/shard_map/ppermute | solution.py:495
  103.2 6.5 %collective-permute-start.19 = (bf16[256,224]{1,0:T(8,128)(2,1)S(1)}, bf16[256,224]{1,0:T(8,128)(2,1)S(1)}, u32[]{:S(2)}, u32[]{:S(2)}) collective-permute-start(bf16[256,224]{1,0:T(8,128)(2,1)S(1)} %get-tuple-element.54), channel_id=1, source_target_pairs={{0,2},{2,0},{4,6},{6,4},{8,10},{10,8},{12,14},{14,12},{16,18},{18,... | collective-permute-start | bytes 344072 | tf_op jit(solution)/shard_map/ppermute | solution.py:495
  104.3 7.6 %collective-permute-start.17 = (bf16[256,448]{1,0:T(8,128)(2,1)S(1)}, bf16[256,448]{1,0:T(8,128)(2,1)S(1)}, u32[]{:S(2)}, u32[]{:S(2)}) collective-permute-start(bf16[256,448]{1,0:T(8,128)(2,1)S(1)} %get-tuple-element.43), channel_id=1, source_target_pairs={{0,1},{2,3},{4,5},{6,7},{8,9},{10,11},{12,13},{14,15},{17,16},{19,... | collective-permute-start | bytes 688136 | tf_op jit(solution)/shard_map/ppermute | solution.py:508
  110.0 6.4 %collective-permute-start.23 = (bf16[256,224]{1,0:T(8,128)(2,1)S(1)}, bf16[256,224]{1,0:T(8,128)(2,1)S(1)}, u32[]{:S(2)}, u32[]{:S(2)}) collective-permute-start(bf16[256,224]{1,0:T(8,128)(2,1)S(1)} %get-tuple-element.47.refs_0_), channel_id=1, source_target_pairs={{0,4},{2,6},{4,0},{6,2},{8,12},{10,14},{12,8},{14,10},{16,20},{18,... | collective-permute-start | bytes 344072 | tf_op jit(solution)/shard_map/ppermute | solution.py:495
  111.7 6.5 %collective-permute-start.24 = (bf16[256,224]{1,0:T(8,128)(2,1)S(1)}, bf16[256,224]{1,0:T(8,128)(2,1)S(1)}, u32[]{:S(2)}, u32[]{:S(2)}) collective-permute-start(bf16[256,224]{1,0:T(8,128)(2,1)S(1)} %get-tuple-element.48.refs_1_), channel_id=1, source_target_pairs={{0,6},{2,4},{4,2},{6,0},{8,14},{10,12},{12,10},{14,8},{16,22},{18,... | collective-permute-start | bytes 344072 | tf_op jit(solution)/shard_map/ppermute | solution.py:495
  112.0 6.5 %collective-permute-start.22 = (bf16[256,224]{1,0:T(8,128)(2,1)S(1)}, bf16[256,224]{1,0:T(8,128)(2,1)S(1)}, u32[]{:S(2)}, u32[]{:S(2)}) collective-permute-start(bf16[256,224]{1,0:T(8,128)(2,1)S(1)} %get-tuple-element.50), channel_id=1, source_target_pairs={{0,2},{2,0},{4,6},{6,4},{8,10},{10,8},{12,14},{14,12},{16,18},{18,... | collective-permute-start | bytes 344072 | tf_op jit(solution)/shard_map/ppermute | solution.py:495
  (4 other events, 3.1 us)

commit v4 on v3

--- a/solution.py
+++ b/solution.py
@@ -13,7 +13,8 @@
 INNER = 4
 LOG2E = 1.4426950408889634
 VMEM_LIMIT = 63 * 2**20
-JOIN_LIMIT = 63 * 2**20
+JOIN_COST = 10**9 + 1
+ATTENTION_COST = 9 * 10**8
 F32 = jnp.float32
 BF16 = jnp.bfloat16
 
@@ -189,18 +190,15 @@
 
 def standing(layers):
     layer = lax.axis_index("seq") // INNER
-    at_edge = (layer == 0) | (layer == layers - 1)
-    return at_edge, lax.axis_index("head") == layer // (layers // 2)
-
-
-def fetch_either(choice, first, second, weight, sem):
-    @pl.when(choice)
-    def _():
-        pltpu.make_async_copy(first, weight, sem).start()
-
-    @pl.when(jnp.logical_not(choice))
-    def _():
-        pltpu.make_async_copy(second, weight, sem).start()
+    return lax.axis_index("head") == layer // (layers // 2)
+
+
+def fetch_by_layer(sources, weight, sem):
+    layer = lax.axis_index("seq") // INNER
+    for z, source in enumerate(sources):
+        @pl.when(layer == z)
+        def _():
+            pltpu.make_async_copy(source, weight, sem).start()
 
 
 def times(grad, weight):
@@ -208,14 +206,14 @@
 
 
 def send_kernel(layers, count, *refs):
-    grads, (own, edge, mid) = refs[:count], refs[count : count + 3]
+    grads, (own, *third) = refs[:count], refs[count : count + 1 + layers]
     send, gathered, held, weight, sems = refs[-5:]
     tokens, cols = grads[0].shape[0], weight.shape[0]
-    at_edge, same = standing(layers)
+    same = standing(layers)
 
     @pl.when(same)
     def _():
-        fetch_either(at_edge, edge, mid, weight, sems.at[count])
+        fetch_by_layer(third, weight, sems.at[count])
 
     @pl.when(jnp.logical_not(same))
     def _():
@@ -237,13 +235,13 @@
         store.wait()
 
 
-def keep_kernel(layers, held, own, mate, edge, mid, *refs):
+def keep_kernel(layers, held, own, *refs):
+    mate, third = refs[:layers], refs[layers : 2 * layers]
     keep, mate_full, mate_low, weights, sems = refs[-5:]
     cols = weights.shape[1]
     tokens = held.shape[0] // INNER
-    at_edge, same = standing(layers)
-    mate_copy = pltpu.make_async_copy(mate, weights.at[1], sems.at[1])
-    mate_copy.start()
+    same = standing(layers)
+    fetch_by_layer(mate, weights.at[1], sems.at[1])
 
     @pl.when(same)
     def _():
@@ -251,9 +249,9 @@
 
     @pl.when(jnp.logical_not(same))
     def _():
-        fetch_either(at_edge, edge, mid, weights.at[0], sems.at[0])
-
-    mate_copy.wait()
+        fetch_by_layer(third, weights.at[0], sems.at[0])
+
+    pltpu.make_async_copy(own, weights.at[1], sems.at[1]).wait()
     for t in range(INNER):
         product = times(held[t * tokens : (t + 1) * tokens, :], weights[1])
         mate_full[t] = product
@@ -263,18 +261,21 @@
         keep[t] = times(held[t * tokens : (t + 1) * tokens, :], weights[0])
 
 
-def last_kernel(parts, layers, held, piece, passed, *refs):
-    outs, weight, sem = refs[-2 - 2 * len(parts) : -2], refs[-2], refs[-1]
-    at_edge, _ = standing(layers)
-    fetch_either(at_edge, piece, passed, weight, sem)
-    pltpu.make_async_copy(piece, weight, sem).wait()
+def last_kernel(order, layers, held, *refs):
+    full, first, second, weight, sem = refs[-5:]
+    fetch_by_layer(refs[:layers], weight, sem)
+    pltpu.make_async_copy(refs[0], weight, sem).wait()
     tokens, cols = held.shape[0] // INNER, weight.shape[0]
-    for i, picks in enumerate(parts):
-        full, low = outs[2 * i : 2 * i + 2]
-        for k, t in enumerate(picks):
-            product = times(held[t * tokens : (t + 1) * tokens, :], weight[...])
-            full[k] = product
-            low[:, k * cols : (k + 1) * cols] = product.astype(BF16)
+    edge = first.shape[1]
+    for k, t in enumerate(order):
+        product = times(held[t * tokens : (t + 1) * tokens, :], weight[...])
+        full[t] = product
+        low = product.astype(BF16)
+        lo, hi = k * cols, (k + 1) * cols
+        if lo < edge:
+            first[:, lo : min(hi, edge)] = low[:, : min(hi, edge) - lo]
+        if hi > edge:
+            second[:, max(lo, edge) - edge : hi - edge] = low[:, max(lo, edge) - lo :]
 
 
 def project(kernel, layers, operands, in_vmem, outs, scratch, limit, name):
@@ -292,13 +293,13 @@
     )(*operands)
 
 
-def project_send(layers, grads, own, edge, mid):
+def project_send(layers, grads, own, third):
     tokens = grads[0].shape[0]
     cols, depth = own.shape
     return project(
         lambda layers, *refs: send_kernel(layers, len(grads), *refs),
         layers,
-        [*grads, own, edge, mid],
+        [*grads, own, *third],
         0,
         [(True, (tokens, INNER * cols), BF16), (False, (INNER * tokens, depth), BF16)],
         [
@@ -311,14 +312,14 @@
     )
 
 
-def project_keep(layers, gathered, own, mate, edge, mid, after):
+def project_keep(layers, gathered, own, mate, third, after):
     tokens, depth = gathered.shape[0] // INNER, gathered.shape[1]
     cols = own.shape[0]
     full = (True, (INNER, tokens, cols), F32)
     return project(
         keep_kernel,
         layers,
-        [gathered, own, mate, edge, mid, *after],
+        [gathered, own, *mate, *third, *after],
         1,
         [full, full, (True, (tokens, INNER * cols), BF16)],
         [pltpu.VMEM((2, cols, depth), BF16), pltpu.SemaphoreType.DMA((2,))],
@@ -327,52 +328,59 @@
     )
 
 
-def project_last(parts, layers, gathered, piece, passed, after):
-    tokens, cols = gathered.shape[0] // INNER, piece.shape[0]
-    outs = []
-    for picks in parts:
-        outs.append((True, (len(picks), tokens, cols), F32))
-        outs.append((True, (tokens, len(picks) * cols), BF16))
+def project_last(order, layers, gathered, late, after):
+    tokens, cols = gathered.shape[0] // INNER, late[0].shape[0]
+    edge = -(-INNER // 2 * cols // HEAD_SIZE) * HEAD_SIZE
     return project(
-        functools.partial(last_kernel, parts),
+        functools.partial(last_kernel, order),
         layers,
-        [gathered, piece, passed, *after],
+        [gathered, *late, *after],
         1,
-        outs,
-        [pltpu.VMEM(piece.shape, BF16), pltpu.SemaphoreType.DMA],
+        [
+            (True, (INNER, tokens, cols), F32),
+            (True, (tokens, edge), BF16),
+            (True, (tokens, INNER * cols - edge), BF16),
+        ],
+        [pltpu.VMEM(late[0].shape, BF16), pltpu.SemaphoreType.DMA],
         10 * 2**20,
         "project_last",
     )
 
 
-def combine_kernel(layers, picks, last_full, mate_full, got_mate, got_last, *refs):
-    outs = refs[-len(picks) :]
-    _, same = standing(layers)
+def combine_kernel(layers, order, picks, count, last_full, mate_full, got_mate, *refs):
+    gots, outs = refs[:count], refs[-len(picks) :]
+    same = standing(layers)
     cols = last_full.shape[2]
-    for k, r in enumerate(picks):
+    for out, r in zip(outs, picks):
         @pl.when(same)
         def _():
             got = got_mate[:, r * cols : (r + 1) * cols].astype(F32)
-            outs[k][...] = (mate_full[r] + got).astype(BF16)
+            out[...] = (mate_full[r] + got).astype(BF16)
 
         @pl.when(jnp.logical_not(same))
         def _():
-            got = got_last[:, k * cols : (k + 1) * cols].astype(F32)
-            outs[k][...] = (last_full[k] + got).astype(BF16)
-
-
-def combine(layers, picks, last_full, mate_full, got_mate, got_last, after):
+            start, begin = order.index(r) * cols, 0
+            for got in gots:
+                lo, hi = max(start, begin), min(start + cols, begin + got.shape[1])
+                if lo < hi:
+                    part = got[:, lo - begin : hi - begin].astype(F32)
+                    total = last_full[r, :, lo - start : hi - start] + part
+                    out[:, lo - start : hi - start] = total.astype(BF16)
+                begin += got.shape[1]
+
+
+def combine(layers, order, picks, last_full, mate_full, got_mate, gots, after):
     _, tokens, cols = last_full.shape
     vmem = pl.BlockSpec(memory_space=pltpu.VMEM)
     return pl.pallas_call(
-        functools.partial(combine_kernel, layers, picks),
-        in_specs=[vmem] * 4 + [pl.BlockSpec(memory_space=pltpu.HBM)] * len(after),
+        functools.partial(combine_kernel, layers, order, picks, len(gots)),
+        in_specs=[vmem] * (3 + len(gots)) + [pl.BlockSpec(memory_space=pltpu.HBM)] * len(after),
         out_specs=[vmem] * len(picks),
         out_shape=[jax.ShapeDtypeStruct((tokens, cols), BF16)] * len(picks),
         compiler_params=pltpu.CompilerParams(vmem_limit_bytes=12 * 2**20),
         cost_estimate=pl.CostEstimate(flops=1, transcendentals=0, bytes_accessed=1),
         name="combine",
-    )(last_full, mate_full, got_mate, got_last, *after)
+    )(last_full, mate_full, got_mate, *gots, *after)
 
 
 def place_kernel(layers, tasks, *refs):
@@ -382,7 +390,7 @@
         out[...] = refs[-2][...]
     seq = lax.axis_index("seq")
     layer, inner = seq // INNER, seq % INNER
-    _, same = standing(layers)
+    same = standing(layers)
     lower = layer // (layers // 2) == 0
     first_low = jnp.where(same, layer % 2 == 0, lower)
     for i in range(INNER):
@@ -462,26 +470,56 @@
     )(array, *deps)
 
 
-def join_kernel(dq, own, near, far, *refs):
+def is_odd():
+    return lax.axis_index("seq") % 2 == 1
+
+
+def choose_kernel(odd_ref, even_ref, out):
+    @pl.when(is_odd())
+    def _():
+        out[...] = odd_ref[...]
+
+    @pl.when(jnp.logical_not(is_odd()))
+    def _():
+        out[...] = even_ref[...]
+
+
+def merge_kernel(far, got, *refs):
+    out = refs[-1]
+    out[...] = far[...]
+
+    @pl.when(is_odd())
+    def _():
+        out[...] = (far[...].astype(F32) + got[...].astype(F32)).astype(BF16)
+
+
+def join_kernel(dq, own, got, back, *refs):
     out = refs[-1]
     width = dq.shape[1]
     out[:, :width] = dq[...]
-    out[:, width:] = (own[...] + near[...].astype(F32) + far[...].astype(F32)).astype(BF16)
-
-
-def join(dq, own, near, far, deps):
-    tokens, width = dq.shape
+    total = own[...] + back[...].astype(F32)
+
+    @pl.when(is_odd())
+    def _():
+        out[:, width:] = total.astype(BF16)
+
+    @pl.when(jnp.logical_not(is_odd()))
+    def _():
+        out[:, width:] = (total + got[...].astype(F32)).astype(BF16)
+
+
+def small(kernel, arrays, deps, width, name, limit=6 * 2**20, cost=1):
     vmem = pl.BlockSpec(memory_space=pltpu.VMEM)
     hbm = pl.BlockSpec(memory_space=pltpu.HBM)
     return pl.pallas_call(
-        join_kernel,
-        in_specs=[vmem] * 4 + [hbm] * len(deps),
+        kernel,
+        in_specs=[vmem] * len(arrays) + [hbm] * len(deps),
         out_specs=vmem,
-        out_shape=jax.ShapeDtypeStruct((tokens, width + own.shape[1]), BF16),
-        compiler_params=pltpu.CompilerParams(vmem_limit_bytes=JOIN_LIMIT),
-        cost_estimate=pl.CostEstimate(flops=2 * 10**9, transcendentals=0, bytes_accessed=1),
-        name="join",
-    )(dq, own, near, far, *deps)
+        out_shape=jax.ShapeDtypeStruct((arrays[0].shape[0], width), BF16),
+        compiler_params=pltpu.CompilerParams(vmem_limit_bytes=limit),
+        cost_estimate=pl.CostEstimate(flops=cost, transcendentals=0, bytes_accessed=1),
+        name=name,
+    )(*arrays, *deps)
 
 
 def shifted(array, by):
@@ -562,29 +600,34 @@
         pair = jnp.concatenate([key, value], 1)
         weight = jnp.concatenate([w_query, key_weight, value_weight], 1)
     pair_width = pair.shape[1]
-    near = shifted(pair, 1)
     far = shifted(pair, 2)
+    near = swapped(small(choose_kernel, [far, pair], [], pair.shape[1], "choose"), 1)
     if line:
-        mate = layered(weight, [(0, 1), (1, 0), (2, 3), (3, 2)])
-        mid = layered(weight, [(1, 2), (2, 1)])
-        third = layered(mid, [(1, 0), (2, 3)])
-        fourth = layered(mate, [(1, 2), (2, 1)])
+        up = layered(weight, [(0, 1), (1, 2), (2, 3)])
+        down = layered(weight, [(1, 0), (2, 1), (3, 2)])
     first = (seq * tokens).astype(jnp.int32).reshape(1)
     groups = key.shape[1] // HEAD_SIZE
     dq, earlier = [], []
     for g in range(groups):
         dq_part, *parts = attention(
-            g, (4 if g else 24) * 10**9, first, doc_lengths, query, output_gradient, output, lse,
+            g, ATTENTION_COST, first, doc_lengths, query, output_gradient, output, lse,
             pair, near, far, earlier,
         )
         dq.append(dq_part)
         earlier += parts
     own_part, near_part, far_part = parts
     dq_y = [swapped(part, 2) for part in dq[:-1]]
-    back_near = shifted(near_part, -1)
-    back_far = shifted(far_part, -2)
-    deps = [mate, mid, *dq_y] if line else []
-    joined = join(dq[-1], own_part, back_near, back_far, deps)
+    if line:
+        down = gate(down, dq_y)
+        up_on = layered(up, [(1, 2), (2, 3)])
+        down_on = layered(down, [(1, 0), (2, 1)])
+    got = swapped(near_part, 1)
+    back = shifted(small(merge_kernel, [far_part, got], [], pair.shape[1], "merge"), -2)
+    deps = [up, down] if line else []
+    width = dq[-1].shape[1] + pair.shape[1]
+    joined = small(
+        join_kernel, [dq[-1], own_part, got, back], deps, width, "join", VMEM_LIMIT, JOIN_COST
+    )
     joined_y = swapped(joined, 2)
     grads = [*dq[:-1], joined, *dq_y, joined_y]
     others = [swapped(g, 1) for g in grads]
@@ -598,26 +641,25 @@
         return project_gathered(four, weight, layers, tokens, head, inner)
 
     early = [o for o, g in zip(others, grads) if g is not joined and g is not joined_y]
-    weight = gate(weight, [third, fourth, joined_y, *early])
+    weight = gate(weight, [up_on, down_on, joined_y, *early])
     last = layered(weight, [(0, 3), (3, 0)])
-    send, held = project_send(layers, grads, weight, third, mid)
+    mate, third = [down, up, down, up], [down_on, down, up, up_on]
+    late = [last, down_on, up_on, last]
+    send, held = project_send(layers, grads, weight, third)
     got = lax.ppermute(send, "head", [(0, 1), (1, 0)])
-    keep, mate_full, mate_low = project_keep(layers, held, weight, mate, third, mid, [send])
+    keep, mate_full, mate_low = project_keep(layers, held, weight, mate, third, [send])
     got_mate = crossed(mate_low, layers, True)
-    parts = ((1, 3), (0, 2))
-    outs = project_last(parts, layers, held, last, fourth, [got])
-    halves = [
-        (picks, outs[2 * i], crossed(outs[2 * i + 1], layers, False))
-        for i, picks in enumerate(parts)
-    ]
+    order = (1, 3, 0, 2)
+    last_full, *lows = project_last(order, layers, held, late, [got])
+    gots = [crossed(low, layers, False) for low in lows]
 
     def lanes(array, k):
         return array[:, k * rows : (k + 1) * rows].astype(F32)
 
     sets = [returned([(keep[r] + lanes(got, r)).astype(BF16) for r in range(INNER)])]
     blocks, after = [None] * INNER, sets[0][1:]
-    for picks, full, got_last in halves:
-        after = combine(layers, picks, full, mate_full, got_mate, got_last, after)
+    for k, picks in enumerate((order[:2], order[2:])):
+        after = combine(layers, order, picks, last_full, mate_full, got_mate, gots[: k + 1], after)
         for r, block in zip(picks, after):
             blocks[r] = block
     sets.append(returned(blocks))

time: 120 us -> 119 us (level)
  starting transfers between devices: 44.6 us -> 38 us
  waiting for transfers between devices: 38 us -> 40.7 us
  local copies, waits for them, and re-layouts: 1.67 us -> 3.49 us
    ppermute x12 -> x14, waiting for transfers between devices: 21.5 us -> 28.8 us  [swapped(): return lax.ppermute(array, 'seq', [(i, i ^ bits) for i in range(peers)])]
    ppermute x12 -> x14, starting transfers between devices: 15.1 us -> 8.59 us  [swapped(): return lax.ppermute(array, 'seq', [(i, i ^ bits) for i in range(peers)])]
    ppermute x5, waiting for transfers between devices: 10.6 us -> 7 us  [layered(): return lax.ppermute(array, 'seq', pairs)]
    ppermute x4 -> x2, starting transfers between devices: 8.93 us -> 6.18 us  [shifted(): return lax.ppermute(array, 'seq', pairs)]
    ppermute x5, starting transfers between devices: 12.6 us -> 15.4 us  [layered(): return lax.ppermute(array, 'seq', pairs)]
    unnamed x22, local copies, waits for them, and re-layouts: 1.67 us -> 3.49 us
    pallas_call x3 -> x5, Pallas kernels: 2.7 us -> 2.76 us  [the longest x3 2.35 us: small(): pl.pallas_call(kernel, in_specs=[vmem] * len(arrays) + [hbm] * len(deps),...]
    ppermute x4 -> x2, waiting for transfers between devices: 4.53 us -> 4.5 us  [shifted(): return lax.ppermute(array, 'seq', pairs)]
  transfers between devices with their start and end apart: 25 -> 25, of which waited for: 11 -> 13; matrix products, arithmetic and copies ran while one was open for 0% -> 0% of each run, Pallas kernels for 26% -> 27%
where the time goes in v4:
time: 119 us; the launch traced here: 118 us
  waiting for transfers between devices  40.7 us (34%)
  starting transfers between devices  38 us (32%)
  Pallas kernels  35.4 us (30%)
  local copies, waits for them, and re-layouts  3.49 us (3%)
    ppermute x14, waiting for transfers between devices, swapped(): return lax.ppermute(array, 'seq', [(i, i ^ bits) for i in range(peers)])  28.8 us
    pallas_call x3, Pallas kernels, project(): pl.pallas_call(functools.partial(kernel, layers), in_specs=[vmem] * in_vm...  16.8 us
    ppermute x5, starting transfers between devices, layered(): return lax.ppermute(array, 'seq', pairs)  15.4 us
    pallas_call x2, Pallas kernels, attention(): pl.pallas_call(functools.partial(attention_kernel, group, groups), grid=(...  12.1 us
    ppermute x14, starting transfers between devices, swapped(): return lax.ppermute(array, 'seq', [(i, i ^ bits) for i in range(peers)])  8.59 us
    ppermute x5, waiting for transfers between devices, layered(): return lax.ppermute(array, 'seq', pairs)  7 us
    ppermute x3, starting transfers between devices, crossed(): return lax.ppermute(array, ('seq', 'head'), pairs)  6.3 us
    ppermute x2, starting transfers between devices, shifted(): return lax.ppermute(array, 'seq', pairs)  6.18 us
  transfers between devices with their start and end apart: 25, of which 13 were waited for; matrix products, arithmetic and copies ran while one was open for 0% of the time, Pallas kernels for 27%

profile of v4, /device:TPU:0, one launch (start us, length us, event | category | flops | bytes accessed | tf_op | source)
XLA Modules:
  0.0 118.0 jit_solution(2224059329862768490)
XLA Ops:
  0.0 2.4 %pack.1 = (bf16[256,512]{1,0:T(8,128)(2,1)}, bf16[224,2304]{1,0:T(8,128)(2,1)}) custom-call(bf16[256,256]{1,0:T(8,128)(2,1)} %refs_0_.1, bf16[256,256]{1,0:T(8,128)(2,1)} %refs_1_.1, bf16[224,1792]{1,0:T(8,128)(2,1)} %refs_2_.1, bf16[224,256]{1,0:T(8,128)(2,1)} %refs_3_.1, bf16[224,256]{1,0:T(8,128)(2,1)} %refs_4_.1), custom_call_target="tpu_custom_call" | custom-call | flops 1 | bytes 1 | tf_op jit(solution)/shard_map/pack/pallas_call | solution.py:440
  2.4 4.9 %collective-permute-start = (bf16[256,512]{1,0:T(8,128)(2,1)}, bf16[256,512]{1,0:T(8,128)(2,1)S(1)}, u32[]{:S(2)}, u32[]{:S(2)}) collective-permute-start(bf16[256,512]{1,0:T(8,128)(2,1)} %get-tuple-element.27.even_ref.k_own_ref.v_own_ref), channel_id=1, source_target_pairs={{0,4},{2,6},{4,8},{6,10},{8,12},{10,14},{12,16},{14,18},{16,20},{1... | collective-permute-start | bytes 786440 | tf_op jit(solution)/shard_map/ppermute | solution.py:528
  7.3 1.3 %collective-permute-start.5 = (bf16[224,2304]{1,0:T(8,128)(2,1)}, bf16[224,2304]{1,0:T(8,128)(2,1)}, u32[]{:S(2)}, u32[]{:S(2)}) collective-permute-start(bf16[224,2304]{1,0:T(8,128)(2,1)} %get-tuple-element.36.refs_0_), channel_id=1, source_target_pairs={{8,0},{10,2},{12,4},{14,6},{16,8},{18,10},{20,12},{22,14},{24,16},... | collective-permute-start | bytes 3096584 | tf_op jit(solution)/shard_map/ppermute | solution.py:538
  8.6 5.5 %collective-permute-start.4 = (bf16[224,2304]{1,0:T(8,128)(2,1)}, bf16[224,2304]{1,0:T(8,128)(2,1)}, u32[]{:S(2)}, u32[]{:S(2)}) collective-permute-start(bf16[224,2304]{1,0:T(8,128)(2,1)} %get-tuple-element.36.refs_0_), channel_id=1, source_target_pairs={{0,8},{2,10},{4,12},{6,14},{8,16},{10,18},{12,20},{14,22},{16,24},... | collective-permute-start | bytes 3096584 | tf_op jit(solution)/shard_map/ppermute | solution.py:538
  15.2 1.5 %collective-permute-done.1.k_near_ref.v_near_ref = bf16[256,512]{1,0:T(8,128)(2,1)S(1)} collective-permute-done((bf16[256,512]{1,0:T(8,128)(2,1)S(1)}, bf16[256,512]{1,0:T(8,128)(2,1)S(1)}, u32[]{:S(2)}, u32[]{:S(2)}) %collective-permute-start.1) | collective-permute-done | bytes 262176 | tf_op jit(solution)/shard_map/ppermute | solution.py:533
  17.4 5.8 %attention.2 = (bf16[256,896]{1,0:T(8,128)(2,1)}, f32[256,256]{1,0:T(8,128)}, bf16[256,256]{1,0:T(8,128)(2,1)}, bf16[256,256]{1,0:T(8,128)(2,1)}) custom-call(s32[1]{0:T(128)} %bitcast.first_ref, s32[4]{0:T(128)} %docs_ref.3, bf16[256,1792]{1,0:T(8,128)(2,1)} %q_ref.3, bf16[256,1792]{1,0:T(8,128)(2,1)} %do_ref.3, bf16[256,1792]{1,0:T(8,128)(2,1)} %o_ref.3, ...), custom_call_target="tpu_custom_call" | custom-call | flops 900000000 | bytes 1 | tf_op jit(solution)/shard_map/attention/pallas_call | solution.py:131
  23.2 1.5 %collective-permute-start.6 = (bf16[256,896]{1,0:T(8,128)(2,1)}, bf16[256,896]{1,0:T(8,128)(2,1)S(1)}, u32[]{:S(2)}, u32[]{:S(2)}) collective-permute-start(bf16[256,896]{1,0:T(8,128)(2,1)} %get-tuple-element.28.refs_0_), channel_id=1, source_target_pairs={{0,4},{2,6},{4,0},{6,2},{8,12},{10,14},{12,8},{14,10},{16,20},{18,... | collective-permute-start | bytes 1376264 | tf_op jit(solution)/shard_map/ppermute | solution.py:533
  24.7 6.3 %attention.3 = (bf16[256,896]{1,0:T(8,128)(2,1)}, f32[256,512]{1,0:T(8,128)}, bf16[256,512]{1,0:T(8,128)(2,1)}, bf16[256,512]{1,0:T(8,128)(2,1)}) custom-call(s32[1]{0:T(128)} %bitcast.first_ref, s32[4]{0:T(128)} %docs_ref.3, bf16[256,1792]{1,0:T(8,128)(2,1)} %q_ref.3, bf16[256,1792]{1,0:T(8,128)(2,1)} %do_ref.3, bf16[256,1792]{1,0:T(8,128)(2,1)} %o_ref.3, ...), custom_call_target="tpu_custom_call" | custom-call | flops 900000000 | bytes 1 | tf_op jit(solution)/shard_map/attention/pallas_call | solution.py:131
  31.0 1.7 %collective-permute-done.2.got = bf16[256,512]{1,0:T(8,128)(2,1)S(1)} collective-permute-done((bf16[256,512]{1,0:T(8,128)(2,1)}, bf16[256,512]{1,0:T(8,128)(2,1)S(1)}, u32[]{:S(2)}, u32[]{:S(2)}) %collective-permute-start.2) | collective-permute-done | bytes 262176 | tf_op jit(solution)/shard_map/ppermute | solution.py:533
  33.8 1.3 %collective-permute-start.3 = (bf16[256,512]{1,0:T(8,128)(2,1)S(1)}, bf16[256,512]{1,0:T(8,128)(2,1)}, u32[]{:S(2)}, u32[]{:S(2)}) collective-permute-start(bf16[256,512]{1,0:T(8,128)(2,1)S(1)} %merge.1), channel_id=1, source_target_pairs={{4,0},{6,2},{8,4},{10,6},{12,8},{14,10},{16,12},{18,14},{20,16},{2... | collective-permute-start | bytes 786440 | tf_op jit(solution)/shard_map/ppermute | solution.py:528
  36.8 1.3 %collective-permute-start.13 = (bf16[224,2304]{1,0:T(8,128)(2,1)}, bf16[224,2304]{1,0:T(8,128)(2,1)}, u32[]{:S(2)}, u32[]{:S(2)}) collective-permute-start(bf16[224,2304]{1,0:T(8,128)(2,1)} %gate.2.refs_1_.refs_10_.refs_0_.refs_2_.refs_5_), channel_id=1, source_target_pairs={{8,0},{10,2},{12,4},{14,6},{16,8},{18,10},{20,12},{22,14},{9,1},{1... | collective-permute-start | bytes 3096584 | tf_op jit(solution)/shard_map/ppermute | solution.py:538
  38.1 1.6 %collective-permute-start.12 = (bf16[224,2304]{1,0:T(8,128)(2,1)}, bf16[224,2304]{1,0:T(8,128)(2,1)}, u32[]{:S(2)}, u32[]{:S(2)}) collective-permute-start(bf16[224,2304]{1,0:T(8,128)(2,1)} %collective-permute-done.4.refs_0_.refs_11_.refs_1_.refs_3_.refs_6_), channel_id=1, source_target_pairs={{8,16},{10,18},{12,20},{14,22},{16,24},{18,26},{20,28},{22,30},{9,... | collective-permute-start | bytes 3096584 | tf_op jit(solution)/shard_map/ppermute | solution.py:538
  39.7 4.5 %collective-permute-done.3.back = bf16[256,512]{1,0:T(8,128)(2,1)} collective-permute-done((bf16[256,512]{1,0:T(8,128)(2,1)S(1)}, bf16[256,512]{1,0:T(8,128)(2,1)}, u32[]{:S(2)}, u32[]{:S(2)}) %collective-permute-start.3) | collective-permute-done | bytes 262176 | tf_op jit(solution)/shard_map/ppermute | solution.py:528
  44.2 2.3 %join.1.refs_1_ = bf16[256,1408]{1,0:T(8,128)(2,1)} custom-call(bf16[256,896]{1,0:T(8,128)(2,1)} %get-tuple-element.32.dq, f32[256,512]{1,0:T(8,128)} %get-tuple-element.33.own, bf16[256,512]{1,0:T(8,128)(2,1)} %copy-done.4, bf16[256,512]{1,0:T(8,128)(2,1)} %collective-permute-done.3.back, ...), custom_call_target="tpu_custom_call" | custom-call | flops 1000000000 | bytes 1 | tf_op jit(solution)/shard_map/join/pallas_call | solution.py:514
  46.6 2.2 %collective-permute-start.7 = (bf16[256,1408]{1,0:T(8,128)(2,1)}, bf16[256,1408]{1,0:T(8,128)(2,1)S(1)}, u32[]{:S(2)}, u32[]{:S(2)}) collective-permute-start(bf16[256,1408]{1,0:T(8,128)(2,1)} %join.1.refs_1_), channel_id=1, source_target_pairs={{0,4},{2,6},{4,0},{6,2},{8,12},{10,14},{12,8},{14,10},{16,20},{18,... | collective-permute-start | bytes 2162696 | tf_op jit(solution)/shard_map/ppermute | solution.py:533
  49.2 2.1 %collective-permute-done.8.refs_4_ = bf16[256,896]{1,0:T(8,128)(2,1)S(1)} collective-permute-done((bf16[256,896]{1,0:T(8,128)(2,1)}, bf16[256,896]{1,0:T(8,128)(2,1)S(1)}, u32[]{:S(2)}, u32[]{:S(2)}) %collective-permute-start.8) | collective-permute-done | bytes 458784 | tf_op jit(solution)/shard_map/ppermute | solution.py:533
  51.5 12.6 %collective-permute-done.7.refs_3_ = bf16[256,1408]{1,0:T(8,128)(2,1)S(1)} collective-permute-done((bf16[256,1408]{1,0:T(8,128)(2,1)}, bf16[256,1408]{1,0:T(8,128)(2,1)S(1)}, u32[]{:S(2)}, u32[]{:S(2)}) %collective-permute-start.7) | collective-permute-done | bytes 720928 | tf_op jit(solution)/shard_map/ppermute | solution.py:533
  64.2 2.1 %collective-permute-done.13.refs_2_.refs_9_.refs_1_.refs_4_ = bf16[224,2304]{1,0:T(8,128)(2,1)} collective-permute-done((bf16[224,2304]{1,0:T(8,128)(2,1)}, bf16[224,2304]{1,0:T(8,128)(2,1)}, u32[]{:S(2)}, u32[]{:S(2)}) %collective-permute-start.13) | collective-permute-done | bytes 1032224 | tf_op jit(solution)/shard_map/ppermute | solution.py:538
  66.3 5.6 %collective-permute-start.14 = (bf16[224,2304]{1,0:T(8,128)(2,1)}, bf16[224,2304]{1,0:T(8,128)(2,1)}, u32[]{:S(2)}, u32[]{:S(2)}) collective-permute-start(bf16[224,2304]{1,0:T(8,128)(2,1)} %gate.3.refs_8_.own), channel_id=1, source_target_pairs={{0,24},{2,26},{4,28},{6,30},{24,0},{26,2},{28,4},{30,6},{1,25},{3,... | collective-permute-start | bytes 3096584 | tf_op jit(solution)/shard_map/ppermute | solution.py:538
  72.0 6.1 %project_send.1 = (bf16[256,896]{1,0:T(8,128)(2,1)}, bf16[1024,2304]{1,0:T(8,128)(2,1)}) custom-call(bf16[256,896]{1,0:T(8,128)(2,1)} %get-tuple-element.28.refs_0_, bf16[256,1408]{1,0:T(8,128)(2,1)} %join.1.refs_1_, bf16[256,896]{1,0:T(8,128)(2,1)} %copy-done.9, bf16[256,1408]{1,0:T(8,128)(2,1)} %copy-done.7, bf16[256,896]{1,0:T(8,128)(2,1)} %copy-done.8, ...), custom_call_target="tpu_custom_call" | custom-call | flops 1 | bytes 1 | tf_op jit(solution)/shard_map/project_send/pallas_call | solution.py:284
  78.1 1.6 %collective-permute-start.15 = (bf16[256,896]{1,0:T(8,128)(2,1)}, bf16[256,896]{1,0:T(8,128)(2,1)S(1)}, u32[]{:S(2)}, u32[]{:S(2)}) collective-permute-start(bf16[256,896]{1,0:T(8,128)(2,1)} %get-tuple-element.38.refs_8_), channel_id=1, source_target_pairs={{0,1},{1,0},{2,3},{3,2},{4,5},{5,4},{6,7},{7,6},{8,9},{9,8},{10,11... | collective-permute-start | bytes 1376264 | tf_op jit(solution)/shard_map/ppermute | solution.py:649
  79.7 7.9 %project_keep.1 = (f32[4,256,224]{2,1,0:T(8,128)}, f32[4,256,224]{2,1,0:T(8,128)}, bf16[256,896]{1,0:T(8,128)(2,1)}) custom-call(bf16[1024,2304]{1,0:T(8,128)(2,1)} %get-tuple-element.37.held, bf16[224,2304]{1,0:T(8,128)(2,1)} %gate.3.refs_8_.own, bf16[224,2304]{1,0:T(8,128)(2,1)} %gate.2.refs_1_.refs_10_.refs_0_.refs_2_.refs_5_, ...), custom_call_target="tpu_custom_call" | custom-call | flops 1 | bytes 1 | tf_op jit(solution)/shard_map/project_keep/pallas_call | solution.py:284
  87.6 1.6 %collective-permute-start.16 = (bf16[256,896]{1,0:T(8,128)(2,1)}, bf16[256,896]{1,0:T(8,128)(2,1)S(1)}, u32[]{:S(2)}, u32[]{:S(2)}) collective-permute-start(bf16[256,896]{1,0:T(8,128)(2,1)} %get-tuple-element.41), channel_id=1, source_target_pairs={{1,0},{3,2},{5,4},{7,6},{9,8},{11,10},{13,12},{15,14},{16,17},{18,... | collective-permute-start | bytes 1376264 | tf_op jit(solution)/shard_map/ppermute | solution.py:546
  89.6 4.8 %collective-permute-done.14.refs_0_.refs_3_ = bf16[224,2304]{1,0:T(8,128)(2,1)} collective-permute-done((bf16[224,2304]{1,0:T(8,128)(2,1)}, bf16[224,2304]{1,0:T(8,128)(2,1)}, u32[]{:S(2)}, u32[]{:S(2)}) %collective-permute-start.14) | collective-permute-done | bytes 1032224 | tf_op jit(solution)/shard_map/ppermute | solution.py:538
  94.4 2.7 %project_last.1 = (f32[4,256,224]{2,1,0:T(8,128)S(1)}, bf16[256,512]{1,0:T(8,128)(2,1)S(1)}, bf16[256,384]{1,0:T(8,128)(2,1)S(1)}) custom-call(bf16[1024,2304]{1,0:T(8,128)(2,1)S(1)} %copy-done, bf16[224,2304]{1,0:T(8,128)(2,1)} %collective-permute-done.14.refs_0_.refs_3_, bf16[224,2304]{1,0:T(8,128)(2,1)} %collective-permute-done.13.refs_2_.refs_9_.refs_1_.refs_4_, ...), custom_call_target="tpu_custom_call" | custom-call | flops 1 | bytes 1 | tf_op jit(solution)/shard_map/project_last/pallas_call | solution.py:284
  97.2 3.4 %collective-permute-start.17 = (bf16[256,512]{1,0:T(8,128)(2,1)S(1)}, bf16[256,512]{1,0:T(8,128)(2,1)S(1)}, u32[]{:S(2)}, u32[]{:S(2)}) collective-permute-start(bf16[256,512]{1,0:T(8,128)(2,1)S(1)} %get-tuple-element.42), channel_id=1, source_target_pairs={{0,1},{2,3},{4,5},{6,7},{8,9},{10,11},{12,13},{14,15},{17,16},{19,... | collective-permute-start | bytes 786440 | tf_op jit(solution)/shard_map/ppermute | solution.py:546
  102.7 1.3 %collective-permute-start.18 = (bf16[256,384]{1,0:T(8,128)(2,1)S(1)}, bf16[256,384]{1,0:T(8,128)(2,1)S(1)}, u32[]{:S(2)}, u32[]{:S(2)}) collective-permute-start(bf16[256,384]{1,0:T(8,128)(2,1)S(1)} %get-tuple-element.43), channel_id=1, source_target_pairs={{0,1},{2,3},{4,5},{6,7},{8,9},{10,11},{12,13},{14,15},{17,16},{19,... | collective-permute-start | bytes 589832 | tf_op jit(solution)/shard_map/ppermute | solution.py:546
  104.0 2.5 %collective-permute-done.21.refs_3_ = bf16[256,224]{1,0:T(8,128)(2,1)S(1)} collective-permute-done((bf16[256,224]{1,0:T(8,128)(2,1)S(1)}, bf16[256,224]{1,0:T(8,128)(2,1)S(1)}, u32[]{:S(2)}, u32[]{:S(2)}) %collective-permute-start.21) | collective-permute-done | bytes 114720 | tf_op jit(solution)/shard_map/ppermute | solution.py:533
  106.6 2.1 %collective-permute-done.20.refs_2_ = bf16[256,224]{1,0:T(8,128)(2,1)S(1)} collective-permute-done((bf16[256,224]{1,0:T(8,128)(2,1)S(1)}, bf16[256,224]{1,0:T(8,128)(2,1)S(1)}, u32[]{:S(2)}, u32[]{:S(2)}) %collective-permute-start.20) | collective-permute-done | bytes 114720 | tf_op jit(solution)/shard_map/ppermute | solution.py:533
  111.4 4.0 %collective-permute-done.23.refs_4_ = bf16[256,224]{1,0:T(8,128)(2,1)S(1)} collective-permute-done((bf16[256,224]{1,0:T(8,128)(2,1)S(1)}, bf16[256,224]{1,0:T(8,128)(2,1)S(1)}, u32[]{:S(2)}, u32[]{:S(2)}) %collective-permute-start.23) | collective-permute-done | bytes 114720 | tf_op jit(solution)/shard_map/ppermute | solution.py:533
  115.4 1.2 %collective-permute-done.24.refs_5_ = bf16[256,224]{1,0:T(8,128)(2,1)S(1)} collective-permute-done((bf16[256,224]{1,0:T(8,128)(2,1)S(1)}, bf16[256,224]{1,0:T(8,128)(2,1)S(1)}, u32[]{:S(2)}, u32[]{:S(2)}) %collective-permute-start.24) | collective-permute-done | bytes 114720 | tf_op jit(solution)/shard_map/ppermute | solution.py:533
  116.9 1.1 place.3
  (56 shorter events, 10.6 us)
Async XLA Ops:
  2.4 11.7 %collective-permute-start = (bf16[256,512]{1,0:T(8,128)(2,1)}, bf16[256,512]{1,0:T(8,128)(2,1)S(1)}, u32[]{:S(2)}, u32[]{:S(2)}) collective-permute-start(bf16[256,512]{1,0:T(8,128)(2,1)} %get-tuple-element.27.even_ref.k_own_ref.v_own_ref), channel_id=1, source_target_pairs={{0,4},{2,6},{4,8},{6,10},{8,12},{10,14},{12,16},{14,18},{16,20},{1... | collective-permute-start | bytes 786440 | tf_op jit(solution)/shard_map/ppermute | solution.py:528
  7.3 28.7 %collective-permute-start.5 = (bf16[224,2304]{1,0:T(8,128)(2,1)}, bf16[224,2304]{1,0:T(8,128)(2,1)}, u32[]{:S(2)}, u32[]{:S(2)}) collective-permute-start(bf16[224,2304]{1,0:T(8,128)(2,1)} %get-tuple-element.36.refs_0_), channel_id=1, source_target_pairs={{8,0},{10,2},{12,4},{14,6},{16,8},{18,10},{20,12},{22,14},{24,16},... | collective-permute-start | bytes 3096584 | tf_op jit(solution)/shard_map/ppermute | solution.py:538
  8.6 29.5 %collective-permute-start.4 = (bf16[224,2304]{1,0:T(8,128)(2,1)}, bf16[224,2304]{1,0:T(8,128)(2,1)}, u32[]{:S(2)}, u32[]{:S(2)}) collective-permute-start(bf16[224,2304]{1,0:T(8,128)(2,1)} %get-tuple-element.36.refs_0_), channel_id=1, source_target_pairs={{0,8},{2,10},{4,12},{6,14},{8,16},{10,18},{12,20},{14,22},{16,24},... | collective-permute-start | bytes 3096584 | tf_op jit(solution)/shard_map/ppermute | solution.py:538
  15.1 1.6 %copy-start.2 = (bf16[256,512]{1,0:T(8,128)(2,1)}, bf16[256,512]{1,0:T(8,128)(2,1)S(1)}, u32[]{:S(2)}) copy-start(bf16[256,512]{1,0:T(8,128)(2,1)S(1)} %collective-permute-done.odd_ref.k_far_ref.v_far_ref) | copy-start | bytes 786436
  15.1 1.6 %collective-permute-start.1 = (bf16[256,512]{1,0:T(8,128)(2,1)S(1)}, bf16[256,512]{1,0:T(8,128)(2,1)S(1)}, u32[]{:S(2)}, u32[]{:S(2)}) collective-permute-start(bf16[256,512]{1,0:T(8,128)(2,1)S(1)} %choose.1), channel_id=1, source_target_pairs={{0,2},{2,0},{4,6},{6,4},{8,10},{10,8},{12,14},{14,12},{16,18},{18,... | collective-permute-start | bytes 786440 | tf_op jit(solution)/shard_map/ppermute | solution.py:533
  23.2 12.8 %collective-permute-start.6 = (bf16[256,896]{1,0:T(8,128)(2,1)}, bf16[256,896]{1,0:T(8,128)(2,1)S(1)}, u32[]{:S(2)}, u32[]{:S(2)}) collective-permute-start(bf16[256,896]{1,0:T(8,128)(2,1)} %get-tuple-element.28.refs_0_), channel_id=1, source_target_pairs={{0,4},{2,6},{4,0},{6,2},{8,12},{10,14},{12,8},{14,10},{16,20},{18,... | collective-permute-start | bytes 1376264 | tf_op jit(solution)/shard_map/ppermute | solution.py:533
  31.0 1.7 %collective-permute-start.2 = (bf16[256,512]{1,0:T(8,128)(2,1)}, bf16[256,512]{1,0:T(8,128)(2,1)S(1)}, u32[]{:S(2)}, u32[]{:S(2)}) collective-permute-start(bf16[256,512]{1,0:T(8,128)(2,1)} %get-tuple-element.34), channel_id=1, source_target_pairs={{0,2},{2,0},{4,6},{6,4},{8,10},{10,8},{12,14},{14,12},{16,18},{18,... | collective-permute-start | bytes 786440 | tf_op jit(solution)/shard_map/ppermute | solution.py:533
  32.8 11.5 %copy-start.4 = (bf16[256,512]{1,0:T(8,128)(2,1)}, bf16[256,512]{1,0:T(8,128)(2,1)S(1)}, u32[]{:S(2)}) copy-start(bf16[256,512]{1,0:T(8,128)(2,1)S(1)} %collective-permute-done.2.got) | copy-start | bytes 786436
  33.8 10.4 %collective-permute-start.3 = (bf16[256,512]{1,0:T(8,128)(2,1)S(1)}, bf16[256,512]{1,0:T(8,128)(2,1)}, u32[]{:S(2)}, u32[]{:S(2)}) collective-permute-start(bf16[256,512]{1,0:T(8,128)(2,1)S(1)} %merge.1), channel_id=1, source_target_pairs={{4,0},{6,2},{8,4},{10,6},{12,8},{14,10},{16,12},{18,14},{20,16},{2... | collective-permute-start | bytes 786440 | tf_op jit(solution)/shard_map/ppermute | solution.py:528
  36.8 29.5 %collective-permute-start.13 = (bf16[224,2304]{1,0:T(8,128)(2,1)}, bf16[224,2304]{1,0:T(8,128)(2,1)}, u32[]{:S(2)}, u32[]{:S(2)}) collective-permute-start(bf16[224,2304]{1,0:T(8,128)(2,1)} %gate.2.refs_1_.refs_10_.refs_0_.refs_2_.refs_5_), channel_id=1, source_target_pairs={{8,0},{10,2},{12,4},{14,6},{16,8},{18,10},{20,12},{22,14},{9,1},{1... | collective-permute-start | bytes 3096584 | tf_op jit(solution)/shard_map/ppermute | solution.py:538
  38.1 28.2 %collective-permute-start.12 = (bf16[224,2304]{1,0:T(8,128)(2,1)}, bf16[224,2304]{1,0:T(8,128)(2,1)}, u32[]{:S(2)}, u32[]{:S(2)}) collective-permute-start(bf16[224,2304]{1,0:T(8,128)(2,1)} %collective-permute-done.4.refs_0_.refs_11_.refs_1_.refs_3_.refs_6_), channel_id=1, source_target_pairs={{8,16},{10,18},{12,20},{14,22},{16,24},{18,26},{20,28},{22,30},{9,... | collective-permute-start | bytes 3096584 | tf_op jit(solution)/shard_map/ppermute | solution.py:538
  46.6 17.6 %collective-permute-start.7 = (bf16[256,1408]{1,0:T(8,128)(2,1)}, bf16[256,1408]{1,0:T(8,128)(2,1)S(1)}, u32[]{:S(2)}, u32[]{:S(2)}) collective-permute-start(bf16[256,1408]{1,0:T(8,128)(2,1)} %join.1.refs_1_), channel_id=1, source_target_pairs={{0,4},{2,6},{4,0},{6,2},{8,12},{10,14},{12,8},{14,10},{16,20},{18,... | collective-permute-start | bytes 2162696 | tf_op jit(solution)/shard_map/ppermute | solution.py:533
  48.7 2.7 %collective-permute-start.8 = (bf16[256,896]{1,0:T(8,128)(2,1)}, bf16[256,896]{1,0:T(8,128)(2,1)S(1)}, u32[]{:S(2)}, u32[]{:S(2)}) collective-permute-start(bf16[256,896]{1,0:T(8,128)(2,1)} %get-tuple-element.28.refs_0_), channel_id=1, source_target_pairs={{0,2},{2,0},{4,6},{6,4},{8,10},{10,8},{12,14},{14,12},{16,18},{18,... | collective-permute-start | bytes 1376264 | tf_op jit(solution)/shard_map/ppermute | solution.py:533
  48.7 15.4 %collective-permute-start.10 = (bf16[256,896]{1,0:T(8,128)(2,1)}, bf16[256,896]{1,0:T(8,128)(2,1)}, u32[]{:S(2)}, u32[]{:S(2)}) collective-permute-start(bf16[256,896]{1,0:T(8,128)(2,1)} %copy-done.9), channel_id=1, source_target_pairs={{0,2},{2,0},{4,6},{6,4},{8,10},{10,8},{12,14},{14,12},{16,18},{18,... | collective-permute-start | bytes 1376264 | tf_op jit(solution)/shard_map/ppermute | solution.py:533
  51.4 12.8 %copy-start.8 = (bf16[256,896]{1,0:T(8,128)(2,1)}, bf16[256,896]{1,0:T(8,128)(2,1)S(1)}, u32[]{:S(2)}) copy-start(bf16[256,896]{1,0:T(8,128)(2,1)S(1)} %collective-permute-done.8.refs_4_) | copy-start | bytes 1376260
  51.4 20.6 %collective-permute-start.9 = (bf16[256,1408]{1,0:T(8,128)(2,1)}, bf16[256,1408]{1,0:T(8,128)(2,1)}, u32[]{:S(2)}, u32[]{:S(2)}) collective-permute-start(bf16[256,1408]{1,0:T(8,128)(2,1)} %join.1.refs_1_), channel_id=1, source_target_pairs={{0,2},{2,0},{4,6},{6,4},{8,10},{10,8},{12,14},{14,12},{16,18},{18,... | collective-permute-start | bytes 2162696 | tf_op jit(solution)/shard_map/ppermute | solution.py:533
  64.2 2.2 %copy-start.7 = (bf16[256,1408]{1,0:T(8,128)(2,1)}, bf16[256,1408]{1,0:T(8,128)(2,1)S(1)}, u32[]{:S(2)}) copy-start(bf16[256,1408]{1,0:T(8,128)(2,1)S(1)} %collective-permute-done.7.refs_3_) | copy-start | bytes 2162692
  64.2 7.8 %collective-permute-start.11 = (bf16[256,1408]{1,0:T(8,128)(2,1)S(1)}, bf16[256,1408]{1,0:T(8,128)(2,1)}, u32[]{:S(2)}, u32[]{:S(2)}) collective-permute-start(bf16[256,1408]{1,0:T(8,128)(2,1)S(1)} %collective-permute-done.7.refs_3_), channel_id=1, source_target_pairs={{0,2},{2,0},{4,6},{6,4},{8,10},{10,8},{12,14},{14,12},{16,18},{18,... | collective-permute-start | bytes 2162696 | tf_op jit(solution)/shard_map/ppermute | solution.py:533
  66.3 28.1 %collective-permute-start.14 = (bf16[224,2304]{1,0:T(8,128)(2,1)}, bf16[224,2304]{1,0:T(8,128)(2,1)}, u32[]{:S(2)}, u32[]{:S(2)}) collective-permute-start(bf16[224,2304]{1,0:T(8,128)(2,1)} %gate.3.refs_8_.own), channel_id=1, source_target_pairs={{0,24},{2,26},{4,28},{6,30},{24,0},{26,2},{28,4},{30,6},{1,25},{3,... | collective-permute-start | bytes 3096584 | tf_op jit(solution)/shard_map/ppermute | solution.py:538
  78.1 11.5 %collective-permute-start.15 = (bf16[256,896]{1,0:T(8,128)(2,1)}, bf16[256,896]{1,0:T(8,128)(2,1)S(1)}, u32[]{:S(2)}, u32[]{:S(2)}) collective-permute-start(bf16[256,896]{1,0:T(8,128)(2,1)} %get-tuple-element.38.refs_8_), channel_id=1, source_target_pairs={{0,1},{1,0},{2,3},{3,2},{4,5},{5,4},{6,7},{7,6},{8,9},{9,8},{10,11... | collective-permute-start | bytes 1376264 | tf_op jit(solution)/shard_map/ppermute | solution.py:649
  79.7 14.8 %copy-start = (bf16[1024,2304]{1,0:T(8,128)(2,1)S(1)}, bf16[1024,2304]{1,0:T(8,128)(2,1)}, u32[]{:S(2)}) copy-start(bf16[1024,2304]{1,0:T(8,128)(2,1)} %get-tuple-element.37.held) | copy-start | bytes 14155780
  87.6 13.0 %copy-start.10 = (f32[4,256,224]{2,1,0:T(8,128)S(1)}, f32[4,256,224]{2,1,0:T(8,128)}, u32[]{:S(2)}) copy-start(f32[4,256,224]{2,1,0:T(8,128)} %get-tuple-element.44) | copy-start | bytes 2752516
  87.6 21.1 %copy-start.3 = (f32[4,256,224]{2,1,0:T(8,128)S(1)}, f32[4,256,224]{2,1,0:T(8,128)}, u32[]{:S(2)}) copy-start(f32[4,256,224]{2,1,0:T(8,128)} %get-tuple-element.40.mate_full) | copy-start | bytes 2752516
  87.6 15.1 %collective-permute-start.16 = (bf16[256,896]{1,0:T(8,128)(2,1)}, bf16[256,896]{1,0:T(8,128)(2,1)S(1)}, u32[]{:S(2)}, u32[]{:S(2)}) collective-permute-start(bf16[256,896]{1,0:T(8,128)(2,1)} %get-tuple-element.41), channel_id=1, source_target_pairs={{1,0},{3,2},{5,4},{7,6},{9,8},{11,10},{13,12},{15,14},{16,17},{18,... | collective-permute-start | bytes 1376264 | tf_op jit(solution)/shard_map/ppermute | solution.py:546
  97.2 11.6 %collective-permute-start.17 = (bf16[256,512]{1,0:T(8,128)(2,1)S(1)}, bf16[256,512]{1,0:T(8,128)(2,1)S(1)}, u32[]{:S(2)}, u32[]{:S(2)}) collective-permute-start(bf16[256,512]{1,0:T(8,128)(2,1)S(1)} %get-tuple-element.42), channel_id=1, source_target_pairs={{0,1},{2,3},{4,5},{6,7},{8,9},{10,11},{12,13},{14,15},{17,16},{19,... | collective-permute-start | bytes 786440 | tf_op jit(solution)/shard_map/ppermute | solution.py:546
  100.8 5.8 %collective-permute-start.21 = (bf16[256,224]{1,0:T(8,128)(2,1)S(1)}, bf16[256,224]{1,0:T(8,128)(2,1)S(1)}, u32[]{:S(2)}, u32[]{:S(2)}) collective-permute-start(bf16[256,224]{1,0:T(8,128)(2,1)S(1)} %get-tuple-element.50), channel_id=1, source_target_pairs={{0,6},{2,4},{4,2},{6,0},{8,14},{10,12},{12,10},{14,8},{16,22},{18,... | collective-permute-start | bytes 344072 | tf_op jit(solution)/shard_map/ppermute | solution.py:533
  100.9 7.8 %collective-permute-start.20 = (bf16[256,224]{1,0:T(8,128)(2,1)S(1)}, bf16[256,224]{1,0:T(8,128)(2,1)S(1)}, u32[]{:S(2)}, u32[]{:S(2)}) collective-permute-start(bf16[256,224]{1,0:T(8,128)(2,1)S(1)} %get-tuple-element.51), channel_id=1, source_target_pairs={{0,4},{2,6},{4,0},{6,2},{8,12},{10,14},{12,8},{14,10},{16,20},{18,... | collective-permute-start | bytes 344072 | tf_op jit(solution)/shard_map/ppermute | solution.py:533
  102.0 6.8 %collective-permute-start.19 = (bf16[256,224]{1,0:T(8,128)(2,1)S(1)}, bf16[256,224]{1,0:T(8,128)(2,1)S(1)}, u32[]{:S(2)}, u32[]{:S(2)}) collective-permute-start(bf16[256,224]{1,0:T(8,128)(2,1)S(1)} %get-tuple-element.52), channel_id=1, source_target_pairs={{0,2},{2,0},{4,6},{6,4},{8,10},{10,8},{12,14},{14,12},{16,18},{18,... | collective-permute-start | bytes 344072 | tf_op jit(solution)/shard_map/ppermute | solution.py:533
  102.7 7.8 %collective-permute-start.18 = (bf16[256,384]{1,0:T(8,128)(2,1)S(1)}, bf16[256,384]{1,0:T(8,128)(2,1)S(1)}, u32[]{:S(2)}, u32[]{:S(2)}) collective-permute-start(bf16[256,384]{1,0:T(8,128)(2,1)S(1)} %get-tuple-element.43), channel_id=1, source_target_pairs={{0,1},{2,3},{4,5},{6,7},{8,9},{10,11},{12,13},{14,15},{17,16},{19,... | collective-permute-start | bytes 589832 | tf_op jit(solution)/shard_map/ppermute | solution.py:546
  109.0 6.4 %collective-permute-start.23 = (bf16[256,224]{1,0:T(8,128)(2,1)S(1)}, bf16[256,224]{1,0:T(8,128)(2,1)S(1)}, u32[]{:S(2)}, u32[]{:S(2)}) collective-permute-start(bf16[256,224]{1,0:T(8,128)(2,1)S(1)} %get-tuple-element.45.refs_2_), channel_id=1, source_target_pairs={{0,4},{2,6},{4,0},{6,2},{8,12},{10,14},{12,8},{14,10},{16,20},{18,... | collective-permute-start | bytes 344072 | tf_op jit(solution)/shard_map/ppermute | solution.py:533
  110.0 6.6 %collective-permute-start.24 = (bf16[256,224]{1,0:T(8,128)(2,1)S(1)}, bf16[256,224]{1,0:T(8,128)(2,1)S(1)}, u32[]{:S(2)}, u32[]{:S(2)}) collective-permute-start(bf16[256,224]{1,0:T(8,128)(2,1)S(1)} %get-tuple-element.46.refs_3_), channel_id=1, source_target_pairs={{0,6},{2,4},{4,2},{6,0},{8,14},{10,12},{12,10},{14,8},{16,22},{18,... | collective-permute-start | bytes 344072 | tf_op jit(solution)/shard_map/ppermute | solution.py:533
  110.7 6.2 %collective-permute-start.22 = (bf16[256,224]{1,0:T(8,128)(2,1)S(1)}, bf16[256,224]{1,0:T(8,128)(2,1)S(1)}, u32[]{:S(2)}, u32[]{:S(2)}) collective-permute-start(bf16[256,224]{1,0:T(8,128)(2,1)S(1)} %get-tuple-element.48), channel_id=1, source_target_pairs={{0,2},{2,0},{4,6},{6,4},{8,10},{10,8},{12,14},{14,12},{16,18},{18,... | collective-permute-start | bytes 344072 | tf_op jit(solution)/shard_map/ppermute | solution.py:533
  (4 other events, 3.5 us)

commit v5 on v4

--- a/solution.py
+++ b/solution.py
@@ -31,7 +31,7 @@
     rows = lax.broadcasted_iota(jnp.int32, (tokens, tokens), 0)
     cols = lax.broadcasted_iota(jnp.int32, (tokens, tokens), 1)
     causal = rows <= cols
-    keep_own = jnp.where(causal, 1.0, 0.0).astype(BF16)
+    none = jnp.zeros((tokens, tokens), BF16)
     first = first_ref[0]
     spot = first + lax.broadcasted_iota(jnp.int32, (8, tokens), 1)
     start = jnp.int32(0)
@@ -91,9 +91,10 @@
             bias_mix,
         )
         p_near, ds_near = both(scores[near], grads[near], bias_near)
-        p_own, ds_own = p_mix * keep_own, ds_mix * keep_own
-        probs[own, turn], probs[near, turn], probs[far, turn] = p_own, p_near, p_mix - p_own
-        dscores[own, turn], dscores[near, turn], dscores[far, turn] = ds_own, ds_near, ds_mix - ds_own
+        p_own, p_far = jnp.where(causal, p_mix, none), jnp.where(causal, none, p_mix)
+        ds_own, ds_far = jnp.where(causal, ds_mix, none), jnp.where(causal, none, ds_mix)
+        probs[own, turn], probs[near, turn], probs[far, turn] = p_own, p_near, p_far
+        dscores[own, turn], dscores[near, turn], dscores[far, turn] = ds_own, ds_near, ds_far
     finish(per_group - 1)
     acc_v = functools.reduce(lambda a, b: a + b, [each[0] for each in sums])
     acc_k = functools.reduce(lambda a, b: a + b, [each[1] for each in sums])

time: 119 us -> 119 us (level)
  no operation moved by 1% of the time
where the time goes in v5:
time: 119 us; the launch traced here: 118 us
  waiting for transfers between devices  40.7 us (34%)
  starting transfers between devices  38 us (32%)
  Pallas kernels  35.4 us (30%)
  local copies, waits for them, and re-layouts  3.49 us (3%)
    ppermute x14, waiting for transfers between devices, swapped(): return lax.ppermute(array, 'seq', [(i, i ^ bits) for i in range(peers)])  28.8 us
    pallas_call x3, Pallas kernels, project(): pl.pallas_call(functools.partial(kernel, layers), in_specs=[vmem] * in_vm...  16.8 us
    ppermute x5, starting transfers between devices, layered(): return lax.ppermute(array, 'seq', pairs)  15.4 us
    pallas_call x2, Pallas kernels, attention(): pl.pallas_call(functools.partial(attention_kernel, group, groups), grid=(...  12.1 us
    ppermute x14, starting transfers between devices, swapped(): return lax.ppermute(array, 'seq', [(i, i ^ bits) for i in range(peers)])  8.57 us
    ppermute x5, waiting for transfers between devices, layered(): return lax.ppermute(array, 'seq', pairs)  6.96 us
    ppermute x3, starting transfers between devices, crossed(): return lax.ppermute(array, ('seq', 'head'), pairs)  6.3 us
    ppermute x2, starting transfers between devices, shifted(): return lax.ppermute(array, 'seq', pairs)  6.18 us
  transfers between devices with their start and end apart: 25, of which 13 were waited for; matrix products, arithmetic and copies ran while one was open for 0% of the time, Pallas kernels for 27%

profile of v5, /device:TPU:0, one launch (start us, length us, event | category | flops | bytes accessed | tf_op | source)
XLA Modules:
  0.0 118.0 jit_solution(15948952369066245047)
XLA Ops:
  0.0 2.4 %pack.1 = (bf16[256,512]{1,0:T(8,128)(2,1)}, bf16[224,2304]{1,0:T(8,128)(2,1)}) custom-call(bf16[256,256]{1,0:T(8,128)(2,1)} %refs_0_.1, bf16[256,256]{1,0:T(8,128)(2,1)} %refs_1_.1, bf16[224,1792]{1,0:T(8,128)(2,1)} %refs_2_.1, bf16[224,256]{1,0:T(8,128)(2,1)} %refs_3_.1, bf16[224,256]{1,0:T(8,128)(2,1)} %refs_4_.1), custom_call_target="tpu_custom_call" | custom-call | flops 1 | bytes 1 | tf_op jit(solution)/shard_map/pack/pallas_call | solution.py:441
  2.4 4.9 %collective-permute-start = (bf16[256,512]{1,0:T(8,128)(2,1)}, bf16[256,512]{1,0:T(8,128)(2,1)S(1)}, u32[]{:S(2)}, u32[]{:S(2)}) collective-permute-start(bf16[256,512]{1,0:T(8,128)(2,1)} %get-tuple-element.27.even_ref.k_own_ref.v_own_ref), channel_id=1, source_target_pairs={{0,4},{2,6},{4,8},{6,10},{8,12},{10,14},{12,16},{14,18},{16,20},{1... | collective-permute-start | bytes 786440 | tf_op jit(solution)/shard_map/ppermute | solution.py:529
  7.3 1.3 %collective-permute-start.5 = (bf16[224,2304]{1,0:T(8,128)(2,1)}, bf16[224,2304]{1,0:T(8,128)(2,1)}, u32[]{:S(2)}, u32[]{:S(2)}) collective-permute-start(bf16[224,2304]{1,0:T(8,128)(2,1)} %get-tuple-element.36.refs_0_), channel_id=1, source_target_pairs={{8,0},{10,2},{12,4},{14,6},{16,8},{18,10},{20,12},{22,14},{24,16},... | collective-permute-start | bytes 3096584 | tf_op jit(solution)/shard_map/ppermute | solution.py:539
  8.6 5.5 %collective-permute-start.4 = (bf16[224,2304]{1,0:T(8,128)(2,1)}, bf16[224,2304]{1,0:T(8,128)(2,1)}, u32[]{:S(2)}, u32[]{:S(2)}) collective-permute-start(bf16[224,2304]{1,0:T(8,128)(2,1)} %get-tuple-element.36.refs_0_), channel_id=1, source_target_pairs={{0,8},{2,10},{4,12},{6,14},{8,16},{10,18},{12,20},{14,22},{16,24},... | collective-permute-start | bytes 3096584 | tf_op jit(solution)/shard_map/ppermute | solution.py:539
  15.2 1.5 %collective-permute-done.1.k_near_ref.v_near_ref = bf16[256,512]{1,0:T(8,128)(2,1)S(1)} collective-permute-done((bf16[256,512]{1,0:T(8,128)(2,1)S(1)}, bf16[256,512]{1,0:T(8,128)(2,1)S(1)}, u32[]{:S(2)}, u32[]{:S(2)}) %collective-permute-start.1) | collective-permute-done | bytes 262176 | tf_op jit(solution)/shard_map/ppermute | solution.py:534
  17.4 5.8 %attention.2 = (bf16[256,896]{1,0:T(8,128)(2,1)}, f32[256,256]{1,0:T(8,128)}, bf16[256,256]{1,0:T(8,128)(2,1)}, bf16[256,256]{1,0:T(8,128)(2,1)}) custom-call(s32[1]{0:T(128)} %bitcast.first_ref, s32[4]{0:T(128)} %docs_ref.3, bf16[256,1792]{1,0:T(8,128)(2,1)} %q_ref.3, bf16[256,1792]{1,0:T(8,128)(2,1)} %do_ref.3, bf16[256,1792]{1,0:T(8,128)(2,1)} %o_ref.3, ...), custom_call_target="tpu_custom_call" | custom-call | flops 900000000 | bytes 1 | tf_op jit(solution)/shard_map/attention/pallas_call | solution.py:132
  23.2 1.5 %collective-permute-start.6 = (bf16[256,896]{1,0:T(8,128)(2,1)}, bf16[256,896]{1,0:T(8,128)(2,1)S(1)}, u32[]{:S(2)}, u32[]{:S(2)}) collective-permute-start(bf16[256,896]{1,0:T(8,128)(2,1)} %get-tuple-element.28.refs_0_), channel_id=1, source_target_pairs={{0,4},{2,6},{4,0},{6,2},{8,12},{10,14},{12,8},{14,10},{16,20},{18,... | collective-permute-start | bytes 1376264 | tf_op jit(solution)/shard_map/ppermute | solution.py:534
  24.7 6.3 %attention.3 = (bf16[256,896]{1,0:T(8,128)(2,1)}, f32[256,512]{1,0:T(8,128)}, bf16[256,512]{1,0:T(8,128)(2,1)}, bf16[256,512]{1,0:T(8,128)(2,1)}) custom-call(s32[1]{0:T(128)} %bitcast.first_ref, s32[4]{0:T(128)} %docs_ref.3, bf16[256,1792]{1,0:T(8,128)(2,1)} %q_ref.3, bf16[256,1792]{1,0:T(8,128)(2,1)} %do_ref.3, bf16[256,1792]{1,0:T(8,128)(2,1)} %o_ref.3, ...), custom_call_target="tpu_custom_call" | custom-call | flops 900000000 | bytes 1 | tf_op jit(solution)/shard_map/attention/pallas_call | solution.py:132
  31.0 1.7 %collective-permute-done.2.got = bf16[256,512]{1,0:T(8,128)(2,1)S(1)} collective-permute-done((bf16[256,512]{1,0:T(8,128)(2,1)}, bf16[256,512]{1,0:T(8,128)(2,1)S(1)}, u32[]{:S(2)}, u32[]{:S(2)}) %collective-permute-start.2) | collective-permute-done | bytes 262176 | tf_op jit(solution)/shard_map/ppermute | solution.py:534
  33.8 1.3 %collective-permute-start.3 = (bf16[256,512]{1,0:T(8,128)(2,1)S(1)}, bf16[256,512]{1,0:T(8,128)(2,1)}, u32[]{:S(2)}, u32[]{:S(2)}) collective-permute-start(bf16[256,512]{1,0:T(8,128)(2,1)S(1)} %merge.1), channel_id=1, source_target_pairs={{4,0},{6,2},{8,4},{10,6},{12,8},{14,10},{16,12},{18,14},{20,16},{2... | collective-permute-start | bytes 786440 | tf_op jit(solution)/shard_map/ppermute | solution.py:529
  36.8 1.3 %collective-permute-start.13 = (bf16[224,2304]{1,0:T(8,128)(2,1)}, bf16[224,2304]{1,0:T(8,128)(2,1)}, u32[]{:S(2)}, u32[]{:S(2)}) collective-permute-start(bf16[224,2304]{1,0:T(8,128)(2,1)} %gate.2.refs_1_.refs_10_.refs_0_.refs_2_.refs_5_), channel_id=1, source_target_pairs={{8,0},{10,2},{12,4},{14,6},{16,8},{18,10},{20,12},{22,14},{9,1},{1... | collective-permute-start | bytes 3096584 | tf_op jit(solution)/shard_map/ppermute | solution.py:539
  38.1 1.6 %collective-permute-start.12 = (bf16[224,2304]{1,0:T(8,128)(2,1)}, bf16[224,2304]{1,0:T(8,128)(2,1)}, u32[]{:S(2)}, u32[]{:S(2)}) collective-permute-start(bf16[224,2304]{1,0:T(8,128)(2,1)} %collective-permute-done.4.refs_0_.refs_11_.refs_1_.refs_3_.refs_6_), channel_id=1, source_target_pairs={{8,16},{10,18},{12,20},{14,22},{16,24},{18,26},{20,28},{22,30},{9,... | collective-permute-start | bytes 3096584 | tf_op jit(solution)/shard_map/ppermute | solution.py:539
  39.7 4.5 %collective-permute-done.3.back = bf16[256,512]{1,0:T(8,128)(2,1)} collective-permute-done((bf16[256,512]{1,0:T(8,128)(2,1)S(1)}, bf16[256,512]{1,0:T(8,128)(2,1)}, u32[]{:S(2)}, u32[]{:S(2)}) %collective-permute-start.3) | collective-permute-done | bytes 262176 | tf_op jit(solution)/shard_map/ppermute | solution.py:529
  44.3 2.3 %join.1.refs_1_ = bf16[256,1408]{1,0:T(8,128)(2,1)} custom-call(bf16[256,896]{1,0:T(8,128)(2,1)} %get-tuple-element.32.dq, f32[256,512]{1,0:T(8,128)} %get-tuple-element.33.own, bf16[256,512]{1,0:T(8,128)(2,1)} %copy-done.4, bf16[256,512]{1,0:T(8,128)(2,1)} %collective-permute-done.3.back, ...), custom_call_target="tpu_custom_call" | custom-call | flops 1000000000 | bytes 1 | tf_op jit(solution)/shard_map/join/pallas_call | solution.py:515
  46.6 2.1 %collective-permute-start.7 = (bf16[256,1408]{1,0:T(8,128)(2,1)}, bf16[256,1408]{1,0:T(8,128)(2,1)S(1)}, u32[]{:S(2)}, u32[]{:S(2)}) collective-permute-start(bf16[256,1408]{1,0:T(8,128)(2,1)} %join.1.refs_1_), channel_id=1, source_target_pairs={{0,4},{2,6},{4,0},{6,2},{8,12},{10,14},{12,8},{14,10},{16,20},{18,... | collective-permute-start | bytes 2162696 | tf_op jit(solution)/shard_map/ppermute | solution.py:534
  49.2 2.1 %collective-permute-done.8.refs_4_ = bf16[256,896]{1,0:T(8,128)(2,1)S(1)} collective-permute-done((bf16[256,896]{1,0:T(8,128)(2,1)}, bf16[256,896]{1,0:T(8,128)(2,1)S(1)}, u32[]{:S(2)}, u32[]{:S(2)}) %collective-permute-start.8) | collective-permute-done | bytes 458784 | tf_op jit(solution)/shard_map/ppermute | solution.py:534
  51.5 12.7 %collective-permute-done.7.refs_3_ = bf16[256,1408]{1,0:T(8,128)(2,1)S(1)} collective-permute-done((bf16[256,1408]{1,0:T(8,128)(2,1)}, bf16[256,1408]{1,0:T(8,128)(2,1)S(1)}, u32[]{:S(2)}, u32[]{:S(2)}) %collective-permute-start.7) | collective-permute-done | bytes 720928 | tf_op jit(solution)/shard_map/ppermute | solution.py:534
  64.2 2.1 %collective-permute-done.13.refs_2_.refs_9_.refs_1_.refs_4_ = bf16[224,2304]{1,0:T(8,128)(2,1)} collective-permute-done((bf16[224,2304]{1,0:T(8,128)(2,1)}, bf16[224,2304]{1,0:T(8,128)(2,1)}, u32[]{:S(2)}, u32[]{:S(2)}) %collective-permute-start.13) | collective-permute-done | bytes 1032224 | tf_op jit(solution)/shard_map/ppermute | solution.py:539
  66.3 5.6 %collective-permute-start.14 = (bf16[224,2304]{1,0:T(8,128)(2,1)}, bf16[224,2304]{1,0:T(8,128)(2,1)}, u32[]{:S(2)}, u32[]{:S(2)}) collective-permute-start(bf16[224,2304]{1,0:T(8,128)(2,1)} %gate.3.refs_8_.own), channel_id=1, source_target_pairs={{0,24},{2,26},{4,28},{6,30},{24,0},{26,2},{28,4},{30,6},{1,25},{3,... | collective-permute-start | bytes 3096584 | tf_op jit(solution)/shard_map/ppermute | solution.py:539
  72.0 6.1 %project_send.1 = (bf16[256,896]{1,0:T(8,128)(2,1)}, bf16[1024,2304]{1,0:T(8,128)(2,1)}) custom-call(bf16[256,896]{1,0:T(8,128)(2,1)} %get-tuple-element.28.refs_0_, bf16[256,1408]{1,0:T(8,128)(2,1)} %join.1.refs_1_, bf16[256,896]{1,0:T(8,128)(2,1)} %copy-done.9, bf16[256,1408]{1,0:T(8,128)(2,1)} %copy-done.7, bf16[256,896]{1,0:T(8,128)(2,1)} %copy-done.8, ...), custom_call_target="tpu_custom_call" | custom-call | flops 1 | bytes 1 | tf_op jit(solution)/shard_map/project_send/pallas_call | solution.py:285
  78.1 1.6 %collective-permute-start.15 = (bf16[256,896]{1,0:T(8,128)(2,1)}, bf16[256,896]{1,0:T(8,128)(2,1)S(1)}, u32[]{:S(2)}, u32[]{:S(2)}) collective-permute-start(bf16[256,896]{1,0:T(8,128)(2,1)} %get-tuple-element.38.refs_8_), channel_id=1, source_target_pairs={{0,1},{1,0},{2,3},{3,2},{4,5},{5,4},{6,7},{7,6},{8,9},{9,8},{10,11... | collective-permute-start | bytes 1376264 | tf_op jit(solution)/shard_map/ppermute | solution.py:650
  79.7 7.9 %project_keep.1 = (f32[4,256,224]{2,1,0:T(8,128)}, f32[4,256,224]{2,1,0:T(8,128)}, bf16[256,896]{1,0:T(8,128)(2,1)}) custom-call(bf16[1024,2304]{1,0:T(8,128)(2,1)} %get-tuple-element.37.held, bf16[224,2304]{1,0:T(8,128)(2,1)} %gate.3.refs_8_.own, bf16[224,2304]{1,0:T(8,128)(2,1)} %gate.2.refs_1_.refs_10_.refs_0_.refs_2_.refs_5_, ...), custom_call_target="tpu_custom_call" | custom-call | flops 1 | bytes 1 | tf_op jit(solution)/shard_map/project_keep/pallas_call | solution.py:285
  87.6 1.6 %collective-permute-start.16 = (bf16[256,896]{1,0:T(8,128)(2,1)}, bf16[256,896]{1,0:T(8,128)(2,1)S(1)}, u32[]{:S(2)}, u32[]{:S(2)}) collective-permute-start(bf16[256,896]{1,0:T(8,128)(2,1)} %get-tuple-element.41), channel_id=1, source_target_pairs={{1,0},{3,2},{5,4},{7,6},{9,8},{11,10},{13,12},{15,14},{16,17},{18,... | collective-permute-start | bytes 1376264 | tf_op jit(solution)/shard_map/ppermute | solution.py:547
  89.6 4.8 %collective-permute-done.14.refs_0_.refs_3_ = bf16[224,2304]{1,0:T(8,128)(2,1)} collective-permute-done((bf16[224,2304]{1,0:T(8,128)(2,1)}, bf16[224,2304]{1,0:T(8,128)(2,1)}, u32[]{:S(2)}, u32[]{:S(2)}) %collective-permute-start.14) | collective-permute-done | bytes 1032224 | tf_op jit(solution)/shard_map/ppermute | solution.py:539
  94.4 2.7 %project_last.1 = (f32[4,256,224]{2,1,0:T(8,128)S(1)}, bf16[256,512]{1,0:T(8,128)(2,1)S(1)}, bf16[256,384]{1,0:T(8,128)(2,1)S(1)}) custom-call(bf16[1024,2304]{1,0:T(8,128)(2,1)S(1)} %copy-done, bf16[224,2304]{1,0:T(8,128)(2,1)} %collective-permute-done.14.refs_0_.refs_3_, bf16[224,2304]{1,0:T(8,128)(2,1)} %collective-permute-done.13.refs_2_.refs_9_.refs_1_.refs_4_, ...), custom_call_target="tpu_custom_call" | custom-call | flops 1 | bytes 1 | tf_op jit(solution)/shard_map/project_last/pallas_call | solution.py:285
  97.2 3.4 %collective-permute-start.17 = (bf16[256,512]{1,0:T(8,128)(2,1)S(1)}, bf16[256,512]{1,0:T(8,128)(2,1)S(1)}, u32[]{:S(2)}, u32[]{:S(2)}) collective-permute-start(bf16[256,512]{1,0:T(8,128)(2,1)S(1)} %get-tuple-element.42), channel_id=1, source_target_pairs={{0,1},{2,3},{4,5},{6,7},{8,9},{10,11},{12,13},{14,15},{17,16},{19,... | collective-permute-start | bytes 786440 | tf_op jit(solution)/shard_map/ppermute | solution.py:547
  102.7 1.3 %collective-permute-start.18 = (bf16[256,384]{1,0:T(8,128)(2,1)S(1)}, bf16[256,384]{1,0:T(8,128)(2,1)S(1)}, u32[]{:S(2)}, u32[]{:S(2)}) collective-permute-start(bf16[256,384]{1,0:T(8,128)(2,1)S(1)} %get-tuple-element.43), channel_id=1, source_target_pairs={{0,1},{2,3},{4,5},{6,7},{8,9},{10,11},{12,13},{14,15},{17,16},{19,... | collective-permute-start | bytes 589832 | tf_op jit(solution)/shard_map/ppermute | solution.py:547
  104.0 2.5 %collective-permute-done.21.refs_3_ = bf16[256,224]{1,0:T(8,128)(2,1)S(1)} collective-permute-done((bf16[256,224]{1,0:T(8,128)(2,1)S(1)}, bf16[256,224]{1,0:T(8,128)(2,1)S(1)}, u32[]{:S(2)}, u32[]{:S(2)}) %collective-permute-start.21) | collective-permute-done | bytes 114720 | tf_op jit(solution)/shard_map/ppermute | solution.py:534
  106.6 2.2 %collective-permute-done.20.refs_2_ = bf16[256,224]{1,0:T(8,128)(2,1)S(1)} collective-permute-done((bf16[256,224]{1,0:T(8,128)(2,1)S(1)}, bf16[256,224]{1,0:T(8,128)(2,1)S(1)}, u32[]{:S(2)}, u32[]{:S(2)}) %collective-permute-start.20) | collective-permute-done | bytes 114720 | tf_op jit(solution)/shard_map/ppermute | solution.py:534
  111.4 4.0 %collective-permute-done.23.refs_4_ = bf16[256,224]{1,0:T(8,128)(2,1)S(1)} collective-permute-done((bf16[256,224]{1,0:T(8,128)(2,1)S(1)}, bf16[256,224]{1,0:T(8,128)(2,1)S(1)}, u32[]{:S(2)}, u32[]{:S(2)}) %collective-permute-start.23) | collective-permute-done | bytes 114720 | tf_op jit(solution)/shard_map/ppermute | solution.py:534
  115.4 1.2 %collective-permute-done.24.refs_5_ = bf16[256,224]{1,0:T(8,128)(2,1)S(1)} collective-permute-done((bf16[256,224]{1,0:T(8,128)(2,1)S(1)}, bf16[256,224]{1,0:T(8,128)(2,1)S(1)}, u32[]{:S(2)}, u32[]{:S(2)}) %collective-permute-start.24) | collective-permute-done | bytes 114720 | tf_op jit(solution)/shard_map/ppermute | solution.py:534
  116.9 1.1 place.3
  (56 shorter events, 10.6 us)
Async XLA Ops:
  2.4 11.7 %collective-permute-start = (bf16[256,512]{1,0:T(8,128)(2,1)}, bf16[256,512]{1,0:T(8,128)(2,1)S(1)}, u32[]{:S(2)}, u32[]{:S(2)}) collective-permute-start(bf16[256,512]{1,0:T(8,128)(2,1)} %get-tuple-element.27.even_ref.k_own_ref.v_own_ref), channel_id=1, source_target_pairs={{0,4},{2,6},{4,8},{6,10},{8,12},{10,14},{12,16},{14,18},{16,20},{1... | collective-permute-start | bytes 786440 | tf_op jit(solution)/shard_map/ppermute | solution.py:529
  7.3 28.7 %collective-permute-start.5 = (bf16[224,2304]{1,0:T(8,128)(2,1)}, bf16[224,2304]{1,0:T(8,128)(2,1)}, u32[]{:S(2)}, u32[]{:S(2)}) collective-permute-start(bf16[224,2304]{1,0:T(8,128)(2,1)} %get-tuple-element.36.refs_0_), channel_id=1, source_target_pairs={{8,0},{10,2},{12,4},{14,6},{16,8},{18,10},{20,12},{22,14},{24,16},... | collective-permute-start | bytes 3096584 | tf_op jit(solution)/shard_map/ppermute | solution.py:539
  8.6 29.5 %collective-permute-start.4 = (bf16[224,2304]{1,0:T(8,128)(2,1)}, bf16[224,2304]{1,0:T(8,128)(2,1)}, u32[]{:S(2)}, u32[]{:S(2)}) collective-permute-start(bf16[224,2304]{1,0:T(8,128)(2,1)} %get-tuple-element.36.refs_0_), channel_id=1, source_target_pairs={{0,8},{2,10},{4,12},{6,14},{8,16},{10,18},{12,20},{14,22},{16,24},... | collective-permute-start | bytes 3096584 | tf_op jit(solution)/shard_map/ppermute | solution.py:539
  15.1 1.6 %copy-start.2 = (bf16[256,512]{1,0:T(8,128)(2,1)}, bf16[256,512]{1,0:T(8,128)(2,1)S(1)}, u32[]{:S(2)}) copy-start(bf16[256,512]{1,0:T(8,128)(2,1)S(1)} %collective-permute-done.odd_ref.k_far_ref.v_far_ref) | copy-start | bytes 786436
  15.1 1.6 %collective-permute-start.1 = (bf16[256,512]{1,0:T(8,128)(2,1)S(1)}, bf16[256,512]{1,0:T(8,128)(2,1)S(1)}, u32[]{:S(2)}, u32[]{:S(2)}) collective-permute-start(bf16[256,512]{1,0:T(8,128)(2,1)S(1)} %choose.1), channel_id=1, source_target_pairs={{0,2},{2,0},{4,6},{6,4},{8,10},{10,8},{12,14},{14,12},{16,18},{18,... | collective-permute-start | bytes 786440 | tf_op jit(solution)/shard_map/ppermute | solution.py:534
  23.2 12.8 %collective-permute-start.6 = (bf16[256,896]{1,0:T(8,128)(2,1)}, bf16[256,896]{1,0:T(8,128)(2,1)S(1)}, u32[]{:S(2)}, u32[]{:S(2)}) collective-permute-start(bf16[256,896]{1,0:T(8,128)(2,1)} %get-tuple-element.28.refs_0_), channel_id=1, source_target_pairs={{0,4},{2,6},{4,0},{6,2},{8,12},{10,14},{12,8},{14,10},{16,20},{18,... | collective-permute-start | bytes 1376264 | tf_op jit(solution)/shard_map/ppermute | solution.py:534
  31.0 1.7 %collective-permute-start.2 = (bf16[256,512]{1,0:T(8,128)(2,1)}, bf16[256,512]{1,0:T(8,128)(2,1)S(1)}, u32[]{:S(2)}, u32[]{:S(2)}) collective-permute-start(bf16[256,512]{1,0:T(8,128)(2,1)} %get-tuple-element.34), channel_id=1, source_target_pairs={{0,2},{2,0},{4,6},{6,4},{8,10},{10,8},{12,14},{14,12},{16,18},{18,... | collective-permute-start | bytes 786440 | tf_op jit(solution)/shard_map/ppermute | solution.py:534
  32.8 11.5 %copy-start.4 = (bf16[256,512]{1,0:T(8,128)(2,1)}, bf16[256,512]{1,0:T(8,128)(2,1)S(1)}, u32[]{:S(2)}) copy-start(bf16[256,512]{1,0:T(8,128)(2,1)S(1)} %collective-permute-done.2.got) | copy-start | bytes 786436
  33.8 10.4 %collective-permute-start.3 = (bf16[256,512]{1,0:T(8,128)(2,1)S(1)}, bf16[256,512]{1,0:T(8,128)(2,1)}, u32[]{:S(2)}, u32[]{:S(2)}) collective-permute-start(bf16[256,512]{1,0:T(8,128)(2,1)S(1)} %merge.1), channel_id=1, source_target_pairs={{4,0},{6,2},{8,4},{10,6},{12,8},{14,10},{16,12},{18,14},{20,16},{2... | collective-permute-start | bytes 786440 | tf_op jit(solution)/shard_map/ppermute | solution.py:529
  36.8 29.5 %collective-permute-start.13 = (bf16[224,2304]{1,0:T(8,128)(2,1)}, bf16[224,2304]{1,0:T(8,128)(2,1)}, u32[]{:S(2)}, u32[]{:S(2)}) collective-permute-start(bf16[224,2304]{1,0:T(8,128)(2,1)} %gate.2.refs_1_.refs_10_.refs_0_.refs_2_.refs_5_), channel_id=1, source_target_pairs={{8,0},{10,2},{12,4},{14,6},{16,8},{18,10},{20,12},{22,14},{9,1},{1... | collective-permute-start | bytes 3096584 | tf_op jit(solution)/shard_map/ppermute | solution.py:539
  38.1 28.2 %collective-permute-start.12 = (bf16[224,2304]{1,0:T(8,128)(2,1)}, bf16[224,2304]{1,0:T(8,128)(2,1)}, u32[]{:S(2)}, u32[]{:S(2)}) collective-permute-start(bf16[224,2304]{1,0:T(8,128)(2,1)} %collective-permute-done.4.refs_0_.refs_11_.refs_1_.refs_3_.refs_6_), channel_id=1, source_target_pairs={{8,16},{10,18},{12,20},{14,22},{16,24},{18,26},{20,28},{22,30},{9,... | collective-permute-start | bytes 3096584 | tf_op jit(solution)/shard_map/ppermute | solution.py:539
  46.6 17.6 %collective-permute-start.7 = (bf16[256,1408]{1,0:T(8,128)(2,1)}, bf16[256,1408]{1,0:T(8,128)(2,1)S(1)}, u32[]{:S(2)}, u32[]{:S(2)}) collective-permute-start(bf16[256,1408]{1,0:T(8,128)(2,1)} %join.1.refs_1_), channel_id=1, source_target_pairs={{0,4},{2,6},{4,0},{6,2},{8,12},{10,14},{12,8},{14,10},{16,20},{18,... | collective-permute-start | bytes 2162696 | tf_op jit(solution)/shard_map/ppermute | solution.py:534
  48.7 2.7 %collective-permute-start.8 = (bf16[256,896]{1,0:T(8,128)(2,1)}, bf16[256,896]{1,0:T(8,128)(2,1)S(1)}, u32[]{:S(2)}, u32[]{:S(2)}) collective-permute-start(bf16[256,896]{1,0:T(8,128)(2,1)} %get-tuple-element.28.refs_0_), channel_id=1, source_target_pairs={{0,2},{2,0},{4,6},{6,4},{8,10},{10,8},{12,14},{14,12},{16,18},{18,... | collective-permute-start | bytes 1376264 | tf_op jit(solution)/shard_map/ppermute | solution.py:534
  48.7 15.5 %collective-permute-start.10 = (bf16[256,896]{1,0:T(8,128)(2,1)}, bf16[256,896]{1,0:T(8,128)(2,1)}, u32[]{:S(2)}, u32[]{:S(2)}) collective-permute-start(bf16[256,896]{1,0:T(8,128)(2,1)} %copy-done.9), channel_id=1, source_target_pairs={{0,2},{2,0},{4,6},{6,4},{8,10},{10,8},{12,14},{14,12},{16,18},{18,... | collective-permute-start | bytes 1376264 | tf_op jit(solution)/shard_map/ppermute | solution.py:534
  51.4 12.8 %copy-start.8 = (bf16[256,896]{1,0:T(8,128)(2,1)}, bf16[256,896]{1,0:T(8,128)(2,1)S(1)}, u32[]{:S(2)}) copy-start(bf16[256,896]{1,0:T(8,128)(2,1)S(1)} %collective-permute-done.8.refs_4_) | copy-start | bytes 1376260
  51.4 20.6 %collective-permute-start.9 = (bf16[256,1408]{1,0:T(8,128)(2,1)}, bf16[256,1408]{1,0:T(8,128)(2,1)}, u32[]{:S(2)}, u32[]{:S(2)}) collective-permute-start(bf16[256,1408]{1,0:T(8,128)(2,1)} %join.1.refs_1_), channel_id=1, source_target_pairs={{0,2},{2,0},{4,6},{6,4},{8,10},{10,8},{12,14},{14,12},{16,18},{18,... | collective-permute-start | bytes 2162696 | tf_op jit(solution)/shard_map/ppermute | solution.py:534
  64.2 2.1 %copy-start.7 = (bf16[256,1408]{1,0:T(8,128)(2,1)}, bf16[256,1408]{1,0:T(8,128)(2,1)S(1)}, u32[]{:S(2)}) copy-start(bf16[256,1408]{1,0:T(8,128)(2,1)S(1)} %collective-permute-done.7.refs_3_) | copy-start | bytes 2162692
  64.2 7.8 %collective-permute-start.11 = (bf16[256,1408]{1,0:T(8,128)(2,1)S(1)}, bf16[256,1408]{1,0:T(8,128)(2,1)}, u32[]{:S(2)}, u32[]{:S(2)}) collective-permute-start(bf16[256,1408]{1,0:T(8,128)(2,1)S(1)} %collective-permute-done.7.refs_3_), channel_id=1, source_target_pairs={{0,2},{2,0},{4,6},{6,4},{8,10},{10,8},{12,14},{14,12},{16,18},{18,... | collective-permute-start | bytes 2162696 | tf_op jit(solution)/shard_map/ppermute | solution.py:534
  66.3 28.1 %collective-permute-start.14 = (bf16[224,2304]{1,0:T(8,128)(2,1)}, bf16[224,2304]{1,0:T(8,128)(2,1)}, u32[]{:S(2)}, u32[]{:S(2)}) collective-permute-start(bf16[224,2304]{1,0:T(8,128)(2,1)} %gate.3.refs_8_.own), channel_id=1, source_target_pairs={{0,24},{2,26},{4,28},{6,30},{24,0},{26,2},{28,4},{30,6},{1,25},{3,... | collective-permute-start | bytes 3096584 | tf_op jit(solution)/shard_map/ppermute | solution.py:539
  78.1 11.5 %collective-permute-start.15 = (bf16[256,896]{1,0:T(8,128)(2,1)}, bf16[256,896]{1,0:T(8,128)(2,1)S(1)}, u32[]{:S(2)}, u32[]{:S(2)}) collective-permute-start(bf16[256,896]{1,0:T(8,128)(2,1)} %get-tuple-element.38.refs_8_), channel_id=1, source_target_pairs={{0,1},{1,0},{2,3},{3,2},{4,5},{5,4},{6,7},{7,6},{8,9},{9,8},{10,11... | collective-permute-start | bytes 1376264 | tf_op jit(solution)/shard_map/ppermute | solution.py:650
  79.7 14.8 %copy-start = (bf16[1024,2304]{1,0:T(8,128)(2,1)S(1)}, bf16[1024,2304]{1,0:T(8,128)(2,1)}, u32[]{:S(2)}) copy-start(bf16[1024,2304]{1,0:T(8,128)(2,1)} %get-tuple-element.37.held) | copy-start | bytes 14155780
  87.6 13.0 %copy-start.10 = (f32[4,256,224]{2,1,0:T(8,128)S(1)}, f32[4,256,224]{2,1,0:T(8,128)}, u32[]{:S(2)}) copy-start(f32[4,256,224]{2,1,0:T(8,128)} %get-tuple-element.44) | copy-start | bytes 2752516
  87.6 21.1 %copy-start.3 = (f32[4,256,224]{2,1,0:T(8,128)S(1)}, f32[4,256,224]{2,1,0:T(8,128)}, u32[]{:S(2)}) copy-start(f32[4,256,224]{2,1,0:T(8,128)} %get-tuple-element.40.mate_full) | copy-start | bytes 2752516
  87.6 15.1 %collective-permute-start.16 = (bf16[256,896]{1,0:T(8,128)(2,1)}, bf16[256,896]{1,0:T(8,128)(2,1)S(1)}, u32[]{:S(2)}, u32[]{:S(2)}) collective-permute-start(bf16[256,896]{1,0:T(8,128)(2,1)} %get-tuple-element.41), channel_id=1, source_target_pairs={{1,0},{3,2},{5,4},{7,6},{9,8},{11,10},{13,12},{15,14},{16,17},{18,... | collective-permute-start | bytes 1376264 | tf_op jit(solution)/shard_map/ppermute | solution.py:547
  97.2 11.6 %collective-permute-start.17 = (bf16[256,512]{1,0:T(8,128)(2,1)S(1)}, bf16[256,512]{1,0:T(8,128)(2,1)S(1)}, u32[]{:S(2)}, u32[]{:S(2)}) collective-permute-start(bf16[256,512]{1,0:T(8,128)(2,1)S(1)} %get-tuple-element.42), channel_id=1, source_target_pairs={{0,1},{2,3},{4,5},{6,7},{8,9},{10,11},{12,13},{14,15},{17,16},{19,... | collective-permute-start | bytes 786440 | tf_op jit(solution)/shard_map/ppermute | solution.py:547
  100.8 5.8 %collective-permute-start.21 = (bf16[256,224]{1,0:T(8,128)(2,1)S(1)}, bf16[256,224]{1,0:T(8,128)(2,1)S(1)}, u32[]{:S(2)}, u32[]{:S(2)}) collective-permute-start(bf16[256,224]{1,0:T(8,128)(2,1)S(1)} %get-tuple-element.50), channel_id=1, source_target_pairs={{0,6},{2,4},{4,2},{6,0},{8,14},{10,12},{12,10},{14,8},{16,22},{18,... | collective-permute-start | bytes 344072 | tf_op jit(solution)/shard_map/ppermute | solution.py:534
  100.9 7.9 %collective-permute-start.20 = (bf16[256,224]{1,0:T(8,128)(2,1)S(1)}, bf16[256,224]{1,0:T(8,128)(2,1)S(1)}, u32[]{:S(2)}, u32[]{:S(2)}) collective-permute-start(bf16[256,224]{1,0:T(8,128)(2,1)S(1)} %get-tuple-element.51), channel_id=1, source_target_pairs={{0,4},{2,6},{4,0},{6,2},{8,12},{10,14},{12,8},{14,10},{16,20},{18,... | collective-permute-start | bytes 344072 | tf_op jit(solution)/shard_map/ppermute | solution.py:534
  102.0 6.8 %collective-permute-start.19 = (bf16[256,224]{1,0:T(8,128)(2,1)S(1)}, bf16[256,224]{1,0:T(8,128)(2,1)S(1)}, u32[]{:S(2)}, u32[]{:S(2)}) collective-permute-start(bf16[256,224]{1,0:T(8,128)(2,1)S(1)} %get-tuple-element.52), channel_id=1, source_target_pairs={{0,2},{2,0},{4,6},{6,4},{8,10},{10,8},{12,14},{14,12},{16,18},{18,... | collective-permute-start | bytes 344072 | tf_op jit(solution)/shard_map/ppermute | solution.py:534
  102.7 7.9 %collective-permute-start.18 = (bf16[256,384]{1,0:T(8,128)(2,1)S(1)}, bf16[256,384]{1,0:T(8,128)(2,1)S(1)}, u32[]{:S(2)}, u32[]{:S(2)}) collective-permute-start(bf16[256,384]{1,0:T(8,128)(2,1)S(1)} %get-tuple-element.43), channel_id=1, source_target_pairs={{0,1},{2,3},{4,5},{6,7},{8,9},{10,11},{12,13},{14,15},{17,16},{19,... | collective-permute-start | bytes 589832 | tf_op jit(solution)/shard_map/ppermute | solution.py:547
  109.0 6.4 %collective-permute-start.23 = (bf16[256,224]{1,0:T(8,128)(2,1)S(1)}, bf16[256,224]{1,0:T(8,128)(2,1)S(1)}, u32[]{:S(2)}, u32[]{:S(2)}) collective-permute-start(bf16[256,224]{1,0:T(8,128)(2,1)S(1)} %get-tuple-element.45.refs_2_), channel_id=1, source_target_pairs={{0,4},{2,6},{4,0},{6,2},{8,12},{10,14},{12,8},{14,10},{16,20},{18,... | collective-permute-start | bytes 344072 | tf_op jit(solution)/shard_map/ppermute | solution.py:534
  110.0 6.6 %collective-permute-start.24 = (bf16[256,224]{1,0:T(8,128)(2,1)S(1)}, bf16[256,224]{1,0:T(8,128)(2,1)S(1)}, u32[]{:S(2)}, u32[]{:S(2)}) collective-permute-start(bf16[256,224]{1,0:T(8,128)(2,1)S(1)} %get-tuple-element.46.refs_3_), channel_id=1, source_target_pairs={{0,6},{2,4},{4,2},{6,0},{8,14},{10,12},{12,10},{14,8},{16,22},{18,... | collective-permute-start | bytes 344072 | tf_op jit(solution)/shard_map/ppermute | solution.py:534
  110.7 6.2 %collective-permute-start.22 = (bf16[256,224]{1,0:T(8,128)(2,1)S(1)}, bf16[256,224]{1,0:T(8,128)(2,1)S(1)}, u32[]{:S(2)}, u32[]{:S(2)}) collective-permute-start(bf16[256,224]{1,0:T(8,128)(2,1)S(1)} %get-tuple-element.48), channel_id=1, source_target_pairs={{0,2},{2,0},{4,6},{6,4},{8,10},{10,8},{12,14},{14,12},{16,18},{18,... | collective-permute-start | bytes 344072 | tf_op jit(solution)/shard_map/ppermute | solution.py:534
  (4 other events, 3.5 us)

commit v6 on v5

--- a/solution.py
+++ b/solution.py
@@ -658,7 +658,7 @@
         return array[:, k * rows : (k + 1) * rows].astype(F32)
 
     sets = [returned([(keep[r] + lanes(got, r)).astype(BF16) for r in range(INNER)])]
-    blocks, after = [None] * INNER, sets[0][1:]
+    blocks, after = [None] * INNER, sets[0][1:2]
     for k, picks in enumerate((order[:2], order[2:])):
         after = combine(layers, order, picks, last_full, mate_full, got_mate, gots[: k + 1], after)
         for r, block in zip(picks, after):

time: 119 us -> 118 us (level)
    ppermute x3, waiting for transfers between devices: 0.01 us -> 3.26 us  [crossed(): return lax.ppermute(array, ('seq', 'head'), pairs)]
    ppermute x14, waiting for transfers between devices: 28.8 us -> 25.6 us  [swapped(): return lax.ppermute(array, 'seq', [(i, i ^ bits) for i in range(peers)])]
  transfers between devices with their start and end apart: 25 -> 25, of which waited for: 13 -> 14; matrix products, arithmetic and copies ran while one was open for 0% -> 0% of each run, Pallas kernels for 27% -> 27%
where the time goes in v6:
time: 118 us; the launch traced here: 117 us
  waiting for transfers between devices  40.7 us (34%)
  starting transfers between devices  37.2 us (32%)
  Pallas kernels  35.4 us (30%)
  local copies, waits for them, and re-layouts  3.49 us (3%)
    ppermute x14, waiting for transfers between devices, swapped(): return lax.ppermute(array, 'seq', [(i, i ^ bits) for i in range(peers)])  25.6 us
    pallas_call x3, Pallas kernels, project(): pl.pallas_call(functools.partial(kernel, layers), in_specs=[vmem] * in_vm...  16.8 us
    ppermute x5, starting transfers between devices, layered(): return lax.ppermute(array, 'seq', pairs)  15.4 us
    pallas_call x2, Pallas kernels, attention(): pl.pallas_call(functools.partial(attention_kernel, group, groups), grid=(...  12.1 us
    ppermute x14, starting transfers between devices, swapped(): return lax.ppermute(array, 'seq', [(i, i ^ bits) for i in range(peers)])  7.77 us
    ppermute x5, waiting for transfers between devices, layered(): return lax.ppermute(array, 'seq', pairs)  6.96 us
    ppermute x3, starting transfers between devices, crossed(): return lax.ppermute(array, ('seq', 'head'), pairs)  6.31 us
    ppermute x2, starting transfers between devices, shifted(): return lax.ppermute(array, 'seq', pairs)  6.18 us
  transfers between devices with their start and end apart: 25, of which 14 were waited for; matrix products, arithmetic and copies ran while one was open for 0% of the time, Pallas kernels for 27%

profile of v6, /device:TPU:0, one launch (start us, length us, event | category | flops | bytes accessed | tf_op | source)
XLA Modules:
  0.0 117.3 jit_solution(3645534417226715722)
XLA Ops:
  0.0 2.4 %pack.1 = (bf16[256,512]{1,0:T(8,128)(2,1)}, bf16[224,2304]{1,0:T(8,128)(2,1)}) custom-call(bf16[256,256]{1,0:T(8,128)(2,1)} %refs_0_.1, bf16[256,256]{1,0:T(8,128)(2,1)} %refs_1_.1, bf16[224,1792]{1,0:T(8,128)(2,1)} %refs_2_.1, bf16[224,256]{1,0:T(8,128)(2,1)} %refs_3_.1, bf16[224,256]{1,0:T(8,128)(2,1)} %refs_4_.1), custom_call_target="tpu_custom_call" | custom-call | flops 1 | bytes 1 | tf_op jit(solution)/shard_map/pack/pallas_call | solution.py:441
  2.4 4.9 %collective-permute-start = (bf16[256,512]{1,0:T(8,128)(2,1)}, bf16[256,512]{1,0:T(8,128)(2,1)S(1)}, u32[]{:S(2)}, u32[]{:S(2)}) collective-permute-start(bf16[256,512]{1,0:T(8,128)(2,1)} %get-tuple-element.27.even_ref.k_own_ref.v_own_ref), channel_id=1, source_target_pairs={{0,4},{2,6},{4,8},{6,10},{8,12},{10,14},{12,16},{14,18},{16,20},{1... | collective-permute-start | bytes 786440 | tf_op jit(solution)/shard_map/ppermute | solution.py:529
  7.3 1.3 %collective-permute-start.5 = (bf16[224,2304]{1,0:T(8,128)(2,1)}, bf16[224,2304]{1,0:T(8,128)(2,1)}, u32[]{:S(2)}, u32[]{:S(2)}) collective-permute-start(bf16[224,2304]{1,0:T(8,128)(2,1)} %get-tuple-element.36.refs_0_), channel_id=1, source_target_pairs={{8,0},{10,2},{12,4},{14,6},{16,8},{18,10},{20,12},{22,14},{24,16},... | collective-permute-start | bytes 3096584 | tf_op jit(solution)/shard_map/ppermute | solution.py:539
  8.6 5.5 %collective-permute-start.4 = (bf16[224,2304]{1,0:T(8,128)(2,1)}, bf16[224,2304]{1,0:T(8,128)(2,1)}, u32[]{:S(2)}, u32[]{:S(2)}) collective-permute-start(bf16[224,2304]{1,0:T(8,128)(2,1)} %get-tuple-element.36.refs_0_), channel_id=1, source_target_pairs={{0,8},{2,10},{4,12},{6,14},{8,16},{10,18},{12,20},{14,22},{16,24},... | collective-permute-start | bytes 3096584 | tf_op jit(solution)/shard_map/ppermute | solution.py:539
  15.2 1.5 %collective-permute-done.1.k_near_ref.v_near_ref = bf16[256,512]{1,0:T(8,128)(2,1)S(1)} collective-permute-done((bf16[256,512]{1,0:T(8,128)(2,1)S(1)}, bf16[256,512]{1,0:T(8,128)(2,1)S(1)}, u32[]{:S(2)}, u32[]{:S(2)}) %collective-permute-start.1) | collective-permute-done | bytes 262176 | tf_op jit(solution)/shard_map/ppermute | solution.py:534
  17.4 5.8 %attention.2 = (bf16[256,896]{1,0:T(8,128)(2,1)}, f32[256,256]{1,0:T(8,128)}, bf16[256,256]{1,0:T(8,128)(2,1)}, bf16[256,256]{1,0:T(8,128)(2,1)}) custom-call(s32[1]{0:T(128)} %bitcast.first_ref, s32[4]{0:T(128)} %docs_ref.3, bf16[256,1792]{1,0:T(8,128)(2,1)} %q_ref.3, bf16[256,1792]{1,0:T(8,128)(2,1)} %do_ref.3, bf16[256,1792]{1,0:T(8,128)(2,1)} %o_ref.3, ...), custom_call_target="tpu_custom_call" | custom-call | flops 900000000 | bytes 1 | tf_op jit(solution)/shard_map/attention/pallas_call | solution.py:132
  23.2 1.5 %collective-permute-start.6 = (bf16[256,896]{1,0:T(8,128)(2,1)}, bf16[256,896]{1,0:T(8,128)(2,1)S(1)}, u32[]{:S(2)}, u32[]{:S(2)}) collective-permute-start(bf16[256,896]{1,0:T(8,128)(2,1)} %get-tuple-element.28.refs_0_), channel_id=1, source_target_pairs={{0,4},{2,6},{4,0},{6,2},{8,12},{10,14},{12,8},{14,10},{16,20},{18,... | collective-permute-start | bytes 1376264 | tf_op jit(solution)/shard_map/ppermute | solution.py:534
  24.7 6.3 %attention.3 = (bf16[256,896]{1,0:T(8,128)(2,1)}, f32[256,512]{1,0:T(8,128)}, bf16[256,512]{1,0:T(8,128)(2,1)}, bf16[256,512]{1,0:T(8,128)(2,1)}) custom-call(s32[1]{0:T(128)} %bitcast.first_ref, s32[4]{0:T(128)} %docs_ref.3, bf16[256,1792]{1,0:T(8,128)(2,1)} %q_ref.3, bf16[256,1792]{1,0:T(8,128)(2,1)} %do_ref.3, bf16[256,1792]{1,0:T(8,128)(2,1)} %o_ref.3, ...), custom_call_target="tpu_custom_call" | custom-call | flops 900000000 | bytes 1 | tf_op jit(solution)/shard_map/attention/pallas_call | solution.py:132
  31.0 1.7 %collective-permute-done.2.got = bf16[256,512]{1,0:T(8,128)(2,1)S(1)} collective-permute-done((bf16[256,512]{1,0:T(8,128)(2,1)}, bf16[256,512]{1,0:T(8,128)(2,1)S(1)}, u32[]{:S(2)}, u32[]{:S(2)}) %collective-permute-start.2) | collective-permute-done | bytes 262176 | tf_op jit(solution)/shard_map/ppermute | solution.py:534
  33.8 1.3 %collective-permute-start.3 = (bf16[256,512]{1,0:T(8,128)(2,1)S(1)}, bf16[256,512]{1,0:T(8,128)(2,1)}, u32[]{:S(2)}, u32[]{:S(2)}) collective-permute-start(bf16[256,512]{1,0:T(8,128)(2,1)S(1)} %merge.1), channel_id=1, source_target_pairs={{4,0},{6,2},{8,4},{10,6},{12,8},{14,10},{16,12},{18,14},{20,16},{2... | collective-permute-start | bytes 786440 | tf_op jit(solution)/shard_map/ppermute | solution.py:529
  36.8 1.3 %collective-permute-start.13 = (bf16[224,2304]{1,0:T(8,128)(2,1)}, bf16[224,2304]{1,0:T(8,128)(2,1)}, u32[]{:S(2)}, u32[]{:S(2)}) collective-permute-start(bf16[224,2304]{1,0:T(8,128)(2,1)} %gate.2.refs_1_.refs_10_.refs_0_.refs_2_.refs_5_), channel_id=1, source_target_pairs={{8,0},{10,2},{12,4},{14,6},{16,8},{18,10},{20,12},{22,14},{9,1},{1... | collective-permute-start | bytes 3096584 | tf_op jit(solution)/shard_map/ppermute | solution.py:539
  38.1 1.6 %collective-permute-start.12 = (bf16[224,2304]{1,0:T(8,128)(2,1)}, bf16[224,2304]{1,0:T(8,128)(2,1)}, u32[]{:S(2)}, u32[]{:S(2)}) collective-permute-start(bf16[224,2304]{1,0:T(8,128)(2,1)} %collective-permute-done.4.refs_0_.refs_11_.refs_1_.refs_3_.refs_6_), channel_id=1, source_target_pairs={{8,16},{10,18},{12,20},{14,22},{16,24},{18,26},{20,28},{22,30},{9,... | collective-permute-start | bytes 3096584 | tf_op jit(solution)/shard_map/ppermute | solution.py:539
  39.7 4.5 %collective-permute-done.3.back = bf16[256,512]{1,0:T(8,128)(2,1)} collective-permute-done((bf16[256,512]{1,0:T(8,128)(2,1)S(1)}, bf16[256,512]{1,0:T(8,128)(2,1)}, u32[]{:S(2)}, u32[]{:S(2)}) %collective-permute-start.3) | collective-permute-done | bytes 262176 | tf_op jit(solution)/shard_map/ppermute | solution.py:529
  44.3 2.3 %join.1.refs_1_ = bf16[256,1408]{1,0:T(8,128)(2,1)} custom-call(bf16[256,896]{1,0:T(8,128)(2,1)} %get-tuple-element.32.dq, f32[256,512]{1,0:T(8,128)} %get-tuple-element.33.own, bf16[256,512]{1,0:T(8,128)(2,1)} %copy-done.4, bf16[256,512]{1,0:T(8,128)(2,1)} %collective-permute-done.3.back, ...), custom_call_target="tpu_custom_call" | custom-call | flops 1000000000 | bytes 1 | tf_op jit(solution)/shard_map/join/pallas_call | solution.py:515
  46.6 2.1 %collective-permute-start.7 = (bf16[256,1408]{1,0:T(8,128)(2,1)}, bf16[256,1408]{1,0:T(8,128)(2,1)S(1)}, u32[]{:S(2)}, u32[]{:S(2)}) collective-permute-start(bf16[256,1408]{1,0:T(8,128)(2,1)} %join.1.refs_1_), channel_id=1, source_target_pairs={{0,4},{2,6},{4,0},{6,2},{8,12},{10,14},{12,8},{14,10},{16,20},{18,... | collective-permute-start | bytes 2162696 | tf_op jit(solution)/shard_map/ppermute | solution.py:534
  49.2 2.1 %collective-permute-done.8.refs_4_ = bf16[256,896]{1,0:T(8,128)(2,1)S(1)} collective-permute-done((bf16[256,896]{1,0:T(8,128)(2,1)}, bf16[256,896]{1,0:T(8,128)(2,1)S(1)}, u32[]{:S(2)}, u32[]{:S(2)}) %collective-permute-start.8) | collective-permute-done | bytes 458784 | tf_op jit(solution)/shard_map/ppermute | solution.py:534
  51.5 12.7 %collective-permute-done.7.refs_3_ = bf16[256,1408]{1,0:T(8,128)(2,1)S(1)} collective-permute-done((bf16[256,1408]{1,0:T(8,128)(2,1)}, bf16[256,1408]{1,0:T(8,128)(2,1)S(1)}, u32[]{:S(2)}, u32[]{:S(2)}) %collective-permute-start.7) | collective-permute-done | bytes 720928 | tf_op jit(solution)/shard_map/ppermute | solution.py:534
  64.2 2.1 %collective-permute-done.13.refs_2_.refs_9_.refs_1_.refs_4_ = bf16[224,2304]{1,0:T(8,128)(2,1)} collective-permute-done((bf16[224,2304]{1,0:T(8,128)(2,1)}, bf16[224,2304]{1,0:T(8,128)(2,1)}, u32[]{:S(2)}, u32[]{:S(2)}) %collective-permute-start.13) | collective-permute-done | bytes 1032224 | tf_op jit(solution)/shard_map/ppermute | solution.py:539
  66.3 5.6 %collective-permute-start.14 = (bf16[224,2304]{1,0:T(8,128)(2,1)}, bf16[224,2304]{1,0:T(8,128)(2,1)}, u32[]{:S(2)}, u32[]{:S(2)}) collective-permute-start(bf16[224,2304]{1,0:T(8,128)(2,1)} %gate.3.refs_8_.own), channel_id=1, source_target_pairs={{0,24},{2,26},{4,28},{6,30},{24,0},{26,2},{28,4},{30,6},{1,25},{3,... | collective-permute-start | bytes 3096584 | tf_op jit(solution)/shard_map/ppermute | solution.py:539
  72.0 6.1 %project_send.1 = (bf16[256,896]{1,0:T(8,128)(2,1)}, bf16[1024,2304]{1,0:T(8,128)(2,1)}) custom-call(bf16[256,896]{1,0:T(8,128)(2,1)} %get-tuple-element.28.refs_0_, bf16[256,1408]{1,0:T(8,128)(2,1)} %join.1.refs_1_, bf16[256,896]{1,0:T(8,128)(2,1)} %copy-done.9, bf16[256,1408]{1,0:T(8,128)(2,1)} %copy-done.7, bf16[256,896]{1,0:T(8,128)(2,1)} %copy-done.8, ...), custom_call_target="tpu_custom_call" | custom-call | flops 1 | bytes 1 | tf_op jit(solution)/shard_map/project_send/pallas_call | solution.py:285
  78.1 1.6 %collective-permute-start.15 = (bf16[256,896]{1,0:T(8,128)(2,1)}, bf16[256,896]{1,0:T(8,128)(2,1)S(1)}, u32[]{:S(2)}, u32[]{:S(2)}) collective-permute-start(bf16[256,896]{1,0:T(8,128)(2,1)} %get-tuple-element.38.refs_8_), channel_id=1, source_target_pairs={{0,1},{1,0},{2,3},{3,2},{4,5},{5,4},{6,7},{7,6},{8,9},{9,8},{10,11... | collective-permute-start | bytes 1376264 | tf_op jit(solution)/shard_map/ppermute | solution.py:650
  79.7 7.9 %project_keep.1 = (f32[4,256,224]{2,1,0:T(8,128)}, f32[4,256,224]{2,1,0:T(8,128)}, bf16[256,896]{1,0:T(8,128)(2,1)}) custom-call(bf16[1024,2304]{1,0:T(8,128)(2,1)} %get-tuple-element.37.held, bf16[224,2304]{1,0:T(8,128)(2,1)} %gate.3.refs_8_.own, bf16[224,2304]{1,0:T(8,128)(2,1)} %gate.2.refs_1_.refs_10_.refs_0_.refs_2_.refs_5_, ...), custom_call_target="tpu_custom_call" | custom-call | flops 1 | bytes 1 | tf_op jit(solution)/shard_map/project_keep/pallas_call | solution.py:285
  87.6 1.6 %collective-permute-start.16 = (bf16[256,896]{1,0:T(8,128)(2,1)}, bf16[256,896]{1,0:T(8,128)(2,1)S(1)}, u32[]{:S(2)}, u32[]{:S(2)}) collective-permute-start(bf16[256,896]{1,0:T(8,128)(2,1)} %get-tuple-element.41), channel_id=1, source_target_pairs={{1,0},{3,2},{5,4},{7,6},{9,8},{11,10},{13,12},{15,14},{16,17},{18,... | collective-permute-start | bytes 1376264 | tf_op jit(solution)/shard_map/ppermute | solution.py:547
  89.6 4.8 %collective-permute-done.14.refs_0_.refs_3_ = bf16[224,2304]{1,0:T(8,128)(2,1)} collective-permute-done((bf16[224,2304]{1,0:T(8,128)(2,1)}, bf16[224,2304]{1,0:T(8,128)(2,1)}, u32[]{:S(2)}, u32[]{:S(2)}) %collective-permute-start.14) | collective-permute-done | bytes 1032224 | tf_op jit(solution)/shard_map/ppermute | solution.py:539
  94.4 2.7 %project_last.1 = (f32[4,256,224]{2,1,0:T(8,128)S(1)}, bf16[256,512]{1,0:T(8,128)(2,1)S(1)}, bf16[256,384]{1,0:T(8,128)(2,1)S(1)}) custom-call(bf16[1024,2304]{1,0:T(8,128)(2,1)S(1)} %copy-done, bf16[224,2304]{1,0:T(8,128)(2,1)} %collective-permute-done.14.refs_0_.refs_3_, bf16[224,2304]{1,0:T(8,128)(2,1)} %collective-permute-done.13.refs_2_.refs_9_.refs_1_.refs_4_, ...), custom_call_target="tpu_custom_call" | custom-call | flops 1 | bytes 1 | tf_op jit(solution)/shard_map/project_last/pallas_call | solution.py:285
  97.2 3.4 %collective-permute-start.17 = (bf16[256,512]{1,0:T(8,128)(2,1)S(1)}, bf16[256,512]{1,0:T(8,128)(2,1)S(1)}, u32[]{:S(2)}, u32[]{:S(2)}) collective-permute-start(bf16[256,512]{1,0:T(8,128)(2,1)S(1)} %get-tuple-element.42), channel_id=1, source_target_pairs={{0,1},{2,3},{4,5},{6,7},{8,9},{10,11},{12,13},{14,15},{17,16},{19,... | collective-permute-start | bytes 786440 | tf_op jit(solution)/shard_map/ppermute | solution.py:547
  100.9 1.3 %collective-permute-start.18 = (bf16[256,384]{1,0:T(8,128)(2,1)S(1)}, bf16[256,384]{1,0:T(8,128)(2,1)S(1)}, u32[]{:S(2)}, u32[]{:S(2)}) collective-permute-start(bf16[256,384]{1,0:T(8,128)(2,1)S(1)} %get-tuple-element.43), channel_id=1, source_target_pairs={{0,1},{2,3},{4,5},{6,7},{8,9},{10,11},{12,13},{14,15},{17,16},{19,... | collective-permute-start | bytes 589832 | tf_op jit(solution)/shard_map/ppermute | solution.py:547
  104.4 2.0 %collective-permute-done.17.refs_0_ = bf16[256,512]{1,0:T(8,128)(2,1)S(1)} collective-permute-done((bf16[256,512]{1,0:T(8,128)(2,1)S(1)}, bf16[256,512]{1,0:T(8,128)(2,1)S(1)}, u32[]{:S(2)}, u32[]{:S(2)}) %collective-permute-start.17) | collective-permute-done | bytes 262176 | tf_op jit(solution)/shard_map/ppermute | solution.py:547
  107.6 1.3 %collective-permute-done.18.refs_1_ = bf16[256,384]{1,0:T(8,128)(2,1)S(1)} collective-permute-done((bf16[256,384]{1,0:T(8,128)(2,1)S(1)}, bf16[256,384]{1,0:T(8,128)(2,1)S(1)}, u32[]{:S(2)}, u32[]{:S(2)}) %collective-permute-start.18) | collective-permute-done | bytes 196640 | tf_op jit(solution)/shard_map/ppermute | solution.py:547
  109.2 2.3 %collective-permute-done.21.refs_2_ = bf16[256,224]{1,0:T(8,128)(2,1)S(1)} collective-permute-done((bf16[256,224]{1,0:T(8,128)(2,1)S(1)}, bf16[256,224]{1,0:T(8,128)(2,1)S(1)}, u32[]{:S(2)}, u32[]{:S(2)}) %collective-permute-start.21) | collective-permute-done | bytes 114720 | tf_op jit(solution)/shard_map/ppermute | solution.py:534
  111.5 2.8 %collective-permute-done.23.refs_4_ = bf16[256,224]{1,0:T(8,128)(2,1)S(1)} collective-permute-done((bf16[256,224]{1,0:T(8,128)(2,1)S(1)}, bf16[256,224]{1,0:T(8,128)(2,1)S(1)}, u32[]{:S(2)}, u32[]{:S(2)}) %collective-permute-start.23) | collective-permute-done | bytes 114720 | tf_op jit(solution)/shard_map/ppermute | solution.py:534
  114.3 1.6 %collective-permute-done.24.refs_5_ = bf16[256,224]{1,0:T(8,128)(2,1)S(1)} collective-permute-done((bf16[256,224]{1,0:T(8,128)(2,1)S(1)}, bf16[256,224]{1,0:T(8,128)(2,1)S(1)}, u32[]{:S(2)}, u32[]{:S(2)}) %collective-permute-start.24) | collective-permute-done | bytes 114720 | tf_op jit(solution)/shard_map/ppermute | solution.py:534
  (56 shorter events, 10.8 us)
Async XLA Ops:
  2.4 11.7 %collective-permute-start = (bf16[256,512]{1,0:T(8,128)(2,1)}, bf16[256,512]{1,0:T(8,128)(2,1)S(1)}, u32[]{:S(2)}, u32[]{:S(2)}) collective-permute-start(bf16[256,512]{1,0:T(8,128)(2,1)} %get-tuple-element.27.even_ref.k_own_ref.v_own_ref), channel_id=1, source_target_pairs={{0,4},{2,6},{4,8},{6,10},{8,12},{10,14},{12,16},{14,18},{16,20},{1... | collective-permute-start | bytes 786440 | tf_op jit(solution)/shard_map/ppermute | solution.py:529
  7.3 28.7 %collective-permute-start.5 = (bf16[224,2304]{1,0:T(8,128)(2,1)}, bf16[224,2304]{1,0:T(8,128)(2,1)}, u32[]{:S(2)}, u32[]{:S(2)}) collective-permute-start(bf16[224,2304]{1,0:T(8,128)(2,1)} %get-tuple-element.36.refs_0_), channel_id=1, source_target_pairs={{8,0},{10,2},{12,4},{14,6},{16,8},{18,10},{20,12},{22,14},{24,16},... | collective-permute-start | bytes 3096584 | tf_op jit(solution)/shard_map/ppermute | solution.py:539
  8.6 29.5 %collective-permute-start.4 = (bf16[224,2304]{1,0:T(8,128)(2,1)}, bf16[224,2304]{1,0:T(8,128)(2,1)}, u32[]{:S(2)}, u32[]{:S(2)}) collective-permute-start(bf16[224,2304]{1,0:T(8,128)(2,1)} %get-tuple-element.36.refs_0_), channel_id=1, source_target_pairs={{0,8},{2,10},{4,12},{6,14},{8,16},{10,18},{12,20},{14,22},{16,24},... | collective-permute-start | bytes 3096584 | tf_op jit(solution)/shard_map/ppermute | solution.py:539
  15.1 1.6 %copy-start.2 = (bf16[256,512]{1,0:T(8,128)(2,1)}, bf16[256,512]{1,0:T(8,128)(2,1)S(1)}, u32[]{:S(2)}) copy-start(bf16[256,512]{1,0:T(8,128)(2,1)S(1)} %collective-permute-done.odd_ref.k_far_ref.v_far_ref) | copy-start | bytes 786436
  15.1 1.6 %collective-permute-start.1 = (bf16[256,512]{1,0:T(8,128)(2,1)S(1)}, bf16[256,512]{1,0:T(8,128)(2,1)S(1)}, u32[]{:S(2)}, u32[]{:S(2)}) collective-permute-start(bf16[256,512]{1,0:T(8,128)(2,1)S(1)} %choose.1), channel_id=1, source_target_pairs={{0,2},{2,0},{4,6},{6,4},{8,10},{10,8},{12,14},{14,12},{16,18},{18,... | collective-permute-start | bytes 786440 | tf_op jit(solution)/shard_map/ppermute | solution.py:534
  23.2 12.8 %collective-permute-start.6 = (bf16[256,896]{1,0:T(8,128)(2,1)}, bf16[256,896]{1,0:T(8,128)(2,1)S(1)}, u32[]{:S(2)}, u32[]{:S(2)}) collective-permute-start(bf16[256,896]{1,0:T(8,128)(2,1)} %get-tuple-element.28.refs_0_), channel_id=1, source_target_pairs={{0,4},{2,6},{4,0},{6,2},{8,12},{10,14},{12,8},{14,10},{16,20},{18,... | collective-permute-start | bytes 1376264 | tf_op jit(solution)/shard_map/ppermute | solution.py:534
  31.0 1.7 %collective-permute-start.2 = (bf16[256,512]{1,0:T(8,128)(2,1)}, bf16[256,512]{1,0:T(8,128)(2,1)S(1)}, u32[]{:S(2)}, u32[]{:S(2)}) collective-permute-start(bf16[256,512]{1,0:T(8,128)(2,1)} %get-tuple-element.34), channel_id=1, source_target_pairs={{0,2},{2,0},{4,6},{6,4},{8,10},{10,8},{12,14},{14,12},{16,18},{18,... | collective-permute-start | bytes 786440 | tf_op jit(solution)/shard_map/ppermute | solution.py:534
  32.8 11.5 %copy-start.4 = (bf16[256,512]{1,0:T(8,128)(2,1)}, bf16[256,512]{1,0:T(8,128)(2,1)S(1)}, u32[]{:S(2)}) copy-start(bf16[256,512]{1,0:T(8,128)(2,1)S(1)} %collective-permute-done.2.got) | copy-start | bytes 786436
  33.8 10.4 %collective-permute-start.3 = (bf16[256,512]{1,0:T(8,128)(2,1)S(1)}, bf16[256,512]{1,0:T(8,128)(2,1)}, u32[]{:S(2)}, u32[]{:S(2)}) collective-permute-start(bf16[256,512]{1,0:T(8,128)(2,1)S(1)} %merge.1), channel_id=1, source_target_pairs={{4,0},{6,2},{8,4},{10,6},{12,8},{14,10},{16,12},{18,14},{20,16},{2... | collective-permute-start | bytes 786440 | tf_op jit(solution)/shard_map/ppermute | solution.py:529
  36.8 29.5 %collective-permute-start.13 = (bf16[224,2304]{1,0:T(8,128)(2,1)}, bf16[224,2304]{1,0:T(8,128)(2,1)}, u32[]{:S(2)}, u32[]{:S(2)}) collective-permute-start(bf16[224,2304]{1,0:T(8,128)(2,1)} %gate.2.refs_1_.refs_10_.refs_0_.refs_2_.refs_5_), channel_id=1, source_target_pairs={{8,0},{10,2},{12,4},{14,6},{16,8},{18,10},{20,12},{22,14},{9,1},{1... | collective-permute-start | bytes 3096584 | tf_op jit(solution)/shard_map/ppermute | solution.py:539
  38.1 28.2 %collective-permute-start.12 = (bf16[224,2304]{1,0:T(8,128)(2,1)}, bf16[224,2304]{1,0:T(8,128)(2,1)}, u32[]{:S(2)}, u32[]{:S(2)}) collective-permute-start(bf16[224,2304]{1,0:T(8,128)(2,1)} %collective-permute-done.4.refs_0_.refs_11_.refs_1_.refs_3_.refs_6_), channel_id=1, source_target_pairs={{8,16},{10,18},{12,20},{14,22},{16,24},{18,26},{20,28},{22,30},{9,... | collective-permute-start | bytes 3096584 | tf_op jit(solution)/shard_map/ppermute | solution.py:539
  46.6 17.6 %collective-permute-start.7 = (bf16[256,1408]{1,0:T(8,128)(2,1)}, bf16[256,1408]{1,0:T(8,128)(2,1)S(1)}, u32[]{:S(2)}, u32[]{:S(2)}) collective-permute-start(bf16[256,1408]{1,0:T(8,128)(2,1)} %join.1.refs_1_), channel_id=1, source_target_pairs={{0,4},{2,6},{4,0},{6,2},{8,12},{10,14},{12,8},{14,10},{16,20},{18,... | collective-permute-start | bytes 2162696 | tf_op jit(solution)/shard_map/ppermute | solution.py:534
  48.7 2.7 %collective-permute-start.8 = (bf16[256,896]{1,0:T(8,128)(2,1)}, bf16[256,896]{1,0:T(8,128)(2,1)S(1)}, u32[]{:S(2)}, u32[]{:S(2)}) collective-permute-start(bf16[256,896]{1,0:T(8,128)(2,1)} %get-tuple-element.28.refs_0_), channel_id=1, source_target_pairs={{0,2},{2,0},{4,6},{6,4},{8,10},{10,8},{12,14},{14,12},{16,18},{18,... | collective-permute-start | bytes 1376264 | tf_op jit(solution)/shard_map/ppermute | solution.py:534
  48.7 15.5 %collective-permute-start.10 = (bf16[256,896]{1,0:T(8,128)(2,1)}, bf16[256,896]{1,0:T(8,128)(2,1)}, u32[]{:S(2)}, u32[]{:S(2)}) collective-permute-start(bf16[256,896]{1,0:T(8,128)(2,1)} %copy-done.9), channel_id=1, source_target_pairs={{0,2},{2,0},{4,6},{6,4},{8,10},{10,8},{12,14},{14,12},{16,18},{18,... | collective-permute-start | bytes 1376264 | tf_op jit(solution)/shard_map/ppermute | solution.py:534
  51.4 12.8 %copy-start.8 = (bf16[256,896]{1,0:T(8,128)(2,1)}, bf16[256,896]{1,0:T(8,128)(2,1)S(1)}, u32[]{:S(2)}) copy-start(bf16[256,896]{1,0:T(8,128)(2,1)S(1)} %collective-permute-done.8.refs_4_) | copy-start | bytes 1376260
  51.4 20.6 %collective-permute-start.9 = (bf16[256,1408]{1,0:T(8,128)(2,1)}, bf16[256,1408]{1,0:T(8,128)(2,1)}, u32[]{:S(2)}, u32[]{:S(2)}) collective-permute-start(bf16[256,1408]{1,0:T(8,128)(2,1)} %join.1.refs_1_), channel_id=1, source_target_pairs={{0,2},{2,0},{4,6},{6,4},{8,10},{10,8},{12,14},{14,12},{16,18},{18,... | collective-permute-start | bytes 2162696 | tf_op jit(solution)/shard_map/ppermute | solution.py:534
  64.2 2.1 %copy-start.7 = (bf16[256,1408]{1,0:T(8,128)(2,1)}, bf16[256,1408]{1,0:T(8,128)(2,1)S(1)}, u32[]{:S(2)}) copy-start(bf16[256,1408]{1,0:T(8,128)(2,1)S(1)} %collective-permute-done.7.refs_3_) | copy-start | bytes 2162692
  64.2 7.8 %collective-permute-start.11 = (bf16[256,1408]{1,0:T(8,128)(2,1)S(1)}, bf16[256,1408]{1,0:T(8,128)(2,1)}, u32[]{:S(2)}, u32[]{:S(2)}) collective-permute-start(bf16[256,1408]{1,0:T(8,128)(2,1)S(1)} %collective-permute-done.7.refs_3_), channel_id=1, source_target_pairs={{0,2},{2,0},{4,6},{6,4},{8,10},{10,8},{12,14},{14,12},{16,18},{18,... | collective-permute-start | bytes 2162696 | tf_op jit(solution)/shard_map/ppermute | solution.py:534
  66.3 28.1 %collective-permute-start.14 = (bf16[224,2304]{1,0:T(8,128)(2,1)}, bf16[224,2304]{1,0:T(8,128)(2,1)}, u32[]{:S(2)}, u32[]{:S(2)}) collective-permute-start(bf16[224,2304]{1,0:T(8,128)(2,1)} %gate.3.refs_8_.own), channel_id=1, source_target_pairs={{0,24},{2,26},{4,28},{6,30},{24,0},{26,2},{28,4},{30,6},{1,25},{3,... | collective-permute-start | bytes 3096584 | tf_op jit(solution)/shard_map/ppermute | solution.py:539
  78.1 11.5 %collective-permute-start.15 = (bf16[256,896]{1,0:T(8,128)(2,1)}, bf16[256,896]{1,0:T(8,128)(2,1)S(1)}, u32[]{:S(2)}, u32[]{:S(2)}) collective-permute-start(bf16[256,896]{1,0:T(8,128)(2,1)} %get-tuple-element.38.refs_8_), channel_id=1, source_target_pairs={{0,1},{1,0},{2,3},{3,2},{4,5},{5,4},{6,7},{7,6},{8,9},{9,8},{10,11... | collective-permute-start | bytes 1376264 | tf_op jit(solution)/shard_map/ppermute | solution.py:650
  79.7 14.8 %copy-start = (bf16[1024,2304]{1,0:T(8,128)(2,1)S(1)}, bf16[1024,2304]{1,0:T(8,128)(2,1)}, u32[]{:S(2)}) copy-start(bf16[1024,2304]{1,0:T(8,128)(2,1)} %get-tuple-element.37.held) | copy-start | bytes 14155780
  87.6 13.0 %copy-start.10 = (f32[4,256,224]{2,1,0:T(8,128)S(1)}, f32[4,256,224]{2,1,0:T(8,128)}, u32[]{:S(2)}) copy-start(f32[4,256,224]{2,1,0:T(8,128)} %get-tuple-element.44) | copy-start | bytes 2752516
  87.6 18.7 %copy-start.3 = (f32[4,256,224]{2,1,0:T(8,128)S(1)}, f32[4,256,224]{2,1,0:T(8,128)}, u32[]{:S(2)}) copy-start(f32[4,256,224]{2,1,0:T(8,128)} %get-tuple-element.40.mate_full) | copy-start | bytes 2752516
  87.6 15.8 %collective-permute-start.16 = (bf16[256,896]{1,0:T(8,128)(2,1)}, bf16[256,896]{1,0:T(8,128)(2,1)S(1)}, u32[]{:S(2)}, u32[]{:S(2)}) collective-permute-start(bf16[256,896]{1,0:T(8,128)(2,1)} %get-tuple-element.41), channel_id=1, source_target_pairs={{1,0},{3,2},{5,4},{7,6},{9,8},{11,10},{13,12},{15,14},{16,17},{18,... | collective-permute-start | bytes 1376264 | tf_op jit(solution)/shard_map/ppermute | solution.py:547
  97.2 9.2 %collective-permute-start.17 = (bf16[256,512]{1,0:T(8,128)(2,1)S(1)}, bf16[256,512]{1,0:T(8,128)(2,1)S(1)}, u32[]{:S(2)}, u32[]{:S(2)}) collective-permute-start(bf16[256,512]{1,0:T(8,128)(2,1)S(1)} %get-tuple-element.42), channel_id=1, source_target_pairs={{0,1},{2,3},{4,5},{6,7},{8,9},{10,11},{12,13},{14,15},{17,16},{19,... | collective-permute-start | bytes 786440 | tf_op jit(solution)/shard_map/ppermute | solution.py:547
  100.8 3.6 %collective-permute-start.19 = (bf16[256,224]{1,0:T(8,128)(2,1)S(1)}, bf16[256,224]{1,0:T(8,128)(2,1)S(1)}, u32[]{:S(2)}, u32[]{:S(2)}) collective-permute-start(bf16[256,224]{1,0:T(8,128)(2,1)S(1)} %get-tuple-element.52), channel_id=1, source_target_pairs={{0,2},{2,0},{4,6},{6,4},{8,10},{10,8},{12,14},{14,12},{16,18},{18,... | collective-permute-start | bytes 344072 | tf_op jit(solution)/shard_map/ppermute | solution.py:534
  100.9 8.1 %collective-permute-start.18 = (bf16[256,384]{1,0:T(8,128)(2,1)S(1)}, bf16[256,384]{1,0:T(8,128)(2,1)S(1)}, u32[]{:S(2)}, u32[]{:S(2)}) collective-permute-start(bf16[256,384]{1,0:T(8,128)(2,1)S(1)} %get-tuple-element.43), channel_id=1, source_target_pairs={{0,1},{2,3},{4,5},{6,7},{8,9},{10,11},{12,13},{14,15},{17,16},{19,... | collective-permute-start | bytes 589832 | tf_op jit(solution)/shard_map/ppermute | solution.py:547
  102.2 7.0 %collective-permute-start.22 = (bf16[256,224]{1,0:T(8,128)(2,1)S(1)}, bf16[256,224]{1,0:T(8,128)(2,1)S(1)}, u32[]{:S(2)}, u32[]{:S(2)}) collective-permute-start(bf16[256,224]{1,0:T(8,128)(2,1)S(1)} %get-tuple-element.49), channel_id=1, source_target_pairs={{0,6},{2,4},{4,2},{6,0},{8,14},{10,12},{12,10},{14,8},{16,22},{18,... | collective-permute-start | bytes 344072 | tf_op jit(solution)/shard_map/ppermute | solution.py:534
  103.4 8.1 %collective-permute-start.21 = (bf16[256,224]{1,0:T(8,128)(2,1)S(1)}, bf16[256,224]{1,0:T(8,128)(2,1)S(1)}, u32[]{:S(2)}, u32[]{:S(2)}) collective-permute-start(bf16[256,224]{1,0:T(8,128)(2,1)S(1)} %get-tuple-element.50), channel_id=1, source_target_pairs={{0,4},{2,6},{4,0},{6,2},{8,12},{10,14},{12,8},{14,10},{16,20},{18,... | collective-permute-start | bytes 344072 | tf_op jit(solution)/shard_map/ppermute | solution.py:534
  106.6 7.7 %collective-permute-start.23 = (bf16[256,224]{1,0:T(8,128)(2,1)S(1)}, bf16[256,224]{1,0:T(8,128)(2,1)S(1)}, u32[]{:S(2)}, u32[]{:S(2)}) collective-permute-start(bf16[256,224]{1,0:T(8,128)(2,1)S(1)} %get-tuple-element.45.refs_2_), channel_id=1, source_target_pairs={{0,4},{2,6},{4,0},{6,2},{8,12},{10,14},{12,8},{14,10},{16,20},{18,... | collective-permute-start | bytes 344072 | tf_op jit(solution)/shard_map/ppermute | solution.py:534
  107.6 8.2 %collective-permute-start.24 = (bf16[256,224]{1,0:T(8,128)(2,1)S(1)}, bf16[256,224]{1,0:T(8,128)(2,1)S(1)}, u32[]{:S(2)}, u32[]{:S(2)}) collective-permute-start(bf16[256,224]{1,0:T(8,128)(2,1)S(1)} %get-tuple-element.46.refs_3_), channel_id=1, source_target_pairs={{0,6},{2,4},{4,2},{6,0},{8,14},{10,12},{12,10},{14,8},{16,22},{18,... | collective-permute-start | bytes 344072 | tf_op jit(solution)/shard_map/ppermute | solution.py:534
  109.1 7.0 %collective-permute-start.20 = (bf16[256,224]{1,0:T(8,128)(2,1)S(1)}, bf16[256,224]{1,0:T(8,128)(2,1)S(1)}, u32[]{:S(2)}, u32[]{:S(2)}) collective-permute-start(bf16[256,224]{1,0:T(8,128)(2,1)S(1)} %get-tuple-element.48), channel_id=1, source_target_pairs={{0,2},{2,0},{4,6},{6,4},{8,10},{10,8},{12,14},{14,12},{16,18},{18,... | collective-permute-start | bytes 344072 | tf_op jit(solution)/shard_map/ppermute | solution.py:534
  (4 other events, 3.5 us)

commit v7 on v6

--- a/solution.py
+++ b/solution.py
@@ -658,7 +658,7 @@
         return array[:, k * rows : (k + 1) * rows].astype(F32)
 
     sets = [returned([(keep[r] + lanes(got, r)).astype(BF16) for r in range(INNER)])]
-    blocks, after = [None] * INNER, sets[0][1:2]
+    blocks, after = [None] * INNER, sets[0][2:3]
     for k, picks in enumerate((order[:2], order[2:])):
         after = combine(layers, order, picks, last_full, mate_full, got_mate, gots[: k + 1], after)
         for r, block in zip(picks, after):

time: 118 us -> 116 us (0.983)
  waiting for transfers between devices: 40.7 us -> 38.4 us
    ppermute x3, waiting for transfers between devices: 3.26 us -> 1.77 us  [crossed(): return lax.ppermute(array, ('seq', 'head'), pairs)]
  transfers between devices with their start and end apart: 25 -> 25, of which waited for: 14 -> 14; matrix products, arithmetic and copies ran while one was open for 0% -> 0% of each run, Pallas kernels for 27% -> 28%
where the time goes in v7:
time: 116 us; the launch traced here: 115 us
  waiting for transfers between devices  38.4 us (33%)
  starting transfers between devices  37.5 us (32%)
  Pallas kernels  35.4 us (31%)
  local copies, waits for them, and re-layouts  3.49 us (3%)
    ppermute x14, waiting for transfers between devices, swapped(): return lax.ppermute(array, 'seq', [(i, i ^ bits) for i in range(peers)])  24.8 us
    pallas_call x3, Pallas kernels, project(): pl.pallas_call(functools.partial(kernel, layers), in_specs=[vmem] * in_vm...  16.8 us
    ppermute x5, starting transfers between devices, layered(): return lax.ppermute(array, 'seq', pairs)  15.4 us
    pallas_call x2, Pallas kernels, attention(): pl.pallas_call(functools.partial(attention_kernel, group, groups), grid=(...  12.1 us
    ppermute x14, starting transfers between devices, swapped(): return lax.ppermute(array, 'seq', [(i, i ^ bits) for i in range(peers)])  8.13 us
    ppermute x5, waiting for transfers between devices, layered(): return lax.ppermute(array, 'seq', pairs)  6.96 us
    ppermute x3, starting transfers between devices, crossed(): return lax.ppermute(array, ('seq', 'head'), pairs)  6.3 us
    ppermute x2, starting transfers between devices, shifted(): return lax.ppermute(array, 'seq', pairs)  6.18 us
  transfers between devices with their start and end apart: 25, of which 14 were waited for; matrix products, arithmetic and copies ran while one was open for 0% of the time, Pallas kernels for 28%

profile of v7, /device:TPU:0, one launch (start us, length us, event | category | flops | bytes accessed | tf_op | source)
XLA Modules:
  0.0 115.3 jit_solution(1710084985786514947)
XLA Ops:
  0.0 2.4 %pack.1 = (bf16[256,512]{1,0:T(8,128)(2,1)}, bf16[224,2304]{1,0:T(8,128)(2,1)}) custom-call(bf16[256,256]{1,0:T(8,128)(2,1)} %refs_0_.1, bf16[256,256]{1,0:T(8,128)(2,1)} %refs_1_.1, bf16[224,1792]{1,0:T(8,128)(2,1)} %refs_2_.1, bf16[224,256]{1,0:T(8,128)(2,1)} %refs_3_.1, bf16[224,256]{1,0:T(8,128)(2,1)} %refs_4_.1), custom_call_target="tpu_custom_call" | custom-call | flops 1 | bytes 1 | tf_op jit(solution)/shard_map/pack/pallas_call | solution.py:441
  2.4 4.9 %collective-permute-start = (bf16[256,512]{1,0:T(8,128)(2,1)}, bf16[256,512]{1,0:T(8,128)(2,1)S(1)}, u32[]{:S(2)}, u32[]{:S(2)}) collective-permute-start(bf16[256,512]{1,0:T(8,128)(2,1)} %get-tuple-element.27.even_ref.k_own_ref.v_own_ref), channel_id=1, source_target_pairs={{0,4},{2,6},{4,8},{6,10},{8,12},{10,14},{12,16},{14,18},{16,20},{1... | collective-permute-start | bytes 786440 | tf_op jit(solution)/shard_map/ppermute | solution.py:529
  7.3 1.3 %collective-permute-start.5 = (bf16[224,2304]{1,0:T(8,128)(2,1)}, bf16[224,2304]{1,0:T(8,128)(2,1)}, u32[]{:S(2)}, u32[]{:S(2)}) collective-permute-start(bf16[224,2304]{1,0:T(8,128)(2,1)} %get-tuple-element.36.refs_0_), channel_id=1, source_target_pairs={{8,0},{10,2},{12,4},{14,6},{16,8},{18,10},{20,12},{22,14},{24,16},... | collective-permute-start | bytes 3096584 | tf_op jit(solution)/shard_map/ppermute | solution.py:539
  8.6 5.5 %collective-permute-start.4 = (bf16[224,2304]{1,0:T(8,128)(2,1)}, bf16[224,2304]{1,0:T(8,128)(2,1)}, u32[]{:S(2)}, u32[]{:S(2)}) collective-permute-start(bf16[224,2304]{1,0:T(8,128)(2,1)} %get-tuple-element.36.refs_0_), channel_id=1, source_target_pairs={{0,8},{2,10},{4,12},{6,14},{8,16},{10,18},{12,20},{14,22},{16,24},... | collective-permute-start | bytes 3096584 | tf_op jit(solution)/shard_map/ppermute | solution.py:539
  15.2 1.5 %collective-permute-done.1.k_near_ref.v_near_ref = bf16[256,512]{1,0:T(8,128)(2,1)S(1)} collective-permute-done((bf16[256,512]{1,0:T(8,128)(2,1)S(1)}, bf16[256,512]{1,0:T(8,128)(2,1)S(1)}, u32[]{:S(2)}, u32[]{:S(2)}) %collective-permute-start.1) | collective-permute-done | bytes 262176 | tf_op jit(solution)/shard_map/ppermute | solution.py:534
  17.4 5.8 %attention.2 = (bf16[256,896]{1,0:T(8,128)(2,1)}, f32[256,256]{1,0:T(8,128)}, bf16[256,256]{1,0:T(8,128)(2,1)}, bf16[256,256]{1,0:T(8,128)(2,1)}) custom-call(s32[1]{0:T(128)} %bitcast.first_ref, s32[4]{0:T(128)} %docs_ref.3, bf16[256,1792]{1,0:T(8,128)(2,1)} %q_ref.3, bf16[256,1792]{1,0:T(8,128)(2,1)} %do_ref.3, bf16[256,1792]{1,0:T(8,128)(2,1)} %o_ref.3, ...), custom_call_target="tpu_custom_call" | custom-call | flops 900000000 | bytes 1 | tf_op jit(solution)/shard_map/attention/pallas_call | solution.py:132
  23.2 1.5 %collective-permute-start.6 = (bf16[256,896]{1,0:T(8,128)(2,1)}, bf16[256,896]{1,0:T(8,128)(2,1)S(1)}, u32[]{:S(2)}, u32[]{:S(2)}) collective-permute-start(bf16[256,896]{1,0:T(8,128)(2,1)} %get-tuple-element.28.refs_0_), channel_id=1, source_target_pairs={{0,4},{2,6},{4,0},{6,2},{8,12},{10,14},{12,8},{14,10},{16,20},{18,... | collective-permute-start | bytes 1376264 | tf_op jit(solution)/shard_map/ppermute | solution.py:534
  24.7 6.3 %attention.3 = (bf16[256,896]{1,0:T(8,128)(2,1)}, f32[256,512]{1,0:T(8,128)}, bf16[256,512]{1,0:T(8,128)(2,1)}, bf16[256,512]{1,0:T(8,128)(2,1)}) custom-call(s32[1]{0:T(128)} %bitcast.first_ref, s32[4]{0:T(128)} %docs_ref.3, bf16[256,1792]{1,0:T(8,128)(2,1)} %q_ref.3, bf16[256,1792]{1,0:T(8,128)(2,1)} %do_ref.3, bf16[256,1792]{1,0:T(8,128)(2,1)} %o_ref.3, ...), custom_call_target="tpu_custom_call" | custom-call | flops 900000000 | bytes 1 | tf_op jit(solution)/shard_map/attention/pallas_call | solution.py:132
  31.0 1.7 %collective-permute-done.2.got = bf16[256,512]{1,0:T(8,128)(2,1)S(1)} collective-permute-done((bf16[256,512]{1,0:T(8,128)(2,1)}, bf16[256,512]{1,0:T(8,128)(2,1)S(1)}, u32[]{:S(2)}, u32[]{:S(2)}) %collective-permute-start.2) | collective-permute-done | bytes 262176 | tf_op jit(solution)/shard_map/ppermute | solution.py:534
  33.8 1.3 %collective-permute-start.3 = (bf16[256,512]{1,0:T(8,128)(2,1)S(1)}, bf16[256,512]{1,0:T(8,128)(2,1)}, u32[]{:S(2)}, u32[]{:S(2)}) collective-permute-start(bf16[256,512]{1,0:T(8,128)(2,1)S(1)} %merge.1), channel_id=1, source_target_pairs={{4,0},{6,2},{8,4},{10,6},{12,8},{14,10},{16,12},{18,14},{20,16},{2... | collective-permute-start | bytes 786440 | tf_op jit(solution)/shard_map/ppermute | solution.py:529
  36.8 1.3 %collective-permute-start.13 = (bf16[224,2304]{1,0:T(8,128)(2,1)}, bf16[224,2304]{1,0:T(8,128)(2,1)}, u32[]{:S(2)}, u32[]{:S(2)}) collective-permute-start(bf16[224,2304]{1,0:T(8,128)(2,1)} %gate.2.refs_1_.refs_10_.refs_0_.refs_2_.refs_5_), channel_id=1, source_target_pairs={{8,0},{10,2},{12,4},{14,6},{16,8},{18,10},{20,12},{22,14},{9,1},{1... | collective-permute-start | bytes 3096584 | tf_op jit(solution)/shard_map/ppermute | solution.py:539
  38.1 1.6 %collective-permute-start.12 = (bf16[224,2304]{1,0:T(8,128)(2,1)}, bf16[224,2304]{1,0:T(8,128)(2,1)}, u32[]{:S(2)}, u32[]{:S(2)}) collective-permute-start(bf16[224,2304]{1,0:T(8,128)(2,1)} %collective-permute-done.4.refs_0_.refs_11_.refs_1_.refs_3_.refs_6_), channel_id=1, source_target_pairs={{8,16},{10,18},{12,20},{14,22},{16,24},{18,26},{20,28},{22,30},{9,... | collective-permute-start | bytes 3096584 | tf_op jit(solution)/shard_map/ppermute | solution.py:539
  39.7 4.5 %collective-permute-done.3.back = bf16[256,512]{1,0:T(8,128)(2,1)} collective-permute-done((bf16[256,512]{1,0:T(8,128)(2,1)S(1)}, bf16[256,512]{1,0:T(8,128)(2,1)}, u32[]{:S(2)}, u32[]{:S(2)}) %collective-permute-start.3) | collective-permute-done | bytes 262176 | tf_op jit(solution)/shard_map/ppermute | solution.py:529
  44.3 2.3 %join.1.refs_1_ = bf16[256,1408]{1,0:T(8,128)(2,1)} custom-call(bf16[256,896]{1,0:T(8,128)(2,1)} %get-tuple-element.32.dq, f32[256,512]{1,0:T(8,128)} %get-tuple-element.33.own, bf16[256,512]{1,0:T(8,128)(2,1)} %copy-done.4, bf16[256,512]{1,0:T(8,128)(2,1)} %collective-permute-done.3.back, ...), custom_call_target="tpu_custom_call" | custom-call | flops 1000000000 | bytes 1 | tf_op jit(solution)/shard_map/join/pallas_call | solution.py:515
  46.6 2.1 %collective-permute-start.7 = (bf16[256,1408]{1,0:T(8,128)(2,1)}, bf16[256,1408]{1,0:T(8,128)(2,1)S(1)}, u32[]{:S(2)}, u32[]{:S(2)}) collective-permute-start(bf16[256,1408]{1,0:T(8,128)(2,1)} %join.1.refs_1_), channel_id=1, source_target_pairs={{0,4},{2,6},{4,0},{6,2},{8,12},{10,14},{12,8},{14,10},{16,20},{18,... | collective-permute-start | bytes 2162696 | tf_op jit(solution)/shard_map/ppermute | solution.py:534
  49.2 2.1 %collective-permute-done.8.refs_4_ = bf16[256,896]{1,0:T(8,128)(2,1)S(1)} collective-permute-done((bf16[256,896]{1,0:T(8,128)(2,1)}, bf16[256,896]{1,0:T(8,128)(2,1)S(1)}, u32[]{:S(2)}, u32[]{:S(2)}) %collective-permute-start.8) | collective-permute-done | bytes 458784 | tf_op jit(solution)/shard_map/ppermute | solution.py:534
  51.5 12.7 %collective-permute-done.7.refs_3_ = bf16[256,1408]{1,0:T(8,128)(2,1)S(1)} collective-permute-done((bf16[256,1408]{1,0:T(8,128)(2,1)}, bf16[256,1408]{1,0:T(8,128)(2,1)S(1)}, u32[]{:S(2)}, u32[]{:S(2)}) %collective-permute-start.7) | collective-permute-done | bytes 720928 | tf_op jit(solution)/shard_map/ppermute | solution.py:534
  64.2 2.1 %collective-permute-done.13.refs_2_.refs_9_.refs_1_.refs_4_ = bf16[224,2304]{1,0:T(8,128)(2,1)} collective-permute-done((bf16[224,2304]{1,0:T(8,128)(2,1)}, bf16[224,2304]{1,0:T(8,128)(2,1)}, u32[]{:S(2)}, u32[]{:S(2)}) %collective-permute-start.13) | collective-permute-done | bytes 1032224 | tf_op jit(solution)/shard_map/ppermute | solution.py:539
  66.3 5.6 %collective-permute-start.14 = (bf16[224,2304]{1,0:T(8,128)(2,1)}, bf16[224,2304]{1,0:T(8,128)(2,1)}, u32[]{:S(2)}, u32[]{:S(2)}) collective-permute-start(bf16[224,2304]{1,0:T(8,128)(2,1)} %gate.3.refs_8_.own), channel_id=1, source_target_pairs={{0,24},{2,26},{4,28},{6,30},{24,0},{26,2},{28,4},{30,6},{1,25},{3,... | collective-permute-start | bytes 3096584 | tf_op jit(solution)/shard_map/ppermute | solution.py:539
  72.0 6.1 %project_send.1 = (bf16[256,896]{1,0:T(8,128)(2,1)}, bf16[1024,2304]{1,0:T(8,128)(2,1)}) custom-call(bf16[256,896]{1,0:T(8,128)(2,1)} %get-tuple-element.28.refs_0_, bf16[256,1408]{1,0:T(8,128)(2,1)} %join.1.refs_1_, bf16[256,896]{1,0:T(8,128)(2,1)} %copy-done.9, bf16[256,1408]{1,0:T(8,128)(2,1)} %copy-done.7, bf16[256,896]{1,0:T(8,128)(2,1)} %copy-done.8, ...), custom_call_target="tpu_custom_call" | custom-call | flops 1 | bytes 1 | tf_op jit(solution)/shard_map/project_send/pallas_call | solution.py:285
  78.1 1.6 %collective-permute-start.15 = (bf16[256,896]{1,0:T(8,128)(2,1)}, bf16[256,896]{1,0:T(8,128)(2,1)S(1)}, u32[]{:S(2)}, u32[]{:S(2)}) collective-permute-start(bf16[256,896]{1,0:T(8,128)(2,1)} %get-tuple-element.38.refs_8_), channel_id=1, source_target_pairs={{0,1},{1,0},{2,3},{3,2},{4,5},{5,4},{6,7},{7,6},{8,9},{9,8},{10,11... | collective-permute-start | bytes 1376264 | tf_op jit(solution)/shard_map/ppermute | solution.py:650
  79.7 7.9 %project_keep.1 = (f32[4,256,224]{2,1,0:T(8,128)}, f32[4,256,224]{2,1,0:T(8,128)}, bf16[256,896]{1,0:T(8,128)(2,1)}) custom-call(bf16[1024,2304]{1,0:T(8,128)(2,1)} %get-tuple-element.37.held, bf16[224,2304]{1,0:T(8,128)(2,1)} %gate.3.refs_8_.own, bf16[224,2304]{1,0:T(8,128)(2,1)} %gate.2.refs_1_.refs_10_.refs_0_.refs_2_.refs_5_, ...), custom_call_target="tpu_custom_call" | custom-call | flops 1 | bytes 1 | tf_op jit(solution)/shard_map/project_keep/pallas_call | solution.py:285
  87.6 1.6 %collective-permute-start.16 = (bf16[256,896]{1,0:T(8,128)(2,1)}, bf16[256,896]{1,0:T(8,128)(2,1)S(1)}, u32[]{:S(2)}, u32[]{:S(2)}) collective-permute-start(bf16[256,896]{1,0:T(8,128)(2,1)} %get-tuple-element.41), channel_id=1, source_target_pairs={{1,0},{3,2},{5,4},{7,6},{9,8},{11,10},{13,12},{15,14},{16,17},{18,... | collective-permute-start | bytes 1376264 | tf_op jit(solution)/shard_map/ppermute | solution.py:547
  89.6 4.8 %collective-permute-done.14.refs_0_.refs_3_ = bf16[224,2304]{1,0:T(8,128)(2,1)} collective-permute-done((bf16[224,2304]{1,0:T(8,128)(2,1)}, bf16[224,2304]{1,0:T(8,128)(2,1)}, u32[]{:S(2)}, u32[]{:S(2)}) %collective-permute-start.14) | collective-permute-done | bytes 1032224 | tf_op jit(solution)/shard_map/ppermute | solution.py:539
  94.4 2.7 %project_last.1 = (f32[4,256,224]{2,1,0:T(8,128)S(1)}, bf16[256,512]{1,0:T(8,128)(2,1)S(1)}, bf16[256,384]{1,0:T(8,128)(2,1)S(1)}) custom-call(bf16[1024,2304]{1,0:T(8,128)(2,1)S(1)} %copy-done, bf16[224,2304]{1,0:T(8,128)(2,1)} %collective-permute-done.14.refs_0_.refs_3_, bf16[224,2304]{1,0:T(8,128)(2,1)} %collective-permute-done.13.refs_2_.refs_9_.refs_1_.refs_4_, ...), custom_call_target="tpu_custom_call" | custom-call | flops 1 | bytes 1 | tf_op jit(solution)/shard_map/project_last/pallas_call | solution.py:285
  97.2 3.4 %collective-permute-start.17 = (bf16[256,512]{1,0:T(8,128)(2,1)S(1)}, bf16[256,512]{1,0:T(8,128)(2,1)S(1)}, u32[]{:S(2)}, u32[]{:S(2)}) collective-permute-start(bf16[256,512]{1,0:T(8,128)(2,1)S(1)} %get-tuple-element.42), channel_id=1, source_target_pairs={{0,1},{2,3},{4,5},{6,7},{8,9},{10,11},{12,13},{14,15},{17,16},{19,... | collective-permute-start | bytes 786440 | tf_op jit(solution)/shard_map/ppermute | solution.py:547
  100.8 1.1 collective-permute-start.19
  101.9 1.3 %collective-permute-start.18 = (bf16[256,384]{1,0:T(8,128)(2,1)S(1)}, bf16[256,384]{1,0:T(8,128)(2,1)S(1)}, u32[]{:S(2)}, u32[]{:S(2)}) collective-permute-start(bf16[256,384]{1,0:T(8,128)(2,1)S(1)} %get-tuple-element.43), channel_id=1, source_target_pairs={{0,1},{2,3},{4,5},{6,7},{8,9},{10,11},{12,13},{14,15},{17,16},{19,... | collective-permute-start | bytes 589832 | tf_op jit(solution)/shard_map/ppermute | solution.py:547
  104.4 1.5 %collective-permute-done.19.refs_1_.refs_2_ = bf16[256,224]{1,0:T(8,128)(2,1)S(1)} collective-permute-done((bf16[256,224]{1,0:T(8,128)(2,1)S(1)}, bf16[256,224]{1,0:T(8,128)(2,1)S(1)}, u32[]{:S(2)}, u32[]{:S(2)}) %collective-permute-start.19) | collective-permute-done | bytes 114720 | tf_op jit(solution)/shard_map/ppermute | solution.py:534
  107.1 1.1 collective-permute-start.23
  109.5 3.6 %collective-permute-done.23.refs_4_ = bf16[256,224]{1,0:T(8,128)(2,1)S(1)} collective-permute-done((bf16[256,224]{1,0:T(8,128)(2,1)S(1)}, bf16[256,224]{1,0:T(8,128)(2,1)S(1)}, u32[]{:S(2)}, u32[]{:S(2)}) %collective-permute-start.23) | collective-permute-done | bytes 114720 | tf_op jit(solution)/shard_map/ppermute | solution.py:534
  114.1 1.1 place.3
  (56 shorter events, 10.4 us)
Async XLA Ops:
  2.4 11.7 %collective-permute-start = (bf16[256,512]{1,0:T(8,128)(2,1)}, bf16[256,512]{1,0:T(8,128)(2,1)S(1)}, u32[]{:S(2)}, u32[]{:S(2)}) collective-permute-start(bf16[256,512]{1,0:T(8,128)(2,1)} %get-tuple-element.27.even_ref.k_own_ref.v_own_ref), channel_id=1, source_target_pairs={{0,4},{2,6},{4,8},{6,10},{8,12},{10,14},{12,16},{14,18},{16,20},{1... | collective-permute-start | bytes 786440 | tf_op jit(solution)/shard_map/ppermute | solution.py:529
  7.3 28.7 %collective-permute-start.5 = (bf16[224,2304]{1,0:T(8,128)(2,1)}, bf16[224,2304]{1,0:T(8,128)(2,1)}, u32[]{:S(2)}, u32[]{:S(2)}) collective-permute-start(bf16[224,2304]{1,0:T(8,128)(2,1)} %get-tuple-element.36.refs_0_), channel_id=1, source_target_pairs={{8,0},{10,2},{12,4},{14,6},{16,8},{18,10},{20,12},{22,14},{24,16},... | collective-permute-start | bytes 3096584 | tf_op jit(solution)/shard_map/ppermute | solution.py:539
  8.6 29.5 %collective-permute-start.4 = (bf16[224,2304]{1,0:T(8,128)(2,1)}, bf16[224,2304]{1,0:T(8,128)(2,1)}, u32[]{:S(2)}, u32[]{:S(2)}) collective-permute-start(bf16[224,2304]{1,0:T(8,128)(2,1)} %get-tuple-element.36.refs_0_), channel_id=1, source_target_pairs={{0,8},{2,10},{4,12},{6,14},{8,16},{10,18},{12,20},{14,22},{16,24},... | collective-permute-start | bytes 3096584 | tf_op jit(solution)/shard_map/ppermute | solution.py:539
  15.1 1.6 %copy-start.2 = (bf16[256,512]{1,0:T(8,128)(2,1)}, bf16[256,512]{1,0:T(8,128)(2,1)S(1)}, u32[]{:S(2)}) copy-start(bf16[256,512]{1,0:T(8,128)(2,1)S(1)} %collective-permute-done.odd_ref.k_far_ref.v_far_ref) | copy-start | bytes 786436
  15.1 1.6 %collective-permute-start.1 = (bf16[256,512]{1,0:T(8,128)(2,1)S(1)}, bf16[256,512]{1,0:T(8,128)(2,1)S(1)}, u32[]{:S(2)}, u32[]{:S(2)}) collective-permute-start(bf16[256,512]{1,0:T(8,128)(2,1)S(1)} %choose.1), channel_id=1, source_target_pairs={{0,2},{2,0},{4,6},{6,4},{8,10},{10,8},{12,14},{14,12},{16,18},{18,... | collective-permute-start | bytes 786440 | tf_op jit(solution)/shard_map/ppermute | solution.py:534
  23.2 12.8 %collective-permute-start.6 = (bf16[256,896]{1,0:T(8,128)(2,1)}, bf16[256,896]{1,0:T(8,128)(2,1)S(1)}, u32[]{:S(2)}, u32[]{:S(2)}) collective-permute-start(bf16[256,896]{1,0:T(8,128)(2,1)} %get-tuple-element.28.refs_0_), channel_id=1, source_target_pairs={{0,4},{2,6},{4,0},{6,2},{8,12},{10,14},{12,8},{14,10},{16,20},{18,... | collective-permute-start | bytes 1376264 | tf_op jit(solution)/shard_map/ppermute | solution.py:534
  31.0 1.7 %collective-permute-start.2 = (bf16[256,512]{1,0:T(8,128)(2,1)}, bf16[256,512]{1,0:T(8,128)(2,1)S(1)}, u32[]{:S(2)}, u32[]{:S(2)}) collective-permute-start(bf16[256,512]{1,0:T(8,128)(2,1)} %get-tuple-element.34), channel_id=1, source_target_pairs={{0,2},{2,0},{4,6},{6,4},{8,10},{10,8},{12,14},{14,12},{16,18},{18,... | collective-permute-start | bytes 786440 | tf_op jit(solution)/shard_map/ppermute | solution.py:534
  32.8 11.5 %copy-start.4 = (bf16[256,512]{1,0:T(8,128)(2,1)}, bf16[256,512]{1,0:T(8,128)(2,1)S(1)}, u32[]{:S(2)}) copy-start(bf16[256,512]{1,0:T(8,128)(2,1)S(1)} %collective-permute-done.2.got) | copy-start | bytes 786436
  33.8 10.4 %collective-permute-start.3 = (bf16[256,512]{1,0:T(8,128)(2,1)S(1)}, bf16[256,512]{1,0:T(8,128)(2,1)}, u32[]{:S(2)}, u32[]{:S(2)}) collective-permute-start(bf16[256,512]{1,0:T(8,128)(2,1)S(1)} %merge.1), channel_id=1, source_target_pairs={{4,0},{6,2},{8,4},{10,6},{12,8},{14,10},{16,12},{18,14},{20,16},{2... | collective-permute-start | bytes 786440 | tf_op jit(solution)/shard_map/ppermute | solution.py:529
  36.8 29.5 %collective-permute-start.13 = (bf16[224,2304]{1,0:T(8,128)(2,1)}, bf16[224,2304]{1,0:T(8,128)(2,1)}, u32[]{:S(2)}, u32[]{:S(2)}) collective-permute-start(bf16[224,2304]{1,0:T(8,128)(2,1)} %gate.2.refs_1_.refs_10_.refs_0_.refs_2_.refs_5_), channel_id=1, source_target_pairs={{8,0},{10,2},{12,4},{14,6},{16,8},{18,10},{20,12},{22,14},{9,1},{1... | collective-permute-start | bytes 3096584 | tf_op jit(solution)/shard_map/ppermute | solution.py:539
  38.1 28.2 %collective-permute-start.12 = (bf16[224,2304]{1,0:T(8,128)(2,1)}, bf16[224,2304]{1,0:T(8,128)(2,1)}, u32[]{:S(2)}, u32[]{:S(2)}) collective-permute-start(bf16[224,2304]{1,0:T(8,128)(2,1)} %collective-permute-done.4.refs_0_.refs_11_.refs_1_.refs_3_.refs_6_), channel_id=1, source_target_pairs={{8,16},{10,18},{12,20},{14,22},{16,24},{18,26},{20,28},{22,30},{9,... | collective-permute-start | bytes 3096584 | tf_op jit(solution)/shard_map/ppermute | solution.py:539
  46.6 17.6 %collective-permute-start.7 = (bf16[256,1408]{1,0:T(8,128)(2,1)}, bf16[256,1408]{1,0:T(8,128)(2,1)S(1)}, u32[]{:S(2)}, u32[]{:S(2)}) collective-permute-start(bf16[256,1408]{1,0:T(8,128)(2,1)} %join.1.refs_1_), channel_id=1, source_target_pairs={{0,4},{2,6},{4,0},{6,2},{8,12},{10,14},{12,8},{14,10},{16,20},{18,... | collective-permute-start | bytes 2162696 | tf_op jit(solution)/shard_map/ppermute | solution.py:534
  48.7 2.7 %collective-permute-start.8 = (bf16[256,896]{1,0:T(8,128)(2,1)}, bf16[256,896]{1,0:T(8,128)(2,1)S(1)}, u32[]{:S(2)}, u32[]{:S(2)}) collective-permute-start(bf16[256,896]{1,0:T(8,128)(2,1)} %get-tuple-element.28.refs_0_), channel_id=1, source_target_pairs={{0,2},{2,0},{4,6},{6,4},{8,10},{10,8},{12,14},{14,12},{16,18},{18,... | collective-permute-start | bytes 1376264 | tf_op jit(solution)/shard_map/ppermute | solution.py:534
  48.7 15.5 %collective-permute-start.10 = (bf16[256,896]{1,0:T(8,128)(2,1)}, bf16[256,896]{1,0:T(8,128)(2,1)}, u32[]{:S(2)}, u32[]{:S(2)}) collective-permute-start(bf16[256,896]{1,0:T(8,128)(2,1)} %copy-done.9), channel_id=1, source_target_pairs={{0,2},{2,0},{4,6},{6,4},{8,10},{10,8},{12,14},{14,12},{16,18},{18,... | collective-permute-start | bytes 1376264 | tf_op jit(solution)/shard_map/ppermute | solution.py:534
  51.4 12.8 %copy-start.8 = (bf16[256,896]{1,0:T(8,128)(2,1)}, bf16[256,896]{1,0:T(8,128)(2,1)S(1)}, u32[]{:S(2)}) copy-start(bf16[256,896]{1,0:T(8,128)(2,1)S(1)} %collective-permute-done.8.refs_4_) | copy-start | bytes 1376260
  51.4 20.6 %collective-permute-start.9 = (bf16[256,1408]{1,0:T(8,128)(2,1)}, bf16[256,1408]{1,0:T(8,128)(2,1)}, u32[]{:S(2)}, u32[]{:S(2)}) collective-permute-start(bf16[256,1408]{1,0:T(8,128)(2,1)} %join.1.refs_1_), channel_id=1, source_target_pairs={{0,2},{2,0},{4,6},{6,4},{8,10},{10,8},{12,14},{14,12},{16,18},{18,... | collective-permute-start | bytes 2162696 | tf_op jit(solution)/shard_map/ppermute | solution.py:534
  64.2 2.1 %copy-start.7 = (bf16[256,1408]{1,0:T(8,128)(2,1)}, bf16[256,1408]{1,0:T(8,128)(2,1)S(1)}, u32[]{:S(2)}) copy-start(bf16[256,1408]{1,0:T(8,128)(2,1)S(1)} %collective-permute-done.7.refs_3_) | copy-start | bytes 2162692
  64.2 7.8 %collective-permute-start.11 = (bf16[256,1408]{1,0:T(8,128)(2,1)S(1)}, bf16[256,1408]{1,0:T(8,128)(2,1)}, u32[]{:S(2)}, u32[]{:S(2)}) collective-permute-start(bf16[256,1408]{1,0:T(8,128)(2,1)S(1)} %collective-permute-done.7.refs_3_), channel_id=1, source_target_pairs={{0,2},{2,0},{4,6},{6,4},{8,10},{10,8},{12,14},{14,12},{16,18},{18,... | collective-permute-start | bytes 2162696 | tf_op jit(solution)/shard_map/ppermute | solution.py:534
  66.3 28.1 %collective-permute-start.14 = (bf16[224,2304]{1,0:T(8,128)(2,1)}, bf16[224,2304]{1,0:T(8,128)(2,1)}, u32[]{:S(2)}, u32[]{:S(2)}) collective-permute-start(bf16[224,2304]{1,0:T(8,128)(2,1)} %gate.3.refs_8_.own), channel_id=1, source_target_pairs={{0,24},{2,26},{4,28},{6,30},{24,0},{26,2},{28,4},{30,6},{1,25},{3,... | collective-permute-start | bytes 3096584 | tf_op jit(solution)/shard_map/ppermute | solution.py:539
  78.1 11.5 %collective-permute-start.15 = (bf16[256,896]{1,0:T(8,128)(2,1)}, bf16[256,896]{1,0:T(8,128)(2,1)S(1)}, u32[]{:S(2)}, u32[]{:S(2)}) collective-permute-start(bf16[256,896]{1,0:T(8,128)(2,1)} %get-tuple-element.38.refs_8_), channel_id=1, source_target_pairs={{0,1},{1,0},{2,3},{3,2},{4,5},{5,4},{6,7},{7,6},{8,9},{9,8},{10,11... | collective-permute-start | bytes 1376264 | tf_op jit(solution)/shard_map/ppermute | solution.py:650
  79.7 14.8 %copy-start = (bf16[1024,2304]{1,0:T(8,128)(2,1)S(1)}, bf16[1024,2304]{1,0:T(8,128)(2,1)}, u32[]{:S(2)}) copy-start(bf16[1024,2304]{1,0:T(8,128)(2,1)} %get-tuple-element.37.held) | copy-start | bytes 14155780
  87.6 13.0 %copy-start.10 = (f32[4,256,224]{2,1,0:T(8,128)S(1)}, f32[4,256,224]{2,1,0:T(8,128)}, u32[]{:S(2)}) copy-start(f32[4,256,224]{2,1,0:T(8,128)} %get-tuple-element.44) | copy-start | bytes 2752516
  87.6 19.2 %copy-start.3 = (f32[4,256,224]{2,1,0:T(8,128)S(1)}, f32[4,256,224]{2,1,0:T(8,128)}, u32[]{:S(2)}) copy-start(f32[4,256,224]{2,1,0:T(8,128)} %get-tuple-element.40.mate_full) | copy-start | bytes 2752516
  87.6 15.7 %collective-permute-start.16 = (bf16[256,896]{1,0:T(8,128)(2,1)}, bf16[256,896]{1,0:T(8,128)(2,1)S(1)}, u32[]{:S(2)}, u32[]{:S(2)}) collective-permute-start(bf16[256,896]{1,0:T(8,128)(2,1)} %get-tuple-element.41), channel_id=1, source_target_pairs={{1,0},{3,2},{5,4},{7,6},{9,8},{11,10},{13,12},{15,14},{16,17},{18,... | collective-permute-start | bytes 1376264 | tf_op jit(solution)/shard_map/ppermute | solution.py:547
  97.2 9.7 %collective-permute-start.17 = (bf16[256,512]{1,0:T(8,128)(2,1)S(1)}, bf16[256,512]{1,0:T(8,128)(2,1)S(1)}, u32[]{:S(2)}, u32[]{:S(2)}) collective-permute-start(bf16[256,512]{1,0:T(8,128)(2,1)S(1)} %get-tuple-element.42), channel_id=1, source_target_pairs={{0,1},{2,3},{4,5},{6,7},{8,9},{10,11},{12,13},{14,15},{17,16},{19,... | collective-permute-start | bytes 786440 | tf_op jit(solution)/shard_map/ppermute | solution.py:547
  100.8 5.0 %collective-permute-start.19 = (bf16[256,224]{1,0:T(8,128)(2,1)S(1)}, bf16[256,224]{1,0:T(8,128)(2,1)S(1)}, u32[]{:S(2)}, u32[]{:S(2)}) collective-permute-start(bf16[256,224]{1,0:T(8,128)(2,1)S(1)} %get-tuple-element.52), channel_id=1, source_target_pairs={{0,4},{2,6},{4,0},{6,2},{8,12},{10,14},{12,8},{14,10},{16,20},{18,... | collective-permute-start | bytes 344072 | tf_op jit(solution)/shard_map/ppermute | solution.py:534
  101.9 7.0 %collective-permute-start.18 = (bf16[256,384]{1,0:T(8,128)(2,1)S(1)}, bf16[256,384]{1,0:T(8,128)(2,1)S(1)}, u32[]{:S(2)}, u32[]{:S(2)}) collective-permute-start(bf16[256,384]{1,0:T(8,128)(2,1)S(1)} %get-tuple-element.43), channel_id=1, source_target_pairs={{0,1},{2,3},{4,5},{6,7},{8,9},{10,11},{12,13},{14,15},{17,16},{19,... | collective-permute-start | bytes 589832 | tf_op jit(solution)/shard_map/ppermute | solution.py:547
  103.2 6.3 %collective-permute-start.22 = (bf16[256,224]{1,0:T(8,128)(2,1)S(1)}, bf16[256,224]{1,0:T(8,128)(2,1)S(1)}, u32[]{:S(2)}, u32[]{:S(2)}) collective-permute-start(bf16[256,224]{1,0:T(8,128)(2,1)S(1)} %get-tuple-element.49), channel_id=1, source_target_pairs={{0,6},{2,4},{4,2},{6,0},{8,14},{10,12},{12,10},{14,8},{16,22},{18,... | collective-permute-start | bytes 344072 | tf_op jit(solution)/shard_map/ppermute | solution.py:534
  103.3 6.2 %collective-permute-start.21 = (bf16[256,224]{1,0:T(8,128)(2,1)S(1)}, bf16[256,224]{1,0:T(8,128)(2,1)S(1)}, u32[]{:S(2)}, u32[]{:S(2)}) collective-permute-start(bf16[256,224]{1,0:T(8,128)(2,1)S(1)} %get-tuple-element.50), channel_id=1, source_target_pairs={{0,2},{2,0},{4,6},{6,4},{8,10},{10,8},{12,14},{14,12},{16,18},{18,... | collective-permute-start | bytes 344072 | tf_op jit(solution)/shard_map/ppermute | solution.py:534
  107.1 6.1 %collective-permute-start.23 = (bf16[256,224]{1,0:T(8,128)(2,1)S(1)}, bf16[256,224]{1,0:T(8,128)(2,1)S(1)}, u32[]{:S(2)}, u32[]{:S(2)}) collective-permute-start(bf16[256,224]{1,0:T(8,128)(2,1)S(1)} %get-tuple-element.45.refs_2_), channel_id=1, source_target_pairs={{0,4},{2,6},{4,0},{6,2},{8,12},{10,14},{12,8},{14,10},{16,20},{18,... | collective-permute-start | bytes 344072 | tf_op jit(solution)/shard_map/ppermute | solution.py:534
  108.1 5.7 %collective-permute-start.24 = (bf16[256,224]{1,0:T(8,128)(2,1)S(1)}, bf16[256,224]{1,0:T(8,128)(2,1)S(1)}, u32[]{:S(2)}, u32[]{:S(2)}) collective-permute-start(bf16[256,224]{1,0:T(8,128)(2,1)S(1)} %get-tuple-element.46.refs_3_), channel_id=1, source_target_pairs={{0,6},{2,4},{4,2},{6,0},{8,14},{10,12},{12,10},{14,8},{16,22},{18,... | collective-permute-start | bytes 344072 | tf_op jit(solution)/shard_map/ppermute | solution.py:534
  109.1 5.1 %collective-permute-start.20 = (bf16[256,224]{1,0:T(8,128)(2,1)S(1)}, bf16[256,224]{1,0:T(8,128)(2,1)S(1)}, u32[]{:S(2)}, u32[]{:S(2)}) collective-permute-start(bf16[256,224]{1,0:T(8,128)(2,1)S(1)} %get-tuple-element.48), channel_id=1, source_target_pairs={{0,2},{2,0},{4,6},{6,4},{8,10},{10,8},{12,14},{14,12},{16,18},{18,... | collective-permute-start | bytes 344072 | tf_op jit(solution)/shard_map/ppermute | solution.py:534
  (4 other events, 3.5 us)
